TPU v7x, 32 devices: a whole 2x2x4 slice. The times are simulated.
32 devices in a mesh: sector: 4 (over z), mode: 8 (over y, x, core).
Axes of the slice: x: 2, y: 2, z: 4, core: 2. Of those that a mesh axis runs over, the one named last changes fastest.
Arguments:
- modes: bfloat16 [256, 3, 16, 80, 128], P('mode', None, 'sector'), may hold values from -0.21875 to 0.21875
- thickness: float32 [16, 80, 128], P('sector'), may hold values from -6 to 6
- stiff_taps: float32 [27], replicated, may hold values from -1.25 to 1.25
- mass_taps: float32 [27], replicated, may hold values from 0.02 to 0.2
- eigenvalues: float32 [256], P('mode'), may hold values from 0.5 to 2
Outputs:
- sensitivity: float32 [256, 256], P('sector', 'mode')
All inputs are finite; a program needn't handle non-finite values.
Results may differ from a plain program's by a relative error of at most 0.0029.
Values may be sent and summed in bfloat16 or wider, within the bound.
No kernel may reach another device: no remote copies, remote signals or barrier semaphores. Data moves between devices by JAX's collectives and lax.ppermute only.
A program may use at most 128 MiB of HBM per device.

v0:
```python
import jax
import jax.numpy as jnp
from jax import lax
from jax.sharding import PartitionSpec as P


def extended(cells, sides, width):
    for axis, dim in sides:
        count = lax.axis_size(axis)
        ends = count - 1
        head = lax.slice_in_dim(cells, 0, width, axis=dim)
        tail = lax.slice_in_dim(cells, cells.shape[dim] - width, cells.shape[dim], axis=dim)
        cells = jnp.concatenate(
            [
                lax.ppermute(tail, axis, [(i, (i + 1) % count) for i in range(ends)]),
                cells,
                lax.ppermute(head, axis, [((i + 1) % count, i) for i in range(ends)]),
            ],
            axis=dim,
        )
    return cells


def stencil(field, padded_thick, stiff_taps, mass_taps, lams):
    size_x = field.shape[2] - 2
    size_y = field.shape[3] - 2
    size_z = field.shape[4] - 2
    shape_out = (field.shape[0], field.shape[1], size_x, size_y, size_z)
    centre = padded_thick[1 : 1 + size_x, 1 : 1 + size_y, 1 : 1 + size_z]
    stiff_acc = jnp.zeros(shape_out, jnp.float32)
    mass_acc = jnp.zeros(shape_out, jnp.float32)
    for aoff in range(3):
        for boff in range(3):
            for doff in range(3):
                index = 9 * aoff + 3 * boff + doff
                coeff = 0.5 * (
                    centre
                    + padded_thick[aoff : aoff + size_x, boff : boff + size_y, doff : doff + size_z]
                )
                moved = (
                    coeff
                    * field[:, :, aoff : aoff + size_x, boff : boff + size_y, doff : doff + size_z]
                )
                stiff_acc = stiff_acc + stiff_taps[index] * moved
                mass_acc = mass_acc + mass_taps[index] * moved
    return (stiff_acc - lams[:, None, None, None, None] * mass_acc).astype(jnp.bfloat16)


def spread(whole):
    sectors = lax.axis_size("sector")
    groups = lax.axis_size("mode")
    total = whole.shape[0]
    arranged = whole.reshape(sectors, total // sectors, groups, total // groups)
    arranged = arranged.transpose(0, 2, 1, 3).reshape(
        sectors * groups * (total // sectors), total // groups
    )
    return lax.psum_scatter(arranged, ("sector", "mode"), scatter_dimension=0, tiled=True)


def on_device(modes, thickness, stiff_taps, mass_taps, eigenvalues):
    local_modes = modes.shape[0]
    size_z = modes.shape[4]
    thick_rim = extended(thickness, (("sector", 0),), 1)
    padded_thick = jnp.pad(thick_rim, ((0, 0), (1, 1), (1, 1)))
    planes = extended(modes, (("sector", 2),), 1)
    field = jnp.pad(planes.astype(jnp.float32), ((0, 0), (0, 0), (0, 0), (1, 1), (1, 1)))
    loaded = stencil(field, padded_thick, stiff_taps, mass_taps, eigenvalues)
    flat_modes = modes.reshape(local_modes, -1, size_z)
    flat_loaded = loaded.reshape(local_modes, -1, size_z)
    all_modes, all_loaded = (
        lax.all_to_all(flat_modes, "mode", split_axis=1, concat_axis=0, tiled=True),
        lax.all_to_all(flat_loaded, "mode", split_axis=1, concat_axis=0, tiled=True),
    )
    whole = lax.dot_general(
        all_modes, all_loaded, (((1, 2), (1, 2)), ((), ())), preferred_element_type=jnp.float32
    )
    return spread(whole)


def solution(mesh):
    in_specs = (P("mode", None, "sector", None, None), P("sector", None, None), P(), P(), P("mode"))
    out_specs = P("sector", "mode")
    return jax.shard_map(
        on_device, mesh=mesh, in_specs=in_specs, out_specs=out_specs, check_vma=False
    )
```

profile of v0, /device:TPU:0, one launch (start us, length us, event | category | flops | bytes accessed | tf_op | source)
XLA Modules:
  0.0 497.9 jit_solution(12665250794048393405)
XLA Ops:
  6.5 4.7 fusion.55
  11.2 5.0 %collective-permute-start.2 = (bf16[32,3,1,80,128]{4,3,2,1,0:T(8,128)(2,1)}, bf16[32,3,1,80,128]{4,3,2,1,0:T(8,128)(2,1)S(1)}, u32[]{:S(2)}, u32[]{:S(2)}) collective-permute-start(bf16[32,3,1,80,128]{4,3,2,1,0:T(8,128)(2,1)} %get-tuple-element.5), channel_id=1, source_target_pairs={{0,8},{8,16},{16,24},{1,9},{9,17},{17,25},{2,10},{10,18},{18,26},{... | collective-permute-start | bytes 5898248 | tf_op jit(solution)/shard_map/ppermute | solution.py:15
  16.3 1.3 collective-permute-start.3
  17.6 0.8 fusion.56
  18.4 4.5 collective-permute-start
  22.9 0.0 copy-start.2
  23.0 0.0 copy-start.3
  23.0 0.0 copy-start
  23.0 1.4 collective-permute-start.1
  24.4 11.4 %copy.13 = bf16[32,3,4,80,128]{4,0,3,2,1:T(8,128)(2,1)} copy(bf16[32,3,4,80,128]{4,3,2,1,0:T(8,128)(2,1)} %param.5) | data formatting | bytes 15728640 | tf_op args[0]
  35.8 5.1 %all-to-all-start.1 = ((bf16[32,960,128]{2,0,1:T(8,128)(2,1)}), bf16[32,960,128]{2,0,1:T(8,128)(2,1)}, u32[]{:S(2)}, u32[]{:S(2)}) async-start(bf16[32,960,128]{2,0,1:T(8,128)(2,1)} %bitcast.75), calls=%async_computation.1 | async-start | bytes 15728640 | tf_op jit(solution)/shard_map/all_to_all | solution.py:71
  40.9 0.0 copy-done.2
  40.9 0.7 fusion.58
  41.6 0.7 fusion.57
  42.3 0.0 copy-done.3
  42.4 0.7 fusion.59
  43.1 0.7 fusion.60
  43.7 15.6 %collective-permute-done = f32[1,80,128]{2,1,0:T(8,128)S(1)} collective-permute-done((f32[1,80,128]{2,1,0:T(8,128)S(1)}, f32[1,80,128]{2,1,0:T(8,128)S(1)}, u32[]{:S(2)}, u32[]{:S(2)}) %collective-permute-start) | collective-permute-done | bytes 40992 | tf_op jit(solution)/shard_map/ppermute | solution.py:15
  59.3 4.2 collective-permute-done.1
  63.6 0.0 copy-done
  63.6 0.2 select_maximum_fusion
  63.8 1.1 fusion.53
  64.9 2.3 fusion.54
  67.1 0.0 copy-start.4
  67.1 0.0 collective-permute-done.2
  67.1 0.0 copy-start.1
  67.1 1.3 copy-done.1
  68.5 0.0 collective-permute-done.3
  68.5 6.2 %maximum_convert_fusion = f32[32,3,6,80,128]{4,3,2,1,0:T(8,128)S(1)} fusion(bf16[32,3,1,80,128]{4,3,2,1,0:T(8,128)(2,1)} %collective-permute-done.3, bf16[32,3,4,80,128]{4,3,2,1,0:T(8,128)(2,1)} %param.5, bf16[32,3,1,80,128]{4,3,2,1,0:T(8,128)(2,1)} %copy-done.1), kind=kLoop, calls=%fused_computation.52 | loop fusion | flops 17694720 | bytes 35389440 | tf_op jit(solution)/shard_map/convert_element_type | solution.py:66
  74.7 0.0 copy-done.4
  74.7 160.8 %subtract_convert_fusion = bf16[32,3,4,80,128]{4,3,2,1,0:T(8,128)(2,1)} fusion(f32[32,3,6,80,128]{4,3,2,1,0:T(8,128)S(1)} %maximum_convert_fusion, f32[]{:T(128)} %bitcast.53, f32[]{:T(128)} %bitcast.52, f32[]{:T(128)} %bitcast.51, f32[]{:T(128)} %bitcast.50, f32[]{:T(128)} %bitcast.49, f32[]{:T(128)} %bitcast.48, f32[]{:T(128)} %bitcast.47, f32[]{:T(128)} %bitcast.46, ...), kind=kLoop, calls=%fused_computation.51 | loop fusion | flops 534773760 | bytes 83067608 | tf_op jit(solution)/shard_map/convert_element_type | solution.py:46
  235.5 11.5 %copy.10 = bf16[32,3,4,80,128]{4,0,3,2,1:T(8,128)(2,1)} copy(bf16[32,3,4,80,128]{4,3,2,1,0:T(8,128)(2,1)} %subtract_convert_fusion) | data formatting | bytes 15728640 | tf_op jit(solution)/shard_map/convert_element_type | solution.py:46
  247.0 0.0 all-to-all-done.1
  247.0 5.0 all-to-all-start
  252.0 0.3 reduce-scatter.4.cloned.1.call-start
  252.2 8.9 %copy.15 = bf16[8,32,120,128]{3,1,0,2:T(8,128)(2,1)} copy(bf16[8,32,120,128]{3,1,2,0:T(8,128)(2,1)} %bitcast.62) | data formatting | bytes 15728640 | tf_op jit(solution)/shard_map/all_to_all | solution.py:71
  261.1 79.3 %all-to-all-done = bf16[32,960,128]{2,0,1:T(8,128)(2,1)} async-done(((bf16[32,960,128]{2,0,1:T(8,128)(2,1)}), bf16[32,960,128]{2,0,1:T(8,128)(2,1)}, u32[]{:S(2)}, u32[]{:S(2)}) %all-to-all-start) | async-done | bytes 7864352 | tf_op jit(solution)/shard_map/all_to_all | solution.py:72
  340.4 0.0 slice-start
  340.4 0.0 slice-start.1
  340.4 8.9 %copy.12 = bf16[8,32,120,128]{3,1,0,2:T(8,128)(2,1)} copy(bf16[8,32,120,128]{3,1,2,0:T(8,128)(2,1)} %bitcast.57) | data formatting | bytes 15728640 | tf_op jit(solution)/shard_map/all_to_all | solution.py:72
  349.3 0.0 slice-done
  349.3 0.0 slice-done.1
  349.3 5.5 %convolution_bitcast_fusion = f32[256,256]{0,1:T(8,128)S(1)} fusion(bf16[256,120,128]{2,0,1:T(8,128)(2,1)} %bitcast.80, bf16[256,120,128]{2,0,1:T(8,128)(2,1)S(1)} %bitcast.79), kind=kOutput, calls=%fused_computation.53 | convolution fusion | flops 2013265920 | bytes 15990784 | tf_op jit(solution)/shard_map/dot_general | solution.py:74
  354.8 0.2 reshape.42
  355.1 1.4 copy.21
  356.4 0.0 reduce-scatter.4.cloned.1.call-update
  356.5 133.2 %reduce-scatter.4.cloned.1.call-done = f32[64,32]{1,0:T(8,128)} async-done(((f32[2048,32]{1,0:T(8,128)}), f32[64,32]{1,0:T(8,128)}) %reduce-scatter.4.cloned.1.call-update) | async-done | bytes 8208
  489.6 1.4 copy.20
  (1 shorter events, 0.0 us)
Async XLA Ops:
  11.2 55.9 %collective-permute-start.2 = (bf16[32,3,1,80,128]{4,3,2,1,0:T(8,128)(2,1)}, bf16[32,3,1,80,128]{4,3,2,1,0:T(8,128)(2,1)S(1)}, u32[]{:S(2)}, u32[]{:S(2)}) collective-permute-start(bf16[32,3,1,80,128]{4,3,2,1,0:T(8,128)(2,1)} %get-tuple-element.5), channel_id=1, source_target_pairs={{0,8},{8,16},{16,24},{1,9},{9,17},{17,25},{2,10},{10,18},{18,26},{... | collective-permute-start | bytes 5898248 | tf_op jit(solution)/shard_map/ppermute | solution.py:15
  16.3 52.2 %collective-permute-start.3 = (bf16[32,3,1,80,128]{4,3,2,1,0:T(8,128)(2,1)}, bf16[32,3,1,80,128]{4,3,2,1,0:T(8,128)(2,1)}, u32[]{:S(2)}, u32[]{:S(2)}) collective-permute-start(bf16[32,3,1,80,128]{4,3,2,1,0:T(8,128)(2,1)} %get-tuple-element.6), channel_id=1, source_target_pairs={{8,0},{16,8},{24,16},{9,1},{17,9},{25,17},{10,2},{18,10},{26,18},{... | collective-permute-start | bytes 5898248 | tf_op jit(solution)/shard_map/ppermute | solution.py:17
  18.4 40.9 %collective-permute-start = (f32[1,80,128]{2,1,0:T(8,128)S(1)}, f32[1,80,128]{2,1,0:T(8,128)S(1)}, u32[]{:S(2)}, u32[]{:S(2)}) collective-permute-start(f32[1,80,128]{2,1,0:T(8,128)S(1)} %get-tuple-element.34), channel_id=1, source_target_pairs={{0,8},{8,16},{16,24},{1,9},{9,17},{17,25},{2,10},{10,18},{18,26},{... | collective-permute-start | bytes 122888 | tf_op jit(solution)/shard_map/ppermute | solution.py:15
  22.9 18.0 %copy-start.2 = (f32[27]{0:T(128)S(1)}, f32[27]{0:T(128)}, u32[]{:S(2)}) copy-start(f32[27]{0:T(128)} %param.7) | copy-start | bytes 328
  23.0 19.4 %copy-start.3 = (f32[27]{0:T(128)S(1)}, f32[27]{0:T(128)}, u32[]{:S(2)}) copy-start(f32[27]{0:T(128)} %param.8) | copy-start | bytes 328
  23.0 40.6 %copy-start = (f32[4,80,128]{2,1,0:T(8,128)S(1)}, f32[4,80,128]{2,1,0:T(8,128)}, u32[]{:S(2)}) copy-start(f32[4,80,128]{2,1,0:T(8,128)} %param.6) | copy-start | bytes 491524
  23.0 40.6 %collective-permute-start.1 = (f32[1,80,128]{2,1,0:T(8,128)S(1)}, f32[1,80,128]{2,1,0:T(8,128)S(1)}, u32[]{:S(2)}, u32[]{:S(2)}) collective-permute-start(f32[1,80,128]{2,1,0:T(8,128)S(1)} %get-tuple-element.35), channel_id=1, source_target_pairs={{8,0},{16,8},{24,16},{9,1},{17,9},{25,17},{10,2},{18,10},{26,18},{... | collective-permute-start | bytes 122888 | tf_op jit(solution)/shard_map/ppermute | solution.py:17
  35.8 211.2 %all-to-all-start.1 = ((bf16[32,960,128]{2,0,1:T(8,128)(2,1)}), bf16[32,960,128]{2,0,1:T(8,128)(2,1)}, u32[]{:S(2)}, u32[]{:S(2)}) async-start(bf16[32,960,128]{2,0,1:T(8,128)(2,1)} %bitcast.75), calls=%async_computation.1 | async-start | bytes 15728640 | tf_op jit(solution)/shard_map/all_to_all | solution.py:71
  67.1 7.5 %copy-start.4 = (f32[32]{0:T(128)S(1)}, f32[32]{0:T(128)}, u32[]{:S(2)}) copy-start(f32[32]{0:T(128)} %param.9) | copy-start | bytes 388
  67.1 1.3 copy-start.1
  247.0 93.4 %all-to-all-start = ((bf16[32,960,128]{2,0,1:T(8,128)(2,1)}), bf16[32,960,128]{2,0,1:T(8,128)(2,1)}, u32[]{:S(2)}, u32[]{:S(2)}) async-start(bf16[32,960,128]{2,0,1:T(8,128)(2,1)} %bitcast.76), calls=%async_computation | async-start | bytes 15728640 | tf_op jit(solution)/shard_map/all_to_all | solution.py:72
  252.0 237.7 %reduce-scatter.4.cloned.1.call-start = ((), (), s32[]{:S(2)}) async-start(), calls=%async_computation.3 | async-start | bytes 1081344
  340.4 8.9 %slice-start = ((s8[7864320]{0:T(1024)(128)(4,1)}), s8[4194304]{0:T(1024)(128)(4,1)S(1)}, s32[]{:S(2)}) async-start(s8[7864320]{0:T(1024)(128)(4,1)} %bitcast.77), calls=%async_computation.4 | async-start | bytes 8388608
  340.4 8.9 %slice-start.1 = ((s8[7864320]{0:T(1024)(128)(4,1)}), s8[3670016]{0:T(1024)(128)(4,1)S(1)}, s32[]{:S(2)}) async-start(s8[7864320]{0:T(1024)(128)(4,1)} %bitcast.77), calls=%async_computation.5 | async-start | bytes 7340032
Sparse Core Ops, SparseCore 0:
  356.6 133.0 reduce-scatter.3
where the time goes:
time: 499 us; the launch traced here: 498 us
  waiting for transfers between devices  232 us (46%)
  other arithmetic  171 us (34%)
  local copies, waits for them, and re-layouts  53.4 us (11%)
  starting transfers between devices  22.6 us (5%)
  between operations  13.5 us (3%)
  matrix products  5.45 us (1%)
    convert_element_type x1, other arithmetic, stencil(): (stiff_acc - lams[:, None, None, None, None] * mass_acc).astype(jnp.bfloa...  161 us
    unnamed x2, waiting for transfers between devices  133 us
    all_to_all x1, waiting for transfers between devices, on_device(): lax.all_to_all(flat_loaded, 'mode', split_axis=1, concat_axis=0, tiled=True)  79.3 us
    ppermute x2, waiting for transfers between devices, extended(): lax.ppermute(tail, axis, [(i, (i + 1) % count) for i in range(ends)])  15.6 us
    unnamed x17, local copies, waits for them, and re-layouts  15.6 us
    convert_element_type x1, local copies, waits for them, and re-layouts, stencil(): (stiff_acc - lams[:, None, None, None, None] * mass_acc).astype(jnp.bfloa...  11.5 us
  transfers between devices with their start and end apart: 7, of which 4 were waited for; matrix products, arithmetic and copies ran while one was open for 41% of the time, Pallas kernels for 0%

commit v1 on v0

v1 whole, which is shorter than its diff:
```python
import functools

import jax
import jax.numpy as jnp
from jax import lax
from jax.experimental import pallas as pl
from jax.experimental.pallas import tpu as pltpu
from jax.sharding import PartitionSpec as P

VMEM_BYTES = 56 * 1024 * 1024
AB = [(a, b) for a in range(3) for b in range(3)]


def chunk_rows(total):
    sizes = [4, 6, 6, 4, 2]
    if sum(sizes) == total:
        return sizes
    sizes = []
    while total > 6:
        sizes.append(4)
        total -= 4
    return sizes + [total]


def pack_kernel(height, parts, chunks, me_ref, in_ref, *rest):
    outs, scr = rest[:-1], rest[-1]
    comps, size_y = in_ref.shape[1], in_ref.shape[3]
    first = chunks[0][0]
    last = chunks[-1][1]
    me = me_ref[0]
    for c in range(comps):
        for start in range(0, size_y, 16):
            wanted = [
                (p, e - first, height * p - 1 + e)
                for p in range(parts)
                for e in range(first, last)
                if start <= height * p - 1 + e < start + 16
            ]
            if not wanted:
                continue
            turned = jnp.swapaxes(in_ref[:, c, 0, start : start + 16, :], 0, 1)
            for p, e, y in wanted:
                scr[p, e, c] = turned[y - start]
        for p in range(parts):
            for e in range(first, last):
                if not 0 <= height * p - 1 + e < size_y:
                    scr[p, e - first, c] = jnp.zeros(scr.shape[3:], scr.dtype)
    for r, (lo, hi) in enumerate(chunks):
        for k in range(parts):
            outs[r * parts + k][0] = scr[me ^ k, lo - first : hi - first]


def pack(modes, me, height, parts, chunks):
    local, comps, planes, size_y, size_z = modes.shape
    shapes = [
        jax.ShapeDtypeStruct((planes, hi - lo, comps, local, size_z), modes.dtype)
        for lo, hi in chunks
        for _ in range(parts)
    ]
    count = chunks[-1][1] - chunks[0][0]
    outs = pl.pallas_call(
        functools.partial(pack_kernel, height, parts, chunks),
        grid=(planes,),
        in_specs=[
            pl.BlockSpec(memory_space=pltpu.SMEM),
            pl.BlockSpec((local, comps, 1, size_y, size_z), lambda x: (0, 0, x, 0, 0)),
        ],
        out_specs=[pl.BlockSpec((1,) + s.shape[1:], lambda x: (x, 0, 0, 0, 0)) for s in shapes],
        out_shape=shapes,
        scratch_shapes=[pltpu.VMEM((parts, count, comps, local, size_z), modes.dtype)],
        compiler_params=pltpu.CompilerParams(vmem_limit_bytes=VMEM_BYTES),
        name="pack",
        cost_estimate=pl.CostEstimate(flops=0, bytes_accessed=2 * modes.size * 2, transcendentals=0),
    )(me, modes)
    return [outs[r * parts : (r + 1) * parts] for r in range(len(chunks))]


def load_kernel(prev_rows, rows, own, *refs):
    if prev_rows:
        (u_ref, lam_ref, s_ref, f_ref, lo_ref, hi_ref, e_ref, fp_ref, lop_ref, hip_ref, ep_ref,
         out_ref, win, other, g_ref, l_ref, sems) = refs
    else:
        (u_ref, lam_ref, f_ref, lo_ref, hi_ref, e_ref,
         out_ref, win, other, g_ref, l_ref, sems) = refs
    planes = f_ref.shape[0]
    size_z = f_ref.shape[-1]
    comps = f_ref.shape[2] // own
    keep = 2 if prev_rows else 0
    done = rows - 2 + keep
    copies = [
        (f_ref, win.at[1 : 1 + planes, keep : keep + rows]),
        (lo_ref, win.at[0, keep : keep + rows]),
        (hi_ref, win.at[planes + 1, keep : keep + rows]),
    ]
    if prev_rows:
        copies += [
            (fp_ref.at[:, prev_rows - 2 : prev_rows], win.at[1 : 1 + planes, 0:2]),
            (lop_ref.at[prev_rows - 2 : prev_rows], win.at[0, 0:2]),
            (hip_ref.at[prev_rows - 2 : prev_rows], win.at[planes + 1, 0:2]),
            (e_ref.at[:, 0 : rows - 1], other.at[:, 1:rows]),
            (ep_ref.at[:, prev_rows - 1 : prev_rows], other.at[:, 0:1]),
        ]
    else:
        copies += [(e_ref.at[:, 1 : rows - 1], other)]
    started = [pltpu.make_async_copy(src, dst, sems.at[n]) for n, (src, dst) in enumerate(copies)]
    for copy in started:
        copy.start()
    if prev_rows:
        out_ref[...] = s_ref[...]
    else:
        out_ref[...] = jnp.zeros_like(out_ref)
    for copy in started:
        copy.wait()

    gap = lax.broadcasted_iota(jnp.int32, (size_z, size_z), 0) - lax.broadcasted_iota(
        jnp.int32, (size_z, size_z), 1
    )
    diag = [gap == d - 1 for d in range(3)]

    def row(y, _):
        for x in range(planes):
            u = u_ref[y, x]
            high = u.astype(jnp.bfloat16).astype(jnp.float32)
            low = u - high
            for ab in range(9):
                for half, part in enumerate((high, low)):
                    for kind in range(2):
                        base = 27 * kind + 3 * ab
                        band = jnp.zeros((size_z, size_z), jnp.float32)
                        for d in range(3):
                            band = jnp.where(diag[d], part[base + d : base + d + 1], band)
                        g_ref[
                            (2 * ab + half) * size_z : (2 * ab + half + 1) * size_z,
                            kind * size_z : (kind + 1) * size_z,
                        ] = band.astype(jnp.bfloat16)
            around = []
            for a, b in AB:
                near = win[x + a, y + b]
                around += [near, near]
            images = jnp.dot(
                jnp.concatenate(around, axis=1), g_ref[...], preferred_element_type=jnp.float32
            )
            for c in range(comps):
                image = images[c * own : (c + 1) * own]
                l_ref[:, (x * comps + c) * size_z : (x * comps + c + 1) * size_z] = (
                    image[:, :size_z] - lam_ref[...] * image[:, size_z:]
                ).astype(jnp.bfloat16)
        cells = [(x, c) for x in range(planes) for c in range(comps)]
        mine = jnp.concatenate([win[x + 1, y + 1, c * own : (c + 1) * own] for x, c in cells], axis=1)
        theirs = jnp.concatenate([other[x, y, c * own : (c + 1) * own] for x, c in cells], axis=1)
        out_ref[...] += lax.dot_general(
            jnp.concatenate([mine, theirs], axis=0),
            l_ref[...],
            (((1,), (1,)), ((), ())),
            preferred_element_type=jnp.float32,
        )
        return 0

    lax.fori_loop(0, done, row, 0)


def load(u, lam, sums, now, before, own):
    rows = now[0].shape[1]
    planes, _, width, size_z = now[0].shape
    prev_rows = before[0].shape[1] if before else 0
    done = rows if before else rows - 2
    vmem = pl.BlockSpec(memory_space=pltpu.VMEM)
    hbm = pl.BlockSpec(memory_space=pl.ANY)
    args = [u, lam] + ([sums] if before else []) + list(now) + (list(before) if before else [])
    specs = [vmem] * (3 if before else 2) + [hbm] * (8 if before else 4)
    out = jax.ShapeDtypeStruct((2 * own, own), jnp.float32)
    taps = 2 * 9 * size_z
    return pl.pallas_call(
        functools.partial(load_kernel, prev_rows, rows, own),
        in_specs=specs,
        out_specs=vmem,
        out_shape=out,
        scratch_shapes=[
            pltpu.VMEM((planes + 2, done + 2, width, size_z), jnp.bfloat16),
            pltpu.VMEM((planes, done, width, size_z), jnp.bfloat16),
            pltpu.VMEM((taps, 2 * size_z), jnp.bfloat16),
            pltpu.VMEM((own, planes * width // own * size_z), jnp.bfloat16),
            pltpu.SemaphoreType.DMA((8,)),
        ],
        compiler_params=pltpu.CompilerParams(vmem_limit_bytes=VMEM_BYTES),
        name="load",
        cost_estimate=pl.CostEstimate(
            flops=2 * done * planes * width * taps * 2 * size_z,
            bytes_accessed=4 * done * planes * width * size_z,
            transcendentals=0,
        ),
    )(*args)


def arrange_kernel(parts, local, pos_ref, s_ref, *outs):
    *outs, rows_ref = outs
    me, mine = pos_ref[0], pos_ref[1]
    own = parts * local
    for h in range(2):
        for k in range(parts):
            slot = (me ^ k) * 2 + (mine ^ h)
            rows_ref[slot] = s_ref[h * own + k * local : h * own + (k + 1) * local]
    whole = rows_ref[...].reshape(2 * own, own)
    for k, out in enumerate(outs):
        rows, lanes = out.shape
        strips = lanes // local
        out[...] = jnp.concatenate(
            [whole[n * rows : (n + 1) * rows, k * local : (k + 1) * local] for n in range(strips)], axis=1
        )


def arrange(pos, sums, parts, local, sectors):
    total, own = sums.shape
    rows = total // sectors
    return pl.pallas_call(
        functools.partial(arrange_kernel, parts, local),
        in_specs=[pl.BlockSpec(memory_space=pltpu.SMEM), pl.BlockSpec(memory_space=pltpu.VMEM)],
        out_specs=[pl.BlockSpec(memory_space=pltpu.VMEM)] * parts,
        out_shape=[jax.ShapeDtypeStruct((rows, sectors * local), jnp.float32)] * parts,
        scratch_shapes=[pltpu.VMEM((2 * parts, local, own), jnp.float32)],
        name="arrange",
    )(pos, sums)


def on_device(modes, thickness, stiff_taps, mass_taps, eigenvalues):
    local, comps, planes, size_y, size_z = modes.shape
    sectors, groups = lax.axis_size("sector"), lax.axis_size("mode")
    parts = groups // 2
    height = size_y // parts
    own = parts * local
    index = lax.axis_index("mode")
    me, mine = index // 2, index % 2

    def other_part(value, k):
        return lax.ppermute(value, "mode", [(i, i ^ (2 * k)) for i in range(groups)])

    def other_half(value):
        return lax.ppermute(value, "mode", [(i, i ^ 1) for i in range(groups)])

    def from_below(value):
        return lax.ppermute(value, "sector", [(i, i + 1) for i in range(sectors - 1)])

    def from_above(value):
        return lax.ppermute(value, "sector", [(i + 1, i) for i in range(sectors - 1)])

    bounds, at = [], 0
    for size in chunk_rows(height + 2):
        bounds.append((at, at + size))
        at += size
    me_word = me.astype(jnp.int32).reshape(1)
    packed = pack(modes, me_word, height, parts, bounds[:1])
    packed += pack(modes, me_word, height, parts, bounds[1:])

    thick = jnp.concatenate([from_below(thickness[-1:]), thickness, from_above(thickness[:1])], axis=0)
    thick = jnp.pad(thick, ((0, 0), (1, 1), (1, 1)))
    thick = lax.dynamic_slice_in_dim(thick, me * height, height + 2, axis=1)
    centre = thick[1 : 1 + planes, 1 : 1 + height, 1 : 1 + size_z]
    coeffs = jnp.stack(
        [
            0.5 * (centre + thick[a : a + planes, b : b + height, d : d + size_z])
            for a in range(3)
            for b in range(3)
            for d in range(3)
        ],
        axis=2,
    )
    coeffs = jnp.concatenate(
        [coeffs * stiff_taps[:, None], coeffs * mass_taps[:, None]], axis=2
    ).transpose(1, 0, 2, 3)

    lams = jnp.concatenate(
        [eigenvalues] + [other_part(eigenvalues, k) for k in range(1, parts)], axis=0
    )
    lams = jnp.broadcast_to(lams[:, None], (own, size_z))

    sums, before, at = None, None, 0
    for (lo, hi), blocks in zip(bounds, packed):
        got = [blocks[0]] + [other_part(blocks[k], k) for k in range(1, parts)]
        field = jnp.concatenate(got, axis=3).reshape(planes, hi - lo, comps * own, size_z)
        now = (field, from_below(field[-1]), from_above(field[0]), other_half(field))
        done = hi - lo - (0 if before else 2)
        sums = load(coeffs[at : at + done], lams, sums, now, before, own)
        at += done
        before = now

    pos = jnp.stack([me, mine]).astype(jnp.int32)
    strips = arrange(pos, sums, parts, local, sectors)
    total = strips[0]
    for k in range(1, parts):
        total = total + other_part(strips[k], k)
    summed = total
    for step in range(1, sectors):
        summed = summed + lax.ppermute(
            total, "sector", [(i, (i + step) % sectors) for i in range(sectors)]
        )
    return lax.dynamic_slice_in_dim(summed, lax.axis_index("sector") * local, local, axis=1)


def solution(mesh):
    in_specs = (P("mode", None, "sector", None, None), P("sector", None, None), P(), P(), P("mode"))
    out_specs = P("sector", "mode")
    return jax.shard_map(
        on_device, mesh=mesh, in_specs=in_specs, out_specs=out_specs, check_vma=False
    )
```

time: 499 us -> 281 us (0.56)
  other arithmetic: 171 us -> 8.08 us
  waiting for transfers between devices: 232 us -> 79.6 us
  Pallas kernels: 0 us -> 96.1 us
  starting transfers between devices: 22.6 us -> 69.3 us
  local copies, waits for them, and re-layouts: 53.4 us -> 25.7 us
  between operations: 13.5 us -> 0.9 us
  matrix products: 5.45 us -> 0 us
    convert_element_type x2 -> x0, other arithmetic: 167 us -> none  [the longest x1 161 us: stencil(): (stiff_acc - lams[:, None, None, None, None] * mass_acc).astype(jnp.bfloa...]
    unnamed x2 -> x0, waiting for transfers between devices: 133 us -> none
    pallas_call x0 -> x8, Pallas kernels: none -> 96.1 us  [the longest x5 81.4 us: load(): pl.pallas_call(functools.partial(load_kernel, prev_rows, rows, own), in_s...]
    all_to_all x2 -> x0, waiting for transfers between devices: 79.3 us -> none  [the longest x1 79.3 us: on_device(): lax.all_to_all(flat_loaded, 'mode', split_axis=1, concat_axis=0, tiled=True)]
    ppermute x4 -> x41, waiting for transfers between devices: 19.8 us -> 79.6 us  [the longest x21 70.1 us: other_part(): return lax.ppermute(value, 'mode', [(i, i ^ 2 * k) for i in range(groups)])]
    ppermute x4 -> x41, starting transfers between devices: 12.3 us -> 69.3 us  [the longest x21 27.4 us: other_part(): return lax.ppermute(value, 'mode', [(i, i ^ 2 * k) for i in range(groups)])]
    all_to_all x2 -> x0, local copies, waits for them, and re-layouts: 17.8 us -> none  [the longest x1 8.93 us: on_device(): lax.all_to_all(flat_loaded, 'mode', split_axis=1, concat_axis=0, tiled=True)]
    convert_element_type x1 -> x0, local copies, waits for them, and re-layouts: 11.5 us -> none  [stencil(): (stiff_acc - lams[:, None, None, None, None] * mass_acc).astype(jnp.bfloa...]
  transfers between devices with their start and end apart: 7 -> 41, of which waited for: 4 -> 13; matrix products, arithmetic and copies ran while one was open for 41% -> 11% of each run, Pallas kernels for 0% -> 30%
where the time goes in v1:
time: 281 us; the launch traced here: 280 us
  Pallas kernels  96.1 us (34%)
  waiting for transfers between devices  79.6 us (28%)
  starting transfers between devices  69.3 us (25%)
  local copies, waits for them, and re-layouts  25.7 us (9%)
  other arithmetic  8.08 us (3%)
    pallas_call x5, Pallas kernels, load(): pl.pallas_call(functools.partial(load_kernel, prev_rows, rows, own), in_s...  81.4 us
    ppermute x21, waiting for transfers between devices, other_part(): return lax.ppermute(value, 'mode', [(i, i ^ 2 * k) for i in range(groups)])  70.1 us
    ppermute x21, starting transfers between devices, other_part(): return lax.ppermute(value, 'mode', [(i, i ^ 2 * k) for i in range(groups)])  27.4 us
    ppermute x6, starting transfers between devices, from_below(): lax.ppermute(value, 'sector', [(i, i + 1) for i in range(sectors - 1)])  26.9 us
    pallas_call x2, Pallas kernels, pack(): pl.pallas_call(functools.partial(pack_kernel, height, parts, chunks), gri...  13 us
    unnamed x89, local copies, waits for them, and re-layouts  12.4 us
    ppermute x6, starting transfers between devices, from_above(): lax.ppermute(value, 'sector', [(i + 1, i) for i in range(sectors - 1)])  7.92 us
    ppermute x3, starting transfers between devices, on_device(): lax.ppermute(total, 'sector', [(i, (i + step) % sectors) for i in range(s...  6.8 us
  transfers between devices with their start and end apart: 41, of which 13 were waited for; matrix products, arithmetic and copies ran while one was open for 11% of the time, Pallas kernels for 30%

profile of v1, /device:TPU:0, one launch (start us, length us, event | category | flops | bytes accessed | tf_op | source)
XLA Modules:
  0.0 279.7 jit_solution(3368205430564849661)
XLA Ops:
  0.0 3.9 %collective-permute-start.4 = (f32[32]{0:T(128)}, f32[32]{0:T(128)S(1)}, u32[]{:S(2)}, u32[]{:S(2)}) collective-permute-start(f32[32]{0:T(128)} %param.9), channel_id=1, source_target_pairs={{0,6},{1,7},{2,4},{3,5},{4,2},{5,3},{6,0},{7,1},{8,14},{9,15},{10,... | collective-permute-start | bytes 392 | tf_op jit(solution)/shard_map/ppermute | solution.py:235
  5.3 3.9 %collective-permute-start = (f32[1,80,128]{2,0,1:T(1,128)S(1)}, f32[1,80,128]{2,0,1:T(1,128)S(1)}, u32[]{:S(2)}, u32[]{:S(2)}) collective-permute-start(f32[1,80,128]{2,0,1:T(1,128)S(1)} %bitcast.150), channel_id=1, source_target_pairs={{0,8},{8,16},{16,24},{1,9},{9,17},{17,25},{2,10},{10,18},{18,26},{... | collective-permute-start | bytes 122888 | tf_op jit(solution)/shard_map/ppermute | solution.py:241
  9.2 1.3 collective-permute-start.1
  12.3 5.3 %pack.2 = (bf16[4,4,3,32,128]{4,3,2,1,0:T(8,128)(2,1)}, bf16[4,4,3,32,128]{4,3,2,1,0:T(8,128)(2,1)}, bf16[4,4,3,32,128]{4,3,2,1,0:T(8,128)(2,1)}, bf16[4,4,3,32,128]{4,3,2,1,0:T(8,128)(2,1)}) custom-call(s32[1]{0:T(128)} %bitcast.me_ref, bf16[32,3,4,80,128]{4,3,2,1,0:T(8,128)(2,1)} %in_ref.3), custom_call_target="tpu_custom_call" | custom-call | bytes 15728640 | tf_op jit(solution)/shard_map/pack/pallas_call | solution.py:61
  17.6 7.7 %pack.3 = (bf16[4,6,3,32,128]{4,3,2,1,0:T(8,128)(2,1)}, bf16[4,6,3,32,128]{4,3,2,1,0:T(8,128)(2,1)}, bf16[4,6,3,32,128]{4,3,2,1,0:T(8,128)(2,1)}, bf16[4,6,3,32,...) custom-call(s32[1]{0:T(128)} %bitcast.me_ref, ...), custom_call_target="tpu_custom_call" | custom-call | bytes 15728640 | tf_op jit(solution)/shard_map/pack/pallas_call | solution.py:61
  28.6 1.4 constant_dynamic-update-slice_fusion.7
  30.0 1.5 collective-permute-start.5
  31.5 1.5 collective-permute-start.6
  34.1 1.5 collective-permute-start.29
  40.0 5.0 %stack.123 = f32[4,20,27,128]{3,2,0,1:T(8,128)S(1)} concatenate(f32[4,20,1,128]{3,2,0,1:T(1,128)} %bitcast.148, f32[4,20,1,128]{3,2,0,1:T(1,128)} %bitcast.147, f32[4,20,1,128]{3,2,0,1:T(1,128)} %bitcast.146, f32[4,20,1,128]{3,2,0,1:T(1,128)} %bitcast.145, f32[4,20,1,128]{3,2,0,1:T(1,128)} %bitcast.144, f32[4,20,1,128]{3,2,0,1:T(1,128)} %bitcast.143, ...), dimensions={2} | concatenate | bytes 2211840 | tf_op jit(solution)/shard_map/stack | solution.py:258
  45.1 1.1 broadcast_multiply_fusion.1
  46.5 1.2 fusion.44
  49.3 7.6 %collective-permute-done.29 = bf16[4,2,3,32,128]{4,3,2,1,0:T(8,128)(2,1)} collective-permute-done((bf16[4,2,3,32,128]{4,3,2,1,0:T(8,128)(2,1)}, bf16[4,2,3,32,128]{4,3,2,1,0:T(8,128)(2,1)}, u32[]{:S(2)}, u32[]{:S(2)}) %collective-permute-start.29) | collective-permute-done | bytes 196640 | tf_op jit(solution)/shard_map/ppermute | solution.py:235
  56.9 2.4 collective-permute-start.31
  61.8 1.7 collective-permute-done.31
  63.6 2.5 collective-permute-start.13
  68.5 1.6 collective-permute-start.17
  70.2 26.0 %collective-permute-done.12 = bf16[4,6,3,32,128]{4,3,2,1,0:T(8,128)(2,1)S(1)} collective-permute-done((bf16[4,6,3,32,128]{4,3,2,1,0:T(8,128)(2,1)S(1)}, bf16[4,6,3,32,128]{4,3,2,1,0:T(8,128)(2,1)S(1)}, u32[]{:S(2)}, u32[]{:S(2)}) %collective-permute-start.12) | collective-permute-done | bytes 589856 | tf_op jit(solution)/shard_map/ppermute | solution.py:235
  96.2 1.3 collective-permute-start.23
  97.6 1.6 collective-permute-start.18
  99.4 1.7 constant_dynamic-update-slice_fusion.1
  101.9 6.3 %collective-permute-done.23 = bf16[4,4,3,32,128]{4,3,2,1,0:T(8,128)(2,1)S(1)} collective-permute-done((bf16[4,4,3,32,128]{4,3,2,1,0:T(8,128)(2,1)S(1)}, bf16[4,4,3,32,128]{4,3,2,1,0:T(8,128)(2,1)S(1)}, u32[]{:S(2)}, u32[]{:S(2)}) %collective-permute-start.23) | collective-permute-done | bytes 393248 | tf_op jit(solution)/shard_map/ppermute | solution.py:235
  108.3 1.2 collective-permute-start.24
  109.6 21.1 %collective-permute-done.18 = bf16[4,6,3,32,128]{4,3,2,1,0:T(8,128)(2,1)S(1)} collective-permute-done((bf16[4,6,3,32,128]{4,3,2,1,0:T(8,128)(2,1)S(1)}, bf16[4,6,3,32,128]{4,3,2,1,0:T(8,128)(2,1)S(1)}, u32[]{:S(2)}, u32[]{:S(2)}) %collective-permute-start.18) | collective-permute-done | bytes 589856 | tf_op jit(solution)/shard_map/ppermute | solution.py:235
  130.8 1.5 collective-permute-start.25
  132.5 4.0 %collective-permute-start.8 = (bf16[4,384,128]{2,1,0:T(8,128)(2,1)S(1)}, bf16[4,384,128]{2,1,0:T(8,128)(2,1)S(1)}, u32[]{:S(2)}, u32[]{:S(2)}) collective-permute-start(bf16[4,384,128]{2,1,0:T(8,128)(2,1)S(1)} %bitcast.120), channel_id=1, source_target_pairs={{0,8},{8,16},{16,24},{1,9},{9,17},{17,25},{2,10},{10,18},{18,26},{... | collective-permute-start | bytes 1179656 | tf_op jit(solution)/shard_map/ppermute | solution.py:241
  136.6 4.3 %collective-permute-done.24 = bf16[4,4,3,32,128]{4,3,2,1,0:T(8,128)(2,1)S(1)} collective-permute-done((bf16[4,4,3,32,128]{4,3,2,1,0:T(8,128)(2,1)S(1)}, bf16[4,4,3,32,128]{4,3,2,1,0:T(8,128)(2,1)S(1)}, u32[]{:S(2)}, u32[]{:S(2)}) %collective-permute-start.24) | collective-permute-done | bytes 393248 | tf_op jit(solution)/shard_map/ppermute | solution.py:235
  140.9 1.3 collective-permute-start.9
  144.3 5.5 %collective-permute-start.14 = (bf16[6,384,128]{2,1,0:T(8,128)(2,1)}, bf16[6,384,128]{2,1,0:T(8,128)(2,1)}, u32[]{:S(2)}, u32[]{:S(2)}) collective-permute-start(bf16[6,384,128]{2,1,0:T(8,128)(2,1)} %bitcast.62), channel_id=1, source_target_pairs={{0,8},{8,16},{16,24},{1,9},{9,17},{17,25},{2,10},{10,18},{18,26},{... | collective-permute-start | bytes 1769480 | tf_op jit(solution)/shard_map/ppermute | solution.py:241
  149.8 4.7 %collective-permute-done.9.refs_4_.refs_9_ = bf16[4,384,128]{2,1,0:T(8,128)(2,1)S(1)} collective-permute-done((bf16[4,384,128]{2,1,0:T(8,128)(2,1)S(1)}, bf16[4,384,128]{2,1,0:T(8,128)(2,1)S(1)}, u32[]{:S(2)}, u32[]{:S(2)}) %collective-permute-start.9) | collective-permute-done | bytes 393248 | tf_op jit(solution)/shard_map/ppermute | solution.py:244
  155.2 1.3 collective-permute-start.15
  156.6 5.2 %collective-permute-start.32 = (bf16[2,384,128]{2,1,0:T(8,128)(2,1)}, bf16[2,384,128]{2,1,0:T(8,128)(2,1)}, u32[]{:S(2)}, u32[]{:S(2)}) collective-permute-start(bf16[2,384,128]{2,1,0:T(8,128)(2,1)} %bitcast.71), channel_id=1, source_target_pairs={{0,8},{8,16},{16,24},{1,9},{9,17},{17,25},{2,10},{10,18},{18,26},{... | collective-permute-start | bytes 589832 | tf_op jit(solution)/shard_map/ppermute | solution.py:241
  162.6 9.6 %load.5.refs_2_ = f32[256,128]{1,0:T(8,128)} custom-call(f32[2,4,54,128]{3,2,1,0:T(8,128)} %get-tuple-element.57.refs_0_, f32[128,128]{1,0:T(8,128)} %broadcast_in_dim.2.refs_1_, bf16[4,4,384,128]{3,2,1,0:T(8,128)(2,1)} %bitcast.110, bf16[4,384,128]{2,1,0:T(8,128)(2,1)} %copy-done.31, bf16[4,384,128]{2,1,0:T(8,128)(2,1)} %copy-done.32, ...), custom_call_target="tpu_custom_call" | custom-call | flops 3623878656 | bytes 1572864 | tf_op jit(solution)/shard_map/load/pallas_call | solution.py:173
  172.3 3.7 %collective-permute-start.20 = (bf16[6,384,128]{2,1,0:T(8,128)(2,1)S(1)}, bf16[6,384,128]{2,1,0:T(8,128)(2,1)S(1)}, u32[]{:S(2)}, u32[]{:S(2)}) collective-permute-start(bf16[6,384,128]{2,1,0:T(8,128)(2,1)S(1)} %bitcast.113), channel_id=1, source_target_pairs={{0,8},{8,16},{16,24},{1,9},{9,17},{17,25},{2,10},{10,18},{18,26},{... | collective-permute-start | bytes 1769480 | tf_op jit(solution)/shard_map/ppermute | solution.py:241
  175.9 1.5 collective-permute-start.21
  177.4 23.0 %load.6.refs_2_ = f32[256,128]{1,0:T(8,128)} custom-call(f32[6,4,54,128]{3,2,1,0:T(8,128)} %get-tuple-element.59.refs_0_, f32[128,128]{1,0:T(8,128)} %broadcast_in_dim.2.refs_1_, f32[256,128]{1,0:T(8,128)} %load.5.refs_2_, bf16[4,6,384,128]{3,2,1,0:T(8,128)(2,1)} %bitcast.104, bf16[6,384,128]{2,1,0:T(8,128)(2,1)} %collective-permute-done.14.refs_4_.refs_8_, ...), custom_call_target="tpu_custom_call" | custom-call | flops 10871635968 | bytes 4718592 | tf_op jit(solution)/shard_map/load/pallas_call | solution.py:173
  200.6 4.6 %collective-permute-start.26 = (bf16[4,384,128]{2,1,0:T(8,128)(2,1)S(1)}, bf16[4,384,128]{2,1,0:T(8,128)(2,1)S(1)}, u32[]{:S(2)}, u32[]{:S(2)}) collective-permute-start(bf16[4,384,128]{2,1,0:T(8,128)(2,1)S(1)} %bitcast.118), channel_id=1, source_target_pairs={{0,8},{8,16},{16,24},{1,9},{9,17},{17,25},{2,10},{10,18},{18,26},{... | collective-permute-start | bytes 1179656 | tf_op jit(solution)/shard_map/ppermute | solution.py:241
  205.2 1.3 collective-permute-start.27
  206.6 23.0 %load.7.refs_2_ = f32[256,128]{1,0:T(8,128)} custom-call(f32[6,4,54,128]{3,2,1,0:T(8,128)} %get-tuple-element.60.refs_0_, f32[128,128]{1,0:T(8,128)} %broadcast_in_dim.2.refs_1_, f32[256,128]{1,0:T(8,128)} %load.6.refs_2_, bf16[4,6,384,128]{3,2,1,0:T(8,128)(2,1)} %bitcast.101, bf16[6,384,128]{2,1,0:T(8,128)(2,1)} %copy-done.25, ...), custom_call_target="tpu_custom_call" | custom-call | flops 10871635968 | bytes 4718592 | tf_op jit(solution)/shard_map/load/pallas_call | solution.py:173
  229.6 1.3 collective-permute-start.33
  231.6 16.3 %load.8.refs_2_ = f32[256,128]{1,0:T(8,128)} custom-call(f32[4,4,54,128]{3,2,1,0:T(8,128)} %slice.215.refs_0_, f32[128,128]{1,0:T(8,128)} %broadcast_in_dim.2.refs_1_, f32[256,128]{1,0:T(8,128)} %load.7.refs_2_, bf16[4,4,384,128]{3,2,1,0:T(8,128)(2,1)} %bitcast.107, bf16[4,384,128]{2,1,0:T(8,128)(2,1)} %copy-done.33, bf16[4,384,128]{2,1,0:T(8,128)(2,1)} %copy-done.34, ...), custom_call_target="tpu_custom_call" | custom-call | flops 7247757312 | bytes 3145728 | tf_op jit(solution)/shard_map/load/pallas_call | solution.py:173
  248.6 9.6 %load.9.s_ref = f32[256,128]{1,0:T(8,128)} custom-call(f32[2,4,54,128]{3,2,1,0:T(8,128)} %get-tuple-element.58.refs_0_, f32[128,128]{1,0:T(8,128)} %broadcast_in_dim.2.refs_1_, f32[256,128]{1,0:T(8,128)} %load.8.refs_2_, bf16[4,2,384,128]{3,2,1,0:T(8,128)(2,1)} %bitcast.115, bf16[2,384,128]{2,1,0:T(8,128)(2,1)} %collective-permute-done.32.refs_4_, ...), custom_call_target="tpu_custom_call" | custom-call | flops 3623878656 | bytes 1572864 | tf_op jit(solution)/shard_map/load/pallas_call | solution.py:173
  258.2 1.7 arrange.1
  260.0 1.5 collective-permute-start.37
  262.4 1.1 collective-permute-start.35
  263.4 1.5 collective-permute-done.37
  267.3 5.9 %collective-permute-start.40 = (f32[64,128]{1,0:T(8,128)S(1)}, f32[64,128]{1,0:T(8,128)S(1)}, u32[]{:S(2)}, u32[]{:S(2)}) collective-permute-start(f32[64,128]{1,0:T(8,128)S(1)} %add_add_fusion), channel_id=1, source_target_pairs={{0,24},{8,0},{16,8},{24,16},{1,25},{9,1},{17,9},{25,17},{2,26},{10... | collective-permute-start | bytes 98312 | tf_op jit(solution)/shard_map/ppermute | solution.py:293
  274.8 3.2 %collective-permute-done.39 = f32[64,128]{1,0:T(8,128)S(1)} collective-permute-done((f32[64,128]{1,0:T(8,128)S(1)}, f32[64,128]{1,0:T(8,128)S(1)}, u32[]{:S(2)}, u32[]{:S(2)}) %collective-permute-start.39) | collective-permute-done | bytes 32800 | tf_op jit(solution)/shard_map/ppermute | solution.py:293
  (159 shorter events, 32.1 us)
Async XLA Ops:
  0.0 30.0 %collective-permute-start.4 = (f32[32]{0:T(128)}, f32[32]{0:T(128)S(1)}, u32[]{:S(2)}, u32[]{:S(2)}) collective-permute-start(f32[32]{0:T(128)} %param.9), channel_id=1, source_target_pairs={{0,6},{1,7},{2,4},{3,5},{4,2},{5,3},{6,0},{7,1},{8,14},{9,15},{10,... | collective-permute-start | bytes 392 | tf_op jit(solution)/shard_map/ppermute | solution.py:235
  3.9 27.6 %collective-permute-start.3 = (f32[32]{0:T(128)}, f32[32]{0:T(128)S(1)}, u32[]{:S(2)}, u32[]{:S(2)}) collective-permute-start(f32[32]{0:T(128)} %param.9), channel_id=1, source_target_pairs={{0,4},{1,5},{2,6},{3,7},{4,0},{5,1},{6,2},{7,3},{8,12},{9,13},{10,... | collective-permute-start | bytes 392 | tf_op jit(solution)/shard_map/ppermute | solution.py:235
  4.4 28.6 %collective-permute-start.2 = (f32[32]{0:T(128)}, f32[32]{0:T(128)S(1)}, u32[]{:S(2)}, u32[]{:S(2)}) collective-permute-start(f32[32]{0:T(128)} %param.9), channel_id=1, source_target_pairs={{0,2},{1,3},{2,0},{3,1},{4,6},{5,7},{6,4},{7,5},{8,10},{9,11},{10,... | collective-permute-start | bytes 392 | tf_op jit(solution)/shard_map/ppermute | solution.py:235
  5.3 28.9 %collective-permute-start = (f32[1,80,128]{2,0,1:T(1,128)S(1)}, f32[1,80,128]{2,0,1:T(1,128)S(1)}, u32[]{:S(2)}, u32[]{:S(2)}) collective-permute-start(f32[1,80,128]{2,0,1:T(1,128)S(1)} %bitcast.150), channel_id=1, source_target_pairs={{0,8},{8,16},{16,24},{1,9},{9,17},{17,25},{2,10},{10,18},{18,26},{... | collective-permute-start | bytes 122888 | tf_op jit(solution)/shard_map/ppermute | solution.py:241
  9.2 26.4 %collective-permute-start.1 = (f32[1,80,128]{2,0,1:T(1,128)S(1)}, f32[1,80,128]{2,0,1:T(1,128)S(1)}, u32[]{:S(2)}, u32[]{:S(2)}) collective-permute-start(f32[1,80,128]{2,0,1:T(1,128)S(1)} %bitcast.149), channel_id=1, source_target_pairs={{8,0},{16,8},{24,16},{9,1},{17,9},{25,17},{10,2},{18,10},{26,18},{... | collective-permute-start | bytes 122888 | tf_op jit(solution)/shard_map/ppermute | solution.py:244
  30.0 36.9 %collective-permute-start.5 = (bf16[4,4,3,32,128]{4,3,2,1,0:T(8,128)(2,1)}, bf16[4,4,3,32,128]{4,3,2,1,0:T(8,128)(2,1)}, u32[]{:S(2)}, u32[]{:S(2)}) collective-permute-start(bf16[4,4,3,32,128]{4,3,2,1,0:T(8,128)(2,1)} %get-tuple-element.30), channel_id=1, source_target_pairs={{0,2},{1,3},{2,0},{3,1},{4,6},{5,7},{6,4},{7,5},{8,10},{9,11},{10,... | collective-permute-start | bytes 1179656 | tf_op jit(solution)/shard_map/ppermute | solution.py:235
  31.5 67.8 %collective-permute-start.6 = (bf16[4,4,3,32,128]{4,3,2,1,0:T(8,128)(2,1)}, bf16[4,4,3,32,128]{4,3,2,1,0:T(8,128)(2,1)}, u32[]{:S(2)}, u32[]{:S(2)}) collective-permute-start(bf16[4,4,3,32,128]{4,3,2,1,0:T(8,128)(2,1)} %get-tuple-element.31), channel_id=1, source_target_pairs={{0,4},{1,5},{2,6},{3,7},{4,0},{5,1},{6,2},{7,3},{8,12},{9,13},{10,... | collective-permute-start | bytes 1179656 | tf_op jit(solution)/shard_map/ppermute | solution.py:235
  33.0 35.5 %collective-permute-start.11 = (bf16[4,6,3,32,128]{4,3,2,1,0:T(8,128)(2,1)}, bf16[4,6,3,32,128]{4,3,2,1,0:T(8,128)(2,1)S(1)}, u32[]{:S(2)}, u32[]{:S(2)}) collective-permute-start(bf16[4,6,3,32,128]{4,3,2,1,0:T(8,128)(2,1)} %get-tuple-element.34), channel_id=1, source_target_pairs={{0,2},{1,3},{2,0},{3,1},{4,6},{5,7},{6,4},{7,5},{8,10},{9,11},{10,... | collective-permute-start | bytes 1769480 | tf_op jit(solution)/shard_map/ppermute | solution.py:235
  34.1 22.7 %collective-permute-start.29 = (bf16[4,2,3,32,128]{4,3,2,1,0:T(8,128)(2,1)}, bf16[4,2,3,32,128]{4,3,2,1,0:T(8,128)(2,1)}, u32[]{:S(2)}, u32[]{:S(2)}) collective-permute-start(bf16[4,2,3,32,128]{4,3,2,1,0:T(8,128)(2,1)} %get-tuple-element.46), channel_id=1, source_target_pairs={{0,2},{1,3},{2,0},{3,1},{4,6},{5,7},{6,4},{7,5},{8,10},{9,11},{10,... | collective-permute-start | bytes 589832 | tf_op jit(solution)/shard_map/ppermute | solution.py:235
  35.6 24.7 %collective-permute-start.30 = (bf16[4,2,3,32,128]{4,3,2,1,0:T(8,128)(2,1)}, bf16[4,2,3,32,128]{4,3,2,1,0:T(8,128)(2,1)}, u32[]{:S(2)}, u32[]{:S(2)}) collective-permute-start(bf16[4,2,3,32,128]{4,3,2,1,0:T(8,128)(2,1)} %get-tuple-element.47), channel_id=1, source_target_pairs={{0,4},{1,5},{2,6},{3,7},{4,0},{5,1},{6,2},{7,3},{8,12},{9,13},{10,... | collective-permute-start | bytes 589832 | tf_op jit(solution)/shard_map/ppermute | solution.py:235
  56.9 6.7 %collective-permute-start.31 = (bf16[4,2,3,32,128]{4,3,2,1,0:T(8,128)(2,1)S(1)}, bf16[4,2,3,32,128]{4,3,2,1,0:T(8,128)(2,1)S(1)}, u32[]{:S(2)}, u32[]{:S(2)}) collective-permute-start(bf16[4,2,3,32,128]{4,3,2,1,0:T(8,128)(2,1)S(1)} %copy-done.35), channel_id=1, source_target_pairs={{0,6},{1,7},{2,4},{3,5},{4,2},{5,3},{6,0},{7,1},{8,14},{9,15},{10,... | collective-permute-start | bytes 589832 | tf_op jit(solution)/shard_map/ppermute | solution.py:235
  60.3 35.9 %collective-permute-start.12 = (bf16[4,6,3,32,128]{4,3,2,1,0:T(8,128)(2,1)S(1)}, bf16[4,6,3,32,128]{4,3,2,1,0:T(8,128)(2,1)S(1)}, u32[]{:S(2)}, u32[]{:S(2)}) collective-permute-start(bf16[4,6,3,32,128]{4,3,2,1,0:T(8,128)(2,1)S(1)} %copy-done.24), channel_id=1, source_target_pairs={{0,4},{1,5},{2,6},{3,7},{4,0},{5,1},{6,2},{7,3},{8,12},{9,13},{10,... | collective-permute-start | bytes 1769480 | tf_op jit(solution)/shard_map/ppermute | solution.py:235
  63.6 32.6 %copy-start.30 = (bf16[4,4,3,32,128]{4,3,2,1,0:T(8,128)(2,1)S(1)}, bf16[4,4,3,32,128]{4,3,2,1,0:T(8,128)(2,1)}, u32[]{:S(2)}) copy-start(bf16[4,4,3,32,128]{4,3,2,1,0:T(8,128)(2,1)} %get-tuple-element.42) | copy-start | bytes 1179652
  63.6 34.0 %collective-permute-start.13 = (bf16[4,6,3,32,128]{4,3,2,1,0:T(8,128)(2,1)S(1)}, bf16[4,6,3,32,128]{4,3,2,1,0:T(8,128)(2,1)S(1)}, u32[]{:S(2)}, u32[]{:S(2)}) collective-permute-start(bf16[4,6,3,32,128]{4,3,2,1,0:T(8,128)(2,1)S(1)} %copy-done.23), channel_id=1, source_target_pairs={{0,6},{1,7},{2,4},{3,5},{4,2},{5,3},{6,0},{7,1},{8,14},{9,15},{10,... | collective-permute-start | bytes 1769480 | tf_op jit(solution)/shard_map/ppermute | solution.py:235
  66.0 31.5 %copy-start.10 = (bf16[4,2,3,128,128]{4,3,2,1,0:T(8,128)(2,1)}, bf16[4,2,3,128,128]{4,3,2,1,0:T(8,128)(2,1)S(1)}, u32[]{:S(2)}) copy-start(bf16[4,2,3,128,128]{4,3,2,1,0:T(8,128)(2,1)S(1)} %constant_dynamic-update-slice_fusion.16) | copy-start | bytes 2359300
  66.9 30.7 %copy-start.21 = (bf16[4,6,3,32,128]{4,3,2,1,0:T(8,128)(2,1)S(1)}, bf16[4,6,3,32,128]{4,3,2,1,0:T(8,128)(2,1)}, u32[]{:S(2)}) copy-start(bf16[4,6,3,32,128]{4,3,2,1,0:T(8,128)(2,1)} %get-tuple-element.39) | copy-start | bytes 1769476
  66.9 34.2 %collective-permute-start.7 = (bf16[4,4,3,32,128]{4,3,2,1,0:T(8,128)(2,1)S(1)}, bf16[4,4,3,32,128]{4,3,2,1,0:T(8,128)(2,1)S(1)}, u32[]{:S(2)}, u32[]{:S(2)}) collective-permute-start(bf16[4,4,3,32,128]{4,3,2,1,0:T(8,128)(2,1)S(1)} %copy-done.29), channel_id=1, source_target_pairs={{0,6},{1,7},{2,4},{3,5},{4,2},{5,3},{6,0},{7,1},{8,14},{9,15},{10,... | collective-permute-start | bytes 1179656 | tf_op jit(solution)/shard_map/ppermute | solution.py:235
  68.5 39.8 %collective-permute-start.17 = (bf16[4,6,3,32,128]{4,3,2,1,0:T(8,128)(2,1)S(1)}, bf16[4,6,3,32,128]{4,3,2,1,0:T(8,128)(2,1)S(1)}, u32[]{:S(2)}, u32[]{:S(2)}) collective-permute-start(bf16[4,6,3,32,128]{4,3,2,1,0:T(8,128)(2,1)S(1)} %copy-done.22), channel_id=1, source_target_pairs={{0,2},{1,3},{2,0},{3,1},{4,6},{5,7},{6,4},{7,5},{8,10},{9,11},{10,... | collective-permute-start | bytes 1769480 | tf_op jit(solution)/shard_map/ppermute | solution.py:235
  96.2 12.1 %collective-permute-start.23 = (bf16[4,4,3,32,128]{4,3,2,1,0:T(8,128)(2,1)S(1)}, bf16[4,4,3,32,128]{4,3,2,1,0:T(8,128)(2,1)S(1)}, u32[]{:S(2)}, u32[]{:S(2)}) collective-permute-start(bf16[4,4,3,32,128]{4,3,2,1,0:T(8,128)(2,1)S(1)} %copy-done.30), channel_id=1, source_target_pairs={{0,2},{1,3},{2,0},{3,1},{4,6},{5,7},{6,4},{7,5},{8,10},{9,11},{10,... | collective-permute-start | bytes 1179656 | tf_op jit(solution)/shard_map/ppermute | solution.py:235
  97.6 33.2 %collective-permute-start.18 = (bf16[4,6,3,32,128]{4,3,2,1,0:T(8,128)(2,1)S(1)}, bf16[4,6,3,32,128]{4,3,2,1,0:T(8,128)(2,1)S(1)}, u32[]{:S(2)}, u32[]{:S(2)}) collective-permute-start(bf16[4,6,3,32,128]{4,3,2,1,0:T(8,128)(2,1)S(1)} %copy-done.21), channel_id=1, source_target_pairs={{0,4},{1,5},{2,6},{3,7},{4,0},{5,1},{6,2},{7,3},{8,12},{9,13},{10,... | collective-permute-start | bytes 1769480 | tf_op jit(solution)/shard_map/ppermute | solution.py:235
  99.3 44.1 %copy-start.3 = (bf16[4,6,3,128,128]{4,3,2,1,0:T(8,128)(2,1)}, bf16[4,6,3,128,128]{4,3,2,1,0:T(8,128)(2,1)S(1)}, u32[]{:S(2)}) copy-start(bf16[4,6,3,128,128]{4,3,2,1,0:T(8,128)(2,1)S(1)} %constant_dynamic-update-slice_fusion.4) | copy-start | bytes 7077892
  99.3 76.6 %collective-permute-start.16 = (bf16[4,6,384,128]{3,2,1,0:T(8,128)(2,1)S(1)}, bf16[4,6,384,128]{3,2,1,0:T(8,128)(2,1)}, u32[]{:S(2)}, u32[]{:S(2)}) collective-permute-start(bf16[4,6,384,128]{3,2,1,0:T(8,128)(2,1)S(1)} %bitcast.103), channel_id=1, source_target_pairs={{0,1},{1,0},{2,3},{3,2},{4,5},{5,4},{6,7},{7,6},{8,9},{9,8},{10,11... | collective-permute-start | bytes 7077896 | tf_op jit(solution)/shard_map/ppermute | solution.py:238
  101.1 31.2 %copy-start = (bf16[4,6,3,128,128]{4,3,2,1,0:T(8,128)(2,1)S(1)}, bf16[4,6,3,128,128]{4,3,2,1,0:T(8,128)(2,1)}, u32[]{:S(2)}) copy-start(bf16[4,6,3,128,128]{4,3,2,1,0:T(8,128)(2,1)} %get-tuple-element.101) | copy-start | bytes 7077892
  101.1 31.4 %collective-permute-start.19 = (bf16[4,6,3,32,128]{4,3,2,1,0:T(8,128)(2,1)S(1)}, bf16[4,6,3,32,128]{4,3,2,1,0:T(8,128)(2,1)S(1)}, u32[]{:S(2)}, u32[]{:S(2)}) collective-permute-start(bf16[4,6,3,32,128]{4,3,2,1,0:T(8,128)(2,1)S(1)} %copy-done.20), channel_id=1, source_target_pairs={{0,6},{1,7},{2,4},{3,5},{4,2},{5,3},{6,0},{7,1},{8,14},{9,15},{10,... | collective-permute-start | bytes 1769480 | tf_op jit(solution)/shard_map/ppermute | solution.py:235
  101.9 30.5 %copy-start.6 = (bf16[4,4,3,128,128]{4,3,2,1,0:T(8,128)(2,1)}, bf16[4,4,3,128,128]{4,3,2,1,0:T(8,128)(2,1)S(1)}, u32[]{:S(2)}) copy-start(bf16[4,4,3,128,128]{4,3,2,1,0:T(8,128)(2,1)S(1)} %constant_dynamic-update-slice_fusion) | copy-start | bytes 4718596
  108.2 48.4 %collective-permute-start.10 = (bf16[4,4,384,128]{3,2,1,0:T(8,128)(2,1)S(1)}, bf16[4,4,384,128]{3,2,1,0:T(8,128)(2,1)S(1)}, u32[]{:S(2)}, u32[]{:S(2)}) collective-permute-start(bf16[4,4,384,128]{3,2,1,0:T(8,128)(2,1)S(1)} %bitcast.109), channel_id=1, source_target_pairs={{0,1},{1,0},{2,3},{3,2},{4,5},{5,4},{6,7},{7,6},{8,9},{9,8},{10,11... | collective-permute-start | bytes 4718600 | tf_op jit(solution)/shard_map/ppermute | solution.py:238
  108.3 32.5 %collective-permute-start.24 = (bf16[4,4,3,32,128]{4,3,2,1,0:T(8,128)(2,1)S(1)}, bf16[4,4,3,32,128]{4,3,2,1,0:T(8,128)(2,1)S(1)}, u32[]{:S(2)}, u32[]{:S(2)}) collective-permute-start(bf16[4,4,3,32,128]{4,3,2,1,0:T(8,128)(2,1)S(1)} %copy-done.28), channel_id=1, source_target_pairs={{0,4},{1,5},{2,6},{3,7},{4,0},{5,1},{6,2},{7,3},{8,12},{9,13},{10,... | collective-permute-start | bytes 1179656 | tf_op jit(solution)/shard_map/ppermute | solution.py:235
  130.8 10.2 %collective-permute-start.25 = (bf16[4,4,3,32,128]{4,3,2,1,0:T(8,128)(2,1)S(1)}, bf16[4,4,3,32,128]{4,3,2,1,0:T(8,128)(2,1)S(1)}, u32[]{:S(2)}, u32[]{:S(2)}) collective-permute-start(bf16[4,4,3,32,128]{4,3,2,1,0:T(8,128)(2,1)S(1)} %copy-done.27), channel_id=1, source_target_pairs={{0,6},{1,7},{2,4},{3,5},{4,2},{5,3},{6,0},{7,1},{8,14},{9,15},{10,... | collective-permute-start | bytes 1179656 | tf_op jit(solution)/shard_map/ppermute | solution.py:235
  132.5 11.8 %collective-permute-start.8 = (bf16[4,384,128]{2,1,0:T(8,128)(2,1)S(1)}, bf16[4,384,128]{2,1,0:T(8,128)(2,1)S(1)}, u32[]{:S(2)}, u32[]{:S(2)}) collective-permute-start(bf16[4,384,128]{2,1,0:T(8,128)(2,1)S(1)} %bitcast.120), channel_id=1, source_target_pairs={{0,8},{8,16},{16,24},{1,9},{9,17},{17,25},{2,10},{10,18},{18,26},{... | collective-permute-start | bytes 1179656 | tf_op jit(solution)/shard_map/ppermute | solution.py:241
  140.9 64.4 %collective-permute-start.22 = (bf16[4,6,384,128]{3,2,1,0:T(8,128)(2,1)S(1)}, bf16[4,6,384,128]{3,2,1,0:T(8,128)(2,1)}, u32[]{:S(2)}, u32[]{:S(2)}) collective-permute-start(bf16[4,6,384,128]{3,2,1,0:T(8,128)(2,1)S(1)} %bitcast.100), channel_id=1, source_target_pairs={{0,1},{1,0},{2,3},{3,2},{4,5},{5,4},{6,7},{7,6},{8,9},{9,8},{10,11... | collective-permute-start | bytes 7077896 | tf_op jit(solution)/shard_map/ppermute | solution.py:238
  140.9 13.5 %collective-permute-start.9 = (bf16[4,384,128]{2,1,0:T(8,128)(2,1)S(1)}, bf16[4,384,128]{2,1,0:T(8,128)(2,1)S(1)}, u32[]{:S(2)}, u32[]{:S(2)}) collective-permute-start(bf16[4,384,128]{2,1,0:T(8,128)(2,1)S(1)} %bitcast.119), channel_id=1, source_target_pairs={{8,0},{16,8},{24,16},{9,1},{17,9},{25,17},{10,2},{18,10},{26,18},{... | collective-permute-start | bytes 1179656 | tf_op jit(solution)/shard_map/ppermute | solution.py:244
  142.3 29.8 %copy-start.4 = (bf16[4,4,3,128,128]{4,3,2,1,0:T(8,128)(2,1)}, bf16[4,4,3,128,128]{4,3,2,1,0:T(8,128)(2,1)S(1)}, u32[]{:S(2)}) copy-start(bf16[4,4,3,128,128]{4,3,2,1,0:T(8,128)(2,1)S(1)} %constant_dynamic-update-slice_fusion.12) | copy-start | bytes 4718596
  144.3 27.9 %collective-permute-start.14 = (bf16[6,384,128]{2,1,0:T(8,128)(2,1)}, bf16[6,384,128]{2,1,0:T(8,128)(2,1)}, u32[]{:S(2)}, u32[]{:S(2)}) collective-permute-start(bf16[6,384,128]{2,1,0:T(8,128)(2,1)} %bitcast.62), channel_id=1, source_target_pairs={{0,8},{8,16},{16,24},{1,9},{9,17},{17,25},{2,10},{10,18},{18,26},{... | collective-permute-start | bytes 1769480 | tf_op jit(solution)/shard_map/ppermute | solution.py:241
  155.2 17.1 %collective-permute-start.15 = (bf16[6,384,128]{2,1,0:T(8,128)(2,1)S(1)}, bf16[6,384,128]{2,1,0:T(8,128)(2,1)}, u32[]{:S(2)}, u32[]{:S(2)}) collective-permute-start(bf16[6,384,128]{2,1,0:T(8,128)(2,1)S(1)} %bitcast.114), channel_id=1, source_target_pairs={{8,0},{16,8},{24,16},{9,1},{17,9},{25,17},{10,2},{18,10},{26,18},{... | collective-permute-start | bytes 1769480 | tf_op jit(solution)/shard_map/ppermute | solution.py:244
  156.6 91.3 %collective-permute-start.32 = (bf16[2,384,128]{2,1,0:T(8,128)(2,1)}, bf16[2,384,128]{2,1,0:T(8,128)(2,1)}, u32[]{:S(2)}, u32[]{:S(2)}) collective-permute-start(bf16[2,384,128]{2,1,0:T(8,128)(2,1)} %bitcast.71), channel_id=1, source_target_pairs={{0,8},{8,16},{16,24},{1,9},{9,17},{17,25},{2,10},{10,18},{18,26},{... | collective-permute-start | bytes 589832 | tf_op jit(solution)/shard_map/ppermute | solution.py:241
  172.2 58.7 %collective-permute-start.28 = (bf16[4,4,384,128]{3,2,1,0:T(8,128)(2,1)S(1)}, bf16[4,4,384,128]{3,2,1,0:T(8,128)(2,1)}, u32[]{:S(2)}, u32[]{:S(2)}) collective-permute-start(bf16[4,4,384,128]{3,2,1,0:T(8,128)(2,1)S(1)} %bitcast.106), channel_id=1, source_target_pairs={{0,1},{1,0},{2,3},{3,2},{4,5},{5,4},{6,7},{7,6},{8,9},{9,8},{10,11... | collective-permute-start | bytes 4718600 | tf_op jit(solution)/shard_map/ppermute | solution.py:238
  172.3 28.2 %collective-permute-start.20 = (bf16[6,384,128]{2,1,0:T(8,128)(2,1)S(1)}, bf16[6,384,128]{2,1,0:T(8,128)(2,1)S(1)}, u32[]{:S(2)}, u32[]{:S(2)}) collective-permute-start(bf16[6,384,128]{2,1,0:T(8,128)(2,1)S(1)} %bitcast.113), channel_id=1, source_target_pairs={{0,8},{8,16},{16,24},{1,9},{9,17},{17,25},{2,10},{10,18},{18,26},{... | collective-permute-start | bytes 1769480 | tf_op jit(solution)/shard_map/ppermute | solution.py:241
  175.9 24.7 %collective-permute-start.21 = (bf16[6,384,128]{2,1,0:T(8,128)(2,1)S(1)}, bf16[6,384,128]{2,1,0:T(8,128)(2,1)S(1)}, u32[]{:S(2)}, u32[]{:S(2)}) collective-permute-start(bf16[6,384,128]{2,1,0:T(8,128)(2,1)S(1)} %bitcast.112), channel_id=1, source_target_pairs={{8,0},{16,8},{24,16},{9,1},{17,9},{25,17},{10,2},{18,10},{26,18},{... | collective-permute-start | bytes 1769480 | tf_op jit(solution)/shard_map/ppermute | solution.py:244
  200.5 47.4 %collective-permute-start.34 = (bf16[4,2,384,128]{3,2,1,0:T(8,128)(2,1)S(1)}, bf16[4,2,384,128]{3,2,1,0:T(8,128)(2,1)}, u32[]{:S(2)}, u32[]{:S(2)}) collective-permute-start(bf16[4,2,384,128]{3,2,1,0:T(8,128)(2,1)S(1)} %bitcast.116), channel_id=1, source_target_pairs={{0,1},{1,0},{2,3},{3,2},{4,5},{5,4},{6,7},{7,6},{8,9},{9,8},{10,11... | collective-permute-start | bytes 2359304 | tf_op jit(solution)/shard_map/ppermute | solution.py:238
  200.6 28.9 %collective-permute-start.26 = (bf16[4,384,128]{2,1,0:T(8,128)(2,1)S(1)}, bf16[4,384,128]{2,1,0:T(8,128)(2,1)S(1)}, u32[]{:S(2)}, u32[]{:S(2)}) collective-permute-start(bf16[4,384,128]{2,1,0:T(8,128)(2,1)S(1)} %bitcast.118), channel_id=1, source_target_pairs={{0,8},{8,16},{16,24},{1,9},{9,17},{17,25},{2,10},{10,18},{18,26},{... | collective-permute-start | bytes 1179656 | tf_op jit(solution)/shard_map/ppermute | solution.py:241
  205.2 25.6 %collective-permute-start.27 = (bf16[4,384,128]{2,1,0:T(8,128)(2,1)S(1)}, bf16[4,384,128]{2,1,0:T(8,128)(2,1)S(1)}, u32[]{:S(2)}, u32[]{:S(2)}) collective-permute-start(bf16[4,384,128]{2,1,0:T(8,128)(2,1)S(1)} %bitcast.117), channel_id=1, source_target_pairs={{8,0},{16,8},{24,16},{9,1},{17,9},{25,17},{10,2},{18,10},{26,18},{... | collective-permute-start | bytes 1179656 | tf_op jit(solution)/shard_map/ppermute | solution.py:244
  229.6 18.3 %collective-permute-start.33 = (bf16[2,384,128]{2,1,0:T(8,128)(2,1)S(1)}, bf16[2,384,128]{2,1,0:T(8,128)(2,1)S(1)}, u32[]{:S(2)}, u32[]{:S(2)}) collective-permute-start(bf16[2,384,128]{2,1,0:T(8,128)(2,1)S(1)} %bitcast.121), channel_id=1, source_target_pairs={{8,0},{16,8},{24,16},{9,1},{17,9},{25,17},{10,2},{18,10},{26,18},{... | collective-permute-start | bytes 589832 | tf_op jit(solution)/shard_map/ppermute | solution.py:244
  260.0 5.0 %collective-permute-start.37 = (f32[64,128]{1,0:T(8,128)}, f32[64,128]{1,0:T(8,128)S(1)}, u32[]{:S(2)}, u32[]{:S(2)}) collective-permute-start(f32[64,128]{1,0:T(8,128)} %get-tuple-element.52), channel_id=1, source_target_pairs={{0,6},{1,7},{2,4},{3,5},{4,2},{5,3},{6,0},{7,1},{8,14},{9,15},{10,... | collective-permute-start | bytes 98312 | tf_op jit(solution)/shard_map/ppermute | solution.py:235
  261.5 4.1 %collective-permute-start.36 = (f32[64,128]{1,0:T(8,128)}, f32[64,128]{1,0:T(8,128)S(1)}, u32[]{:S(2)}, u32[]{:S(2)}) collective-permute-start(f32[64,128]{1,0:T(8,128)} %get-tuple-element.51), channel_id=1, source_target_pairs={{0,4},{1,5},{2,6},{3,7},{4,0},{5,1},{6,2},{7,3},{8,12},{9,13},{10,... | collective-permute-start | bytes 98312 | tf_op jit(solution)/shard_map/ppermute | solution.py:235
  262.4 4.1 %collective-permute-start.35 = (f32[64,128]{1,0:T(8,128)}, f32[64,128]{1,0:T(8,128)S(1)}, u32[]{:S(2)}, u32[]{:S(2)}) collective-permute-start(f32[64,128]{1,0:T(8,128)} %get-tuple-element.50), channel_id=1, source_target_pairs={{0,2},{1,3},{2,0},{3,1},{4,6},{5,7},{6,4},{7,5},{8,10},{9,11},{10,... | collective-permute-start | bytes 98312 | tf_op jit(solution)/shard_map/ppermute | solution.py:235
  267.3 7.5 %collective-permute-start.40 = (f32[64,128]{1,0:T(8,128)S(1)}, f32[64,128]{1,0:T(8,128)S(1)}, u32[]{:S(2)}, u32[]{:S(2)}) collective-permute-start(f32[64,128]{1,0:T(8,128)S(1)} %add_add_fusion), channel_id=1, source_target_pairs={{0,24},{8,0},{16,8},{24,16},{1,25},{9,1},{17,9},{25,17},{2,26},{10... | collective-permute-start | bytes 98312 | tf_op jit(solution)/shard_map/ppermute | solution.py:293
  273.2 4.8 %collective-permute-start.39 = (f32[64,128]{1,0:T(8,128)S(1)}, f32[64,128]{1,0:T(8,128)S(1)}, u32[]{:S(2)}, u32[]{:S(2)}) collective-permute-start(f32[64,128]{1,0:T(8,128)S(1)} %add_add_fusion), channel_id=1, source_target_pairs={{0,16},{8,24},{16,0},{24,8},{1,17},{9,25},{17,1},{25,9},{2,18},{10... | collective-permute-start | bytes 98312 | tf_op jit(solution)/shard_map/ppermute | solution.py:293
  273.2 5.7 %collective-permute-start.38 = (f32[64,128]{1,0:T(8,128)S(1)}, f32[64,128]{1,0:T(8,128)S(1)}, u32[]{:S(2)}, u32[]{:S(2)}) collective-permute-start(f32[64,128]{1,0:T(8,128)S(1)} %add_add_fusion), channel_id=1, source_target_pairs={{0,8},{8,16},{16,24},{24,0},{1,9},{9,17},{17,25},{25,1},{2,10},{10... | collective-permute-start | bytes 98312 | tf_op jit(solution)/shard_map/ppermute | solution.py:293
  (30 other events, 367.5 us)

commit v2 on v1

--- a/solution.py
+++ b/solution.py
@@ -75,79 +75,106 @@
     return [outs[r * parts : (r + 1) * parts] for r in range(len(chunks))]
 
 
-def load_kernel(prev_rows, rows, own, *refs):
+def load_kernel(first_row, prev_rows, rows, own, parts, *refs):
     if prev_rows:
-        (u_ref, lam_ref, s_ref, f_ref, lo_ref, hi_ref, e_ref, fp_ref, lop_ref, hip_ref, ep_ref,
-         out_ref, win, other, g_ref, l_ref, sems) = refs
+        (thick_ref, tap_ref, lam_ref, s_ref, f_ref, lo_ref, hi_ref, e_ref, fp_ref, lop_ref, hip_ref, ep_ref,
+         out_ref, win, other, g0, g1, l_ref, sems) = refs
     else:
-        (u_ref, lam_ref, f_ref, lo_ref, hi_ref, e_ref,
-         out_ref, win, other, g_ref, l_ref, sems) = refs
+        (thick_ref, tap_ref, lam_ref, f_ref, lo_ref, hi_ref, e_ref,
+         out_ref, win, other, g0, g1, l_ref, sems) = refs
     planes = f_ref.shape[0]
     size_z = f_ref.shape[-1]
-    comps = f_ref.shape[2] // own
+    width = f_ref.shape[2]
+    comps = width // own
+    local = own // parts
     keep = 2 if prev_rows else 0
     done = rows - 2 + keep
-    copies = [
-        (f_ref, win.at[1 : 1 + planes, keep : keep + rows]),
-        (lo_ref, win.at[0, keep : keep + rows]),
-        (hi_ref, win.at[planes + 1, keep : keep + rows]),
-    ]
-    if prev_rows:
-        copies += [
-            (fp_ref.at[:, prev_rows - 2 : prev_rows], win.at[1 : 1 + planes, 0:2]),
-            (lop_ref.at[prev_rows - 2 : prev_rows], win.at[0, 0:2]),
-            (hip_ref.at[prev_rows - 2 : prev_rows], win.at[planes + 1, 0:2]),
-            (e_ref.at[:, 0 : rows - 1], other.at[:, 1:rows]),
-            (ep_ref.at[:, prev_rows - 1 : prev_rows], other.at[:, 0:1]),
+    started = []
+    for r in range(done + 2):
+        if r < keep:
+            at = prev_rows - 2 + r
+            sources = (fp_ref, lop_ref, hip_ref)
+        else:
+            at = r - keep
+            sources = (f_ref, lo_ref, hi_ref)
+        started += [
+            pltpu.make_async_copy(sources[0].at[:, at], win.at[1 : 1 + planes, r], sems.at[r, 0]),
+            pltpu.make_async_copy(sources[1].at[at], win.at[0, r], sems.at[r, 1]),
+            pltpu.make_async_copy(sources[2].at[at], win.at[planes + 1, r], sems.at[r, 2]),
         ]
-    else:
-        copies += [(e_ref.at[:, 1 : rows - 1], other)]
-    started = [pltpu.make_async_copy(src, dst, sems.at[n]) for n, (src, dst) in enumerate(copies)]
+        if 1 <= r <= done:
+            theirs = ep_ref if r < keep else e_ref
+            started += [pltpu.make_async_copy(theirs.at[:, at], other.at[:, r - 1], sems.at[r, 3])]
     for copy in started:
         copy.start()
+
+    def arrived(r):
+        pltpu.make_async_copy(f_ref.at[:, 0], win.at[1 : 1 + planes, r], sems.at[r, 0]).wait()
+        pltpu.make_async_copy(lo_ref.at[0], win.at[0, r], sems.at[r, 1]).wait()
+        pltpu.make_async_copy(hi_ref.at[0], win.at[planes + 1, r], sems.at[r, 2]).wait()
+
     if prev_rows:
         out_ref[...] = s_ref[...]
     else:
         out_ref[...] = jnp.zeros_like(out_ref)
-    for copy in started:
-        copy.wait()
 
     gap = lax.broadcasted_iota(jnp.int32, (size_z, size_z), 0) - lax.broadcasted_iota(
         jnp.int32, (size_z, size_z), 1
     )
     diag = [gap == d - 1 for d in range(3)]
 
+    def bands(g_ref, y, x, ab):
+        a, b = AB[ab]
+        row = first_row + y
+        g = 0.5 * (thick_ref[x + 1, row + 1, 1:2] + thick_ref[x + a, row + b])
+        for kind in range(2):
+            coeff = tap_ref[kind, ab] * g
+            high = coeff.astype(jnp.bfloat16).astype(jnp.float32)
+            for half, part in enumerate((high, coeff - high)):
+                band = jnp.zeros((size_z, size_z), jnp.float32)
+                for d in range(3):
+                    band = jnp.where(diag[d], part[d : d + 1], band)
+                g_ref[
+                    (2 * ab + half) * size_z : (2 * ab + half + 1) * size_z,
+                    kind * size_z : (kind + 1) * size_z,
+                ] = band.astype(jnp.bfloat16)
+
+    def modes_of(block, c):
+        return jnp.concatenate(
+            [block[(k * comps + c) * local : (k * comps + c + 1) * local] for k in range(parts)], axis=0
+        )
+
+    for ab in range(9):
+        bands(g0, 0, 0, ab)
+    arrived(0)
+    arrived(1)
+
     def row(y, _):
+        arrived(y + 2)
         for x in range(planes):
-            u = u_ref[y, x]
-            high = u.astype(jnp.bfloat16).astype(jnp.float32)
-            low = u - high
-            for ab in range(9):
-                for half, part in enumerate((high, low)):
-                    for kind in range(2):
-                        base = 27 * kind + 3 * ab
-                        band = jnp.zeros((size_z, size_z), jnp.float32)
-                        for d in range(3):
-                            band = jnp.where(diag[d], part[base + d : base + d + 1], band)
-                        g_ref[
-                            (2 * ab + half) * size_z : (2 * ab + half + 1) * size_z,
-                            kind * size_z : (kind + 1) * size_z,
-                        ] = band.astype(jnp.bfloat16)
-            around = []
-            for a, b in AB:
+            now, then = (g0, g1) if x % 2 == 0 else (g1, g0)
+            images = None
+            for ab, (a, b) in enumerate(AB):
                 near = win[x + a, y + b]
-                around += [near, near]
-            images = jnp.dot(
-                jnp.concatenate(around, axis=1), g_ref[...], preferred_element_type=jnp.float32
-            )
+                image = jnp.dot(
+                    jnp.concatenate([near, near], axis=1),
+                    now[2 * ab * size_z : 2 * (ab + 1) * size_z],
+                    preferred_element_type=jnp.float32,
+                )
+                images = image if images is None else images + image
+                if x + 1 < planes:
+                    bands(then, y, x + 1, ab)
+                else:
+                    bands(then, jnp.minimum(y + 1, done - 1), 0, ab)
             for c in range(comps):
-                image = images[c * own : (c + 1) * own]
+                image = modes_of(images, c)
                 l_ref[:, (x * comps + c) * size_z : (x * comps + c + 1) * size_z] = (
                     image[:, :size_z] - lam_ref[...] * image[:, size_z:]
                 ).astype(jnp.bfloat16)
+        pltpu.make_async_copy(e_ref.at[:, 0], other.at[:, y], sems.at[y + 1, 3]).wait()
         cells = [(x, c) for x in range(planes) for c in range(comps)]
-        mine = jnp.concatenate([win[x + 1, y + 1, c * own : (c + 1) * own] for x, c in cells], axis=1)
-        theirs = jnp.concatenate([other[x, y, c * own : (c + 1) * own] for x, c in cells], axis=1)
+        mine = jnp.concatenate([modes_of(win[x + 1, y + 1], c) for x, c in cells], axis=1)
+        theirs = jnp.concatenate([modes_of(other[x, y], c) for x, c in cells], axis=1)
         out_ref[...] += lax.dot_general(
             jnp.concatenate([mine, theirs], axis=0),
             l_ref[...],
@@ -159,37 +186,71 @@
     lax.fori_loop(0, done, row, 0)
 
 
-def load(u, lam, sums, now, before, own):
+def load(first_row, thick, taps, lam, sums, now, before, own, parts):
     rows = now[0].shape[1]
     planes, _, width, size_z = now[0].shape
     prev_rows = before[0].shape[1] if before else 0
     done = rows if before else rows - 2
     vmem = pl.BlockSpec(memory_space=pltpu.VMEM)
     hbm = pl.BlockSpec(memory_space=pl.ANY)
-    args = [u, lam] + ([sums] if before else []) + list(now) + (list(before) if before else [])
-    specs = [vmem] * (3 if before else 2) + [hbm] * (8 if before else 4)
+    args = [thick, taps, lam] + ([sums] if before else []) + list(now) + (list(before) if before else [])
+    specs = [vmem] * (4 if before else 3) + [hbm] * (8 if before else 4)
     out = jax.ShapeDtypeStruct((2 * own, own), jnp.float32)
-    taps = 2 * 9 * size_z
+    depth = 2 * 9 * size_z
     return pl.pallas_call(
-        functools.partial(load_kernel, prev_rows, rows, own),
+        functools.partial(load_kernel, first_row, prev_rows, rows, own, parts),
         in_specs=specs,
         out_specs=vmem,
         out_shape=out,
         scratch_shapes=[
             pltpu.VMEM((planes + 2, done + 2, width, size_z), jnp.bfloat16),
             pltpu.VMEM((planes, done, width, size_z), jnp.bfloat16),
-            pltpu.VMEM((taps, 2 * size_z), jnp.bfloat16),
+            pltpu.VMEM((depth, 2 * size_z), jnp.bfloat16),
+            pltpu.VMEM((depth, 2 * size_z), jnp.bfloat16),
             pltpu.VMEM((own, planes * width // own * size_z), jnp.bfloat16),
-            pltpu.SemaphoreType.DMA((8,)),
+            pltpu.SemaphoreType.DMA((done + 2, 4)),
         ],
         compiler_params=pltpu.CompilerParams(vmem_limit_bytes=VMEM_BYTES),
         name="load",
         cost_estimate=pl.CostEstimate(
-            flops=2 * done * planes * width * taps * 2 * size_z,
+            flops=2 * done * planes * width * depth * 2 * size_z,
             bytes_accessed=4 * done * planes * width * size_z,
             transcendentals=0,
         ),
     )(*args)
+
+
+def join_kernel(parts, *refs):
+    blocks, (field, lowest, highest, sems) = refs[:parts], refs[parts:]
+    planes = field.shape[0]
+    size = field.shape[2] // parts
+    copies = []
+    for k, block in enumerate(blocks):
+        at = slice(k * size, (k + 1) * size)
+        copies += [
+            pltpu.make_async_copy(block.at[0], lowest.at[:, at], sems.at[k, 0]),
+            pltpu.make_async_copy(block.at[planes - 1], highest.at[:, at], sems.at[k, 1]),
+            pltpu.make_async_copy(block, field.at[:, :, at], sems.at[k, 2]),
+        ]
+    for copy in copies:
+        copy.start()
+    for copy in copies:
+        copy.wait()
+
+
+def join(blocks):
+    planes, rows, size, size_z = blocks[0].shape
+    parts = len(blocks)
+    hbm = pl.BlockSpec(memory_space=pl.ANY)
+    plane = jax.ShapeDtypeStruct((rows, size * parts, size_z), blocks[0].dtype)
+    return pl.pallas_call(
+        functools.partial(join_kernel, parts),
+        in_specs=[hbm] * parts,
+        out_specs=[hbm] * 3,
+        out_shape=[jax.ShapeDtypeStruct((planes,) + plane.shape, plane.dtype), plane, plane],
+        scratch_shapes=[pltpu.SemaphoreType.DMA((parts, 3))],
+        name="join",
+    )(*blocks)
 
 
 def arrange_kernel(parts, local, pos_ref, s_ref, *outs):
@@ -254,19 +315,9 @@
     thick = jnp.concatenate([from_below(thickness[-1:]), thickness, from_above(thickness[:1])], axis=0)
     thick = jnp.pad(thick, ((0, 0), (1, 1), (1, 1)))
     thick = lax.dynamic_slice_in_dim(thick, me * height, height + 2, axis=1)
-    centre = thick[1 : 1 + planes, 1 : 1 + height, 1 : 1 + size_z]
-    coeffs = jnp.stack(
-        [
-            0.5 * (centre + thick[a : a + planes, b : b + height, d : d + size_z])
-            for a in range(3)
-            for b in range(3)
-            for d in range(3)
-        ],
-        axis=2,
-    )
-    coeffs = jnp.concatenate(
-        [coeffs * stiff_taps[:, None], coeffs * mass_taps[:, None]], axis=2
-    ).transpose(1, 0, 2, 3)
+    thick = jnp.stack([thick[:, :, d : d + size_z] for d in range(3)], axis=2)
+    taps = jnp.stack([stiff_taps, mass_taps]).reshape(2, 9, 3, 1)
+    taps = jnp.broadcast_to(taps, (2, 9, 3, size_z))
 
     lams = jnp.concatenate(
         [eigenvalues] + [other_part(eigenvalues, k) for k in range(1, parts)], axis=0
@@ -274,14 +325,38 @@
     lams = jnp.broadcast_to(lams[:, None], (own, size_z))
 
     sums, before, at = None, None, 0
-    for (lo, hi), blocks in zip(bounds, packed):
-        got = [blocks[0]] + [other_part(blocks[k], k) for k in range(1, parts)]
-        field = jnp.concatenate(got, axis=3).reshape(planes, hi - lo, comps * own, size_z)
-        now = (field, from_below(field[-1]), from_above(field[0]), other_half(field))
-        done = hi - lo - (0 if before else 2)
-        sums = load(coeffs[at : at + done], lams, sums, now, before, own)
+    count = len(bounds)
+    received, joined = {}, {}
+
+    def receive(r):
+        received[r] = [packed[r][0]] + [other_part(packed[r][k], k) for k in range(1, parts)]
+
+    def gather(r):
+        planes_, rows_ = received[r][0].shape[:2]
+        blocks = [v.reshape(planes_, rows_, comps * local, size_z) for v in received[r]]
+        field, lowest, highest = join(blocks)
+        joined[r] = (field, from_below(highest), from_above(lowest), other_half(field))
+
+    for r in range(min(2, count)):
+        receive(r)
+    gather(0)
+    sums = None
+    for r in range(count):
+        if r + 2 < count:
+            fenced, packed[r + 2] = lax.optimization_barrier((joined[r][0], packed[r + 2]))
+            joined[r] = (fenced,) + joined[r][1:]
+            receive(r + 2)
+        if r + 1 < count:
+            if r > 0:
+                received[r + 1], sums = lax.optimization_barrier((received[r + 1], sums))
+            gather(r + 1)
+            fenced, nearby = lax.optimization_barrier((joined[r + 1][0], joined[r][1]))
+            joined[r + 1] = (fenced,) + joined[r + 1][1:]
+            joined[r] = (joined[r][0], nearby) + joined[r][2:]
+        before = joined[r - 1] if r else None
+        done = bounds[r][1] - bounds[r][0] - (0 if r else 2)
+        sums = load(at, thick, taps, lams, sums, joined[r], before, own, parts)
         at += done
-        before = now
 
     pos = jnp.stack([me, mine]).astype(jnp.int32)
     strips = arrange(pos, sums, parts, local, sectors)

time: 281 us -> 624 us (2.22)
  Pallas kernels: 96.1 us -> 492 us
  waiting for transfers between devices: 79.6 us -> 53.9 us
  local copies, waits for them, and re-layouts: 25.7 us -> 9.14 us
    pallas_call x5 -> x10, Pallas kernels: 81.4 us -> 478 us  [the longest x5 399 us: join(): pl.pallas_call(functools.partial(join_kernel, parts), in_specs=[hbm] * pa...]
    ppermute x21, waiting for transfers between devices: 70.1 us -> 28.2 us  [other_part(): return lax.ppermute(value, 'mode', [(i, i ^ 2 * k) for i in range(groups)])]
    ppermute x6, waiting for transfers between devices: 0.02 us -> 13.3 us  [from_below(): lax.ppermute(value, 'sector', [(i, i + 1) for i in range(sectors - 1)])]
  transfers between devices with their start and end apart: 41 -> 41, of which waited for: 13 -> 17; matrix products, arithmetic and copies ran while one was open for 11% -> 1% of each run, Pallas kernels for 30% -> 76%
where the time goes in v2:
time: 624 us; the launch traced here: 623 us
  Pallas kernels  492 us (79%)
  starting transfers between devices  64.5 us (10%)
  waiting for transfers between devices  53.9 us (9%)
  local copies, waits for them, and re-layouts  9.14 us (1%)
    pallas_call x5, Pallas kernels, join(): pl.pallas_call(functools.partial(join_kernel, parts), in_specs=[hbm] * pa...  399 us
    pallas_call x5, Pallas kernels, load(): pl.pallas_call(functools.partial(load_kernel, first_row, prev_rows, rows,...  78.7 us
    ppermute x21, waiting for transfers between devices, other_part(): return lax.ppermute(value, 'mode', [(i, i ^ 2 * k) for i in range(groups)])  28.2 us
    ppermute x21, starting transfers between devices, other_part(): return lax.ppermute(value, 'mode', [(i, i ^ 2 * k) for i in range(groups)])  25.7 us
    ppermute x6, starting transfers between devices, from_below(): lax.ppermute(value, 'sector', [(i, i + 1) for i in range(sectors - 1)])  25.4 us
    ppermute x6, waiting for transfers between devices, from_below(): lax.ppermute(value, 'sector', [(i, i + 1) for i in range(sectors - 1)])  13.3 us
    pallas_call x2, Pallas kernels, pack(): pl.pallas_call(functools.partial(pack_kernel, height, parts, chunks), gri...  12.9 us
  transfers between devices with their start and end apart: 41, of which 17 were waited for; matrix products, arithmetic and copies ran while one was open for 1% of the time, Pallas kernels for 76%

profile of v2, /device:TPU:0, one launch (start us, length us, event | category | flops | bytes accessed | tf_op | source)
XLA Modules:
  0.0 623.4 jit_solution(6738125566498699832)
XLA Ops:
  0.0 5.3 pack.2
  5.3 2.9 collective-permute-start.5
  8.2 1.5 collective-permute-start.6
  9.8 7.6 %pack.3 = (bf16[4,6,3,32,128]{4,3,2,1,0:T(8,128)(2,1)}, bf16[4,6,3,32,128]{4,3,2,1,0:T(8,128)(2,1)}, bf16[4,6,3,32,128]{4,3,2,1,0:T(8,128)(2,1)}, bf16[4,6,3,32,...) custom-call(s32[1]{0:T(128)} %bitcast.me_ref, ...), custom_call_target="tpu_custom_call" | custom-call | bytes 15728640 | tf_op jit(solution)/shard_map/pack/pallas_call | solution.py:61
  17.4 2.0 collective-permute-start.11
  19.5 1.5 collective-permute-start.12
  21.4 6.5 %collective-permute-done.6 = bf16[4,4,3,32,128]{4,3,2,1,0:T(8,128)(2,1)S(1)} collective-permute-done((bf16[4,4,3,32,128]{4,3,2,1,0:T(8,128)(2,1)}, bf16[4,4,3,32,128]{4,3,2,1,0:T(8,128)(2,1)S(1)}, u32[]{:S(2)}, u32[]{:S(2)}) %collective-permute-start.6) | collective-permute-done | bytes 393248 | tf_op jit(solution)/shard_map/ppermute | solution.py:296
  29.1 72.7 %join.5 = (bf16[4,4,384,128]{3,2,1,0:T(8,128)(2,1)}, bf16[4,384,128]{2,1,0:T(8,128)(2,1)}, bf16[4,384,128]{2,1,0:T(8,128)(2,1)}) custom-call(bf16[4,4,96,128]{3,2,1,0:T(8,128)(2,1)} %bitcast.37, bf16[4,4,96,128]{3,2,1,0:T(8,128)(2,1)} %bitcast.38, bf16[4,4,96,128]{3,2,1,0:T(8,128)(2,1)} %bitcast.39, bf16[4,4,96,128]{3,2,1,0:T(8,128)(2,1)} %bitcast.41), custom_call_target="tpu_custom_call" | custom-call | tf_op jit(solution)/shard_map/join/pallas_call | solution.py:246
  103.2 108.4 %join.6 = (bf16[4,6,384,128]{3,2,1,0:T(8,128)(2,1)}, bf16[6,384,128]{2,1,0:T(8,128)(2,1)}, bf16[6,384,128]{2,1,0:T(8,128)(2,1)}) custom-call(bf16[4,6,96,128]{3,2,1,0:T(8,128)(2,1)} %bitcast.29, bf16[4,6,96,128]{3,2,1,0:T(8,128)(2,1)} %bitcast.31, bf16[4,6,96,128]{3,2,1,0:T(8,128)(2,1)} %bitcast.33, bf16[4,6,96,128]{3,2,1,0:T(8,128)(2,1)} %bitcast.35), custom_call_target="tpu_custom_call" | custom-call | tf_op jit(solution)/shard_map/join/pallas_call | solution.py:246
  212.1 1.4 collective-permute-start.4
  213.6 4.2 collective-permute-start.14
  219.2 1.6 collective-permute-start.3
  221.0 1.8 collective-permute-done.3
  222.8 1.9 collective-permute-start.2
  224.9 1.5 collective-permute-done.2
  226.4 4.5 collective-permute-start
  231.0 1.5 collective-permute-done
  233.9 4.8 collective-permute-done.1
  238.9 1.9 collective-permute-start.8
  241.1 1.4 collective-permute-start.10
  245.1 9.5 %load.5.refs_3_ = f32[256,128]{1,0:T(8,128)} custom-call(f32[6,22,3,128]{3,2,1,0:T(4,128)} %pad_maximum_fusion.refs_0_, f32[2,9,3,128]{3,2,1,0:T(4,128)} %broadcast_in_dim.14.refs_1_, f32[128,128]{1,0:T(8,128)} %broadcast_in_dim.15.refs_2_, bf16[4,4,384,128]{3,2,1,0:T(8,128)(2,1)} %get-tuple-element.95.refs_3_.refs_8_, ...), custom_call_target="tpu_custom_call" | custom-call | flops 3623878656 | bytes 1572864 | tf_op jit(solution)/shard_map/load/pallas_call | solution.py:200
  255.5 8.8 %collective-permute-done.9 = bf16[4,6,3,32,128]{4,3,2,1,0:T(8,128)(2,1)S(1)} collective-permute-done((bf16[4,6,3,32,128]{4,3,2,1,0:T(8,128)(2,1)S(1)}, bf16[4,6,3,32,128]{4,3,2,1,0:T(8,128)(2,1)S(1)}, u32[]{:S(2)}, u32[]{:S(2)}) %collective-permute-start.9) | collective-permute-done | bytes 589856 | tf_op jit(solution)/shard_map/ppermute | solution.py:296
  265.2 108.4 %join.7 = (bf16[4,6,384,128]{3,2,1,0:T(8,128)(2,1)}, bf16[6,384,128]{2,1,0:T(8,128)(2,1)}, bf16[6,384,128]{2,1,0:T(8,128)(2,1)}) custom-call(bf16[4,6,96,128]{3,2,1,0:T(8,128)(2,1)} %bitcast.28, bf16[4,6,96,128]{3,2,1,0:T(8,128)(2,1)} %bitcast.30, bf16[4,6,96,128]{3,2,1,0:T(8,128)(2,1)} %bitcast.32, bf16[4,6,96,128]{3,2,1,0:T(8,128)(2,1)} %bitcast.34), custom_call_target="tpu_custom_call" | custom-call | tf_op jit(solution)/shard_map/join/pallas_call | solution.py:246
  373.7 3.7 collective-permute-start.17
  377.4 1.3 collective-permute-start.24
  379.2 11.8 %collective-permute-done.17.refs_5_.refs_9_ = bf16[6,384,128]{2,1,0:T(8,128)(2,1)S(1)} collective-permute-done((bf16[6,384,128]{2,1,0:T(8,128)(2,1)}, bf16[6,384,128]{2,1,0:T(8,128)(2,1)S(1)}, u32[]{:S(2)}, u32[]{:S(2)}) %collective-permute-start.17) | collective-permute-done | bytes 589856 | tf_op jit(solution)/shard_map/ppermute | solution.py:302
  391.0 1.7 collective-permute-start.23
  392.8 2.2 collective-permute-done.24.refs_6_.refs_10_
  395.0 3.9 collective-permute-start.26
  398.9 1.4 collective-permute-start.27
  400.3 21.9 %load.6.refs_3_ = f32[256,128]{1,0:T(8,128)} custom-call(f32[6,22,3,128]{3,2,1,0:T(4,128)} %pad_maximum_fusion.refs_0_, f32[2,9,3,128]{3,2,1,0:T(4,128)} %broadcast_in_dim.14.refs_1_, f32[128,128]{1,0:T(8,128)} %broadcast_in_dim.15.refs_2_, f32[256,128]{1,0:T(8,128)} %load.5.refs_3_, bf16[4,6,384,128]{3,2,1,0:T(8,128)(2,1)} %get-tuple-element.129.refs_4_.refs_8_, ...), custom_call_target="tpu_custom_call" | custom-call | flops 10871635968 | bytes 4718592 | tf_op jit(solution)/shard_map/load/pallas_call | solution.py:200
  423.1 72.7 %join.8 = (bf16[4,4,384,128]{3,2,1,0:T(8,128)(2,1)}, bf16[4,384,128]{2,1,0:T(8,128)(2,1)}, bf16[4,384,128]{2,1,0:T(8,128)(2,1)}) custom-call(bf16[4,4,96,128]{3,2,1,0:T(8,128)(2,1)} %bitcast.36, bf16[4,4,96,128]{3,2,1,0:T(8,128)(2,1)} %bitcast.40, bf16[4,4,96,128]{3,2,1,0:T(8,128)(2,1)} %bitcast.42, bf16[4,4,96,128]{3,2,1,0:T(8,128)(2,1)} %bitcast.43), custom_call_target="tpu_custom_call" | custom-call | tf_op jit(solution)/shard_map/join/pallas_call | solution.py:246
  497.7 5.5 collective-permute-done.18
  504.4 4.5 collective-permute-start.29
  509.0 1.5 collective-permute-start.30
  510.5 22.1 %load.7.refs_3_ = f32[256,128]{1,0:T(8,128)} custom-call(f32[6,22,3,128]{3,2,1,0:T(4,128)} %pad_maximum_fusion.refs_0_, f32[2,9,3,128]{3,2,1,0:T(4,128)} %broadcast_in_dim.14.refs_1_, f32[128,128]{1,0:T(8,128)} %broadcast_in_dim.15.refs_2_, f32[256,128]{1,0:T(8,128)} %load.6.refs_3_, bf16[4,6,384,128]{3,2,1,0:T(8,128)(2,1)} %get-tuple-element.133.refs_4_.refs_8_, ...), custom_call_target="tpu_custom_call" | custom-call | flops 10871635968 | bytes 4718592 | tf_op jit(solution)/shard_map/load/pallas_call | solution.py:200
  533.4 36.9 %join.9 = (bf16[4,2,384,128]{3,2,1,0:T(8,128)(2,1)}, bf16[2,384,128]{2,1,0:T(8,128)(2,1)}, bf16[2,384,128]{2,1,0:T(8,128)(2,1)}) custom-call(bf16[4,2,96,128]{3,2,1,0:T(8,128)(2,1)} %bitcast.44, bf16[4,2,96,128]{3,2,1,0:T(8,128)(2,1)} %bitcast.45, bf16[4,2,96,128]{3,2,1,0:T(8,128)(2,1)} %bitcast.46, bf16[4,2,96,128]{3,2,1,0:T(8,128)(2,1)} %bitcast.47), custom_call_target="tpu_custom_call" | custom-call | tf_op jit(solution)/shard_map/join/pallas_call | solution.py:246
  571.1 4.6 collective-permute-start.32
  575.6 1.3 collective-permute-start.33
  576.9 15.8 %load.8.refs_3_ = f32[256,128]{1,0:T(8,128)} custom-call(f32[6,22,3,128]{3,2,1,0:T(4,128)} %pad_maximum_fusion.refs_0_, f32[2,9,3,128]{3,2,1,0:T(4,128)} %broadcast_in_dim.14.refs_1_, f32[128,128]{1,0:T(8,128)} %broadcast_in_dim.15.refs_2_, f32[256,128]{1,0:T(8,128)} %load.7.refs_3_, bf16[4,4,384,128]{3,2,1,0:T(8,128)(2,1)} %get-tuple-element.143.refs_4_.refs_8_, ...), custom_call_target="tpu_custom_call" | custom-call | flops 7247757312 | bytes 3145728 | tf_op jit(solution)/shard_map/load/pallas_call | solution.py:200
  594.5 9.5 %load.9.s_ref = f32[256,128]{1,0:T(8,128)} custom-call(f32[6,22,3,128]{3,2,1,0:T(4,128)} %pad_maximum_fusion.refs_0_, f32[2,9,3,128]{3,2,1,0:T(4,128)} %broadcast_in_dim.14.refs_1_, f32[128,128]{1,0:T(8,128)} %broadcast_in_dim.15.refs_2_, f32[256,128]{1,0:T(8,128)} %load.8.refs_3_, bf16[4,2,384,128]{3,2,1,0:T(8,128)(2,1)} %get-tuple-element.152.refs_4_, ...), custom_call_target="tpu_custom_call" | custom-call | flops 3623878656 | bytes 1572864 | tf_op jit(solution)/shard_map/load/pallas_call | solution.py:200
  604.0 1.7 arrange.1
  605.7 1.7 collective-permute-start.37
  607.8 1.3 collective-permute-start.35
  609.2 1.6 collective-permute-done.37
  612.7 3.6 collective-permute-start.40
  618.0 3.2 collective-permute-done.39
  621.2 1.4 collective-permute-done.38
  (130 shorter events, 23.9 us)
Async XLA Ops:
  5.3 15.7 %collective-permute-start.5 = (bf16[4,4,3,32,128]{4,3,2,1,0:T(8,128)(2,1)}, bf16[4,4,3,32,128]{4,3,2,1,0:T(8,128)(2,1)S(1)}, u32[]{:S(2)}, u32[]{:S(2)}) collective-permute-start(bf16[4,4,3,32,128]{4,3,2,1,0:T(8,128)(2,1)} %get-tuple-element.83), channel_id=1, source_target_pairs={{0,2},{1,3},{2,0},{3,1},{4,6},{5,7},{6,4},{7,5},{8,10},{9,11},{10,... | collective-permute-start | bytes 1179656 | tf_op jit(solution)/shard_map/ppermute | solution.py:296
  8.2 19.7 %collective-permute-start.6 = (bf16[4,4,3,32,128]{4,3,2,1,0:T(8,128)(2,1)}, bf16[4,4,3,32,128]{4,3,2,1,0:T(8,128)(2,1)S(1)}, u32[]{:S(2)}, u32[]{:S(2)}) collective-permute-start(bf16[4,4,3,32,128]{4,3,2,1,0:T(8,128)(2,1)} %get-tuple-element.84), channel_id=1, source_target_pairs={{0,4},{1,5},{2,6},{3,7},{4,0},{5,1},{6,2},{7,3},{8,12},{9,13},{10,... | collective-permute-start | bytes 1179656 | tf_op jit(solution)/shard_map/ppermute | solution.py:296
  9.7 18.6 %collective-permute-start.7 = (bf16[4,4,3,32,128]{4,3,2,1,0:T(8,128)(2,1)}, bf16[4,4,3,32,128]{4,3,2,1,0:T(8,128)(2,1)S(1)}, u32[]{:S(2)}, u32[]{:S(2)}) collective-permute-start(bf16[4,4,3,32,128]{4,3,2,1,0:T(8,128)(2,1)} %get-tuple-element.85), channel_id=1, source_target_pairs={{0,6},{1,7},{2,4},{3,5},{4,2},{5,3},{6,0},{7,1},{8,14},{9,15},{10,... | collective-permute-start | bytes 1179656 | tf_op jit(solution)/shard_map/ppermute | solution.py:296
  17.4 194.8 %copy-start.18 = (f32[32]{0:T(128)S(1)}, f32[32]{0:T(128)}, u32[]{:S(2)}) copy-start(f32[32]{0:T(128)} %param.9) | copy-start | bytes 388
  17.4 196.2 %copy-start.12 = (f32[4,80,128]{2,1,0:T(8,128)S(1)}, f32[4,80,128]{2,1,0:T(8,128)}, u32[]{:S(2)}) copy-start(f32[4,80,128]{2,1,0:T(8,128)} %param.6) | copy-start | bytes 491524
  17.4 203.4 %copy-start.16 = (f32[27]{0:T(128)S(1)}, f32[27]{0:T(128)}, u32[]{:S(2)}) copy-start(f32[27]{0:T(128)} %param.8) | copy-start | bytes 328
  17.4 207.3 %copy-start.17 = (f32[27]{0:T(128)S(1)}, f32[27]{0:T(128)}, u32[]{:S(2)}) copy-start(f32[27]{0:T(128)} %param.7) | copy-start | bytes 328
  17.4 84.5 %collective-permute-start.11 = (bf16[4,6,3,32,128]{4,3,2,1,0:T(8,128)(2,1)}, bf16[4,6,3,32,128]{4,3,2,1,0:T(8,128)(2,1)S(1)}, u32[]{:S(2)}, u32[]{:S(2)}) collective-permute-start(bf16[4,6,3,32,128]{4,3,2,1,0:T(8,128)(2,1)} %get-tuple-element.97), channel_id=1, source_target_pairs={{0,2},{1,3},{2,0},{3,1},{4,6},{5,7},{6,4},{7,5},{8,10},{9,11},{10,... | collective-permute-start | bytes 1769480 | tf_op jit(solution)/shard_map/ppermute | solution.py:296
  19.5 82.5 %collective-permute-start.12 = (bf16[4,6,3,32,128]{4,3,2,1,0:T(8,128)(2,1)}, bf16[4,6,3,32,128]{4,3,2,1,0:T(8,128)(2,1)S(1)}, u32[]{:S(2)}, u32[]{:S(2)}) collective-permute-start(bf16[4,6,3,32,128]{4,3,2,1,0:T(8,128)(2,1)} %get-tuple-element.98), channel_id=1, source_target_pairs={{0,4},{1,5},{2,6},{3,7},{4,0},{5,1},{6,2},{7,3},{8,12},{9,13},{10,... | collective-permute-start | bytes 1769480 | tf_op jit(solution)/shard_map/ppermute | solution.py:296
  21.0 81.0 %collective-permute-start.13 = (bf16[4,6,3,32,128]{4,3,2,1,0:T(8,128)(2,1)}, bf16[4,6,3,32,128]{4,3,2,1,0:T(8,128)(2,1)S(1)}, u32[]{:S(2)}, u32[]{:S(2)}) collective-permute-start(bf16[4,6,3,32,128]{4,3,2,1,0:T(8,128)(2,1)} %get-tuple-element.99), channel_id=1, source_target_pairs={{0,6},{1,7},{2,4},{3,5},{4,2},{5,3},{6,0},{7,1},{8,14},{9,15},{10,... | collective-permute-start | bytes 1769480 | tf_op jit(solution)/shard_map/ppermute | solution.py:296
  101.8 111.8 %copy-start.25 = (bf16[4,384,128]{2,1,0:T(8,128)(2,1)S(1)}, bf16[4,384,128]{2,1,0:T(8,128)(2,1)}, u32[]{:S(2)}) copy-start(bf16[4,384,128]{2,1,0:T(8,128)(2,1)} %get-tuple-element.101) | copy-start | bytes 1179652
  101.8 139.0 %copy-start.22 = (bf16[4,6,3,32,128]{4,3,2,1,0:T(8,128)(2,1)S(1)}, bf16[4,6,3,32,128]{4,3,2,1,0:T(8,128)(2,1)}, u32[]{:S(2)}) copy-start(bf16[4,6,3,32,128]{4,3,2,1,0:T(8,128)(2,1)} %get-tuple-element.93) | copy-start | bytes 1769476
  101.8 139.2 %copy-start.21 = (bf16[4,6,3,32,128]{4,3,2,1,0:T(8,128)(2,1)S(1)}, bf16[4,6,3,32,128]{4,3,2,1,0:T(8,128)(2,1)}, u32[]{:S(2)}) copy-start(bf16[4,6,3,32,128]{4,3,2,1,0:T(8,128)(2,1)} %get-tuple-element.94) | copy-start | bytes 1769476
  101.8 141.8 %collective-permute-start.16 = (bf16[4,4,384,128]{3,2,1,0:T(8,128)(2,1)}, bf16[4,4,384,128]{3,2,1,0:T(8,128)(2,1)}, u32[]{:S(2)}, u32[]{:S(2)}) collective-permute-start(bf16[4,4,384,128]{3,2,1,0:T(8,128)(2,1)} %get-tuple-element.95.refs_3_.refs_8_), channel_id=1, source_target_pairs={{0,1},{1,0},{2,3},{3,2},{4,5},{5,4},{6,7},{7,6},{8,9},{9,8},{10,11... | collective-permute-start | bytes 4718600 | tf_op jit(solution)/shard_map/ppermute | solution.py:299
  211.6 187.3 %collective-permute-start.25 = (bf16[4,6,384,128]{3,2,1,0:T(8,128)(2,1)}, bf16[4,6,384,128]{3,2,1,0:T(8,128)(2,1)}, u32[]{:S(2)}, u32[]{:S(2)}) collective-permute-start(bf16[4,6,384,128]{3,2,1,0:T(8,128)(2,1)} %get-tuple-element.129.refs_4_.refs_8_), channel_id=1, source_target_pairs={{0,1},{1,0},{2,3},{3,2},{4,5},{5,4},{6,7},{7,6},{8,9},{9,8},{10,11... | collective-permute-start | bytes 7077896 | tf_op jit(solution)/shard_map/ppermute | solution.py:299
  212.1 7.1 %collective-permute-start.4 = (f32[32]{0:T(128)S(1)}, f32[32]{0:T(128)S(1)}, u32[]{:S(2)}, u32[]{:S(2)}) collective-permute-start(f32[32]{0:T(128)S(1)} %copy-done.18), channel_id=1, source_target_pairs={{0,6},{1,7},{2,4},{3,5},{4,2},{5,3},{6,0},{7,1},{8,14},{9,15},{10,... | collective-permute-start | bytes 392 | tf_op jit(solution)/shard_map/ppermute | solution.py:296
  213.6 27.3 %collective-permute-start.14 = (bf16[4,384,128]{2,1,0:T(8,128)(2,1)S(1)}, bf16[4,384,128]{2,1,0:T(8,128)(2,1)}, u32[]{:S(2)}, u32[]{:S(2)}) collective-permute-start(bf16[4,384,128]{2,1,0:T(8,128)(2,1)S(1)} %copy-done.25), channel_id=1, source_target_pairs={{0,8},{8,16},{16,24},{1,9},{9,17},{17,25},{2,10},{10,18},{18,26},{... | collective-permute-start | bytes 1179656 | tf_op jit(solution)/shard_map/ppermute | solution.py:302
  217.8 23.2 %collective-permute-start.15 = (bf16[4,384,128]{2,1,0:T(8,128)(2,1)}, bf16[4,384,128]{2,1,0:T(8,128)(2,1)}, u32[]{:S(2)}, u32[]{:S(2)}) collective-permute-start(bf16[4,384,128]{2,1,0:T(8,128)(2,1)} %get-tuple-element.103), channel_id=1, source_target_pairs={{8,0},{16,8},{24,16},{9,1},{17,9},{25,17},{10,2},{18,10},{26,18},{... | collective-permute-start | bytes 1179656 | tf_op jit(solution)/shard_map/ppermute | solution.py:305
  219.2 3.6 collective-permute-start.3
  222.8 3.5 collective-permute-start.2
  226.4 6.2 collective-permute-start
  232.6 6.2 collective-permute-start.1
  238.9 16.5 %collective-permute-start.8 = (bf16[4,6,3,32,128]{4,3,2,1,0:T(8,128)(2,1)}, bf16[4,6,3,32,128]{4,3,2,1,0:T(8,128)(2,1)S(1)}, u32[]{:S(2)}, u32[]{:S(2)}) collective-permute-start(bf16[4,6,3,32,128]{4,3,2,1,0:T(8,128)(2,1)} %get-tuple-element.92), channel_id=1, source_target_pairs={{0,2},{1,3},{2,0},{3,1},{4,6},{5,7},{6,4},{7,5},{8,10},{9,11},{10,... | collective-permute-start | bytes 1769480 | tf_op jit(solution)/shard_map/ppermute | solution.py:296
  240.9 23.4 %collective-permute-start.9 = (bf16[4,6,3,32,128]{4,3,2,1,0:T(8,128)(2,1)S(1)}, bf16[4,6,3,32,128]{4,3,2,1,0:T(8,128)(2,1)S(1)}, u32[]{:S(2)}, u32[]{:S(2)}) collective-permute-start(bf16[4,6,3,32,128]{4,3,2,1,0:T(8,128)(2,1)S(1)} %copy-done.22), channel_id=1, source_target_pairs={{0,4},{1,5},{2,6},{3,7},{4,0},{5,1},{6,2},{7,3},{8,12},{9,13},{10,... | collective-permute-start | bytes 1769480 | tf_op jit(solution)/shard_map/ppermute | solution.py:296
  241.1 23.2 %collective-permute-start.10 = (bf16[4,6,3,32,128]{4,3,2,1,0:T(8,128)(2,1)S(1)}, bf16[4,6,3,32,128]{4,3,2,1,0:T(8,128)(2,1)S(1)}, u32[]{:S(2)}, u32[]{:S(2)}) collective-permute-start(bf16[4,6,3,32,128]{4,3,2,1,0:T(8,128)(2,1)S(1)} %copy-done.21), channel_id=1, source_target_pairs={{0,6},{1,7},{2,4},{3,5},{4,2},{5,3},{6,0},{7,1},{8,14},{9,15},{10,... | collective-permute-start | bytes 1769480 | tf_op jit(solution)/shard_map/ppermute | solution.py:296
  373.7 135.3 %collective-permute-start.28 = (bf16[4,6,384,128]{3,2,1,0:T(8,128)(2,1)}, bf16[4,6,384,128]{3,2,1,0:T(8,128)(2,1)S(1)}, u32[]{:S(2)}, u32[]{:S(2)}) collective-permute-start(bf16[4,6,384,128]{3,2,1,0:T(8,128)(2,1)} %get-tuple-element.133.refs_4_.refs_8_), channel_id=1, source_target_pairs={{0,1},{1,0},{2,3},{3,2},{4,5},{5,4},{6,7},{7,6},{8,9},{9,8},{10,11... | collective-permute-start | bytes 7077896 | tf_op jit(solution)/shard_map/ppermute | solution.py:299
  373.7 17.2 %collective-permute-start.17 = (bf16[6,384,128]{2,1,0:T(8,128)(2,1)}, bf16[6,384,128]{2,1,0:T(8,128)(2,1)S(1)}, u32[]{:S(2)}, u32[]{:S(2)}) collective-permute-start(bf16[6,384,128]{2,1,0:T(8,128)(2,1)} %get-tuple-element.109), channel_id=1, source_target_pairs={{0,8},{8,16},{16,24},{1,9},{9,17},{17,25},{2,10},{10,18},{18,26},{... | collective-permute-start | bytes 1769480 | tf_op jit(solution)/shard_map/ppermute | solution.py:302
  377.4 17.5 %collective-permute-start.24 = (bf16[6,384,128]{2,1,0:T(8,128)(2,1)}, bf16[6,384,128]{2,1,0:T(8,128)(2,1)S(1)}, u32[]{:S(2)}, u32[]{:S(2)}) collective-permute-start(bf16[6,384,128]{2,1,0:T(8,128)(2,1)} %get-tuple-element.131), channel_id=1, source_target_pairs={{8,0},{16,8},{24,16},{9,1},{17,9},{25,17},{10,2},{18,10},{26,18},{... | collective-permute-start | bytes 1769480 | tf_op jit(solution)/shard_map/ppermute | solution.py:305
  378.7 12.3 %collective-permute-start.21 = (bf16[4,4,3,32,128]{4,3,2,1,0:T(8,128)(2,1)}, bf16[4,4,3,32,128]{4,3,2,1,0:T(8,128)(2,1)S(1)}, u32[]{:S(2)}, u32[]{:S(2)}) collective-permute-start(bf16[4,4,3,32,128]{4,3,2,1,0:T(8,128)(2,1)} %get-tuple-element.125), channel_id=1, source_target_pairs={{0,2},{1,3},{2,0},{3,1},{4,6},{5,7},{6,4},{7,5},{8,10},{9,11},{10,... | collective-permute-start | bytes 1179656 | tf_op jit(solution)/shard_map/ppermute | solution.py:296
  390.9 31.2 %collective-permute-start.22 = (bf16[4,4,3,32,128]{4,3,2,1,0:T(8,128)(2,1)}, bf16[4,4,3,32,128]{4,3,2,1,0:T(8,128)(2,1)S(1)}, u32[]{:S(2)}, u32[]{:S(2)}) collective-permute-start(bf16[4,4,3,32,128]{4,3,2,1,0:T(8,128)(2,1)} %get-tuple-element.126), channel_id=1, source_target_pairs={{0,4},{1,5},{2,6},{3,7},{4,0},{5,1},{6,2},{7,3},{8,12},{9,13},{10,... | collective-permute-start | bytes 1179656 | tf_op jit(solution)/shard_map/ppermute | solution.py:296
  391.0 31.2 %collective-permute-start.23 = (bf16[4,4,3,32,128]{4,3,2,1,0:T(8,128)(2,1)}, bf16[4,4,3,32,128]{4,3,2,1,0:T(8,128)(2,1)S(1)}, u32[]{:S(2)}, u32[]{:S(2)}) collective-permute-start(bf16[4,4,3,32,128]{4,3,2,1,0:T(8,128)(2,1)} %get-tuple-element.127), channel_id=1, source_target_pairs={{0,6},{1,7},{2,4},{3,5},{4,2},{5,3},{6,0},{7,1},{8,14},{9,15},{10,... | collective-permute-start | bytes 1179656 | tf_op jit(solution)/shard_map/ppermute | solution.py:296
  395.0 101.7 %collective-permute-start.26 = (bf16[6,384,128]{2,1,0:T(8,128)(2,1)}, bf16[6,384,128]{2,1,0:T(8,128)(2,1)}, u32[]{:S(2)}, u32[]{:S(2)}) collective-permute-start(bf16[6,384,128]{2,1,0:T(8,128)(2,1)} %get-tuple-element.139), channel_id=1, source_target_pairs={{0,8},{8,16},{16,24},{1,9},{9,17},{17,25},{2,10},{10,18},{18,26},{... | collective-permute-start | bytes 1769480 | tf_op jit(solution)/shard_map/ppermute | solution.py:302
  398.9 105.6 %collective-permute-start.27 = (bf16[6,384,128]{2,1,0:T(8,128)(2,1)}, bf16[6,384,128]{2,1,0:T(8,128)(2,1)}, u32[]{:S(2)}, u32[]{:S(2)}) collective-permute-start(bf16[6,384,128]{2,1,0:T(8,128)(2,1)} %get-tuple-element.141), channel_id=1, source_target_pairs={{8,0},{16,8},{24,16},{9,1},{17,9},{25,17},{10,2},{18,10},{26,18},{... | collective-permute-start | bytes 1769480 | tf_op jit(solution)/shard_map/ppermute | solution.py:305
  495.8 81.1 %collective-permute-start.31 = (bf16[4,4,384,128]{3,2,1,0:T(8,128)(2,1)}, bf16[4,4,384,128]{3,2,1,0:T(8,128)(2,1)}, u32[]{:S(2)}, u32[]{:S(2)}) collective-permute-start(bf16[4,4,384,128]{3,2,1,0:T(8,128)(2,1)} %get-tuple-element.143.refs_4_.refs_8_), channel_id=1, source_target_pairs={{0,1},{1,0},{2,3},{3,2},{4,5},{5,4},{6,7},{7,6},{8,9},{9,8},{10,11... | collective-permute-start | bytes 4718600 | tf_op jit(solution)/shard_map/ppermute | solution.py:299
  495.9 7.3 %collective-permute-start.18 = (bf16[4,2,3,32,128]{4,3,2,1,0:T(8,128)(2,1)S(1)}, bf16[4,2,3,32,128]{4,3,2,1,0:T(8,128)(2,1)S(1)}, u32[]{:S(2)}, u32[]{:S(2)}) collective-permute-start(bf16[4,2,3,32,128]{4,3,2,1,0:T(8,128)(2,1)S(1)} %copy-done.28), channel_id=1, source_target_pairs={{0,2},{1,3},{2,0},{3,1},{4,6},{5,7},{6,4},{7,5},{8,10},{9,11},{10,... | collective-permute-start | bytes 589832 | tf_op jit(solution)/shard_map/ppermute | solution.py:296
  496.7 35.9 %collective-permute-start.19 = (bf16[4,2,3,32,128]{4,3,2,1,0:T(8,128)(2,1)}, bf16[4,2,3,32,128]{4,3,2,1,0:T(8,128)(2,1)S(1)}, u32[]{:S(2)}, u32[]{:S(2)}) collective-permute-start(bf16[4,2,3,32,128]{4,3,2,1,0:T(8,128)(2,1)} %get-tuple-element.117), channel_id=1, source_target_pairs={{0,4},{1,5},{2,6},{3,7},{4,0},{5,1},{6,2},{7,3},{8,12},{9,13},{10,... | collective-permute-start | bytes 589832 | tf_op jit(solution)/shard_map/ppermute | solution.py:296
  503.2 29.4 %collective-permute-start.20 = (bf16[4,2,3,32,128]{4,3,2,1,0:T(8,128)(2,1)S(1)}, bf16[4,2,3,32,128]{4,3,2,1,0:T(8,128)(2,1)S(1)}, u32[]{:S(2)}, u32[]{:S(2)}) collective-permute-start(bf16[4,2,3,32,128]{4,3,2,1,0:T(8,128)(2,1)S(1)} %copy-done.27), channel_id=1, source_target_pairs={{0,6},{1,7},{2,4},{3,5},{4,2},{5,3},{6,0},{7,1},{8,14},{9,15},{10,... | collective-permute-start | bytes 589832 | tf_op jit(solution)/shard_map/ppermute | solution.py:296
  504.4 66.6 %collective-permute-start.29 = (bf16[4,384,128]{2,1,0:T(8,128)(2,1)}, bf16[4,384,128]{2,1,0:T(8,128)(2,1)S(1)}, u32[]{:S(2)}, u32[]{:S(2)}) collective-permute-start(bf16[4,384,128]{2,1,0:T(8,128)(2,1)} %get-tuple-element.149), channel_id=1, source_target_pairs={{0,8},{8,16},{16,24},{1,9},{9,17},{17,25},{2,10},{10,18},{18,26},{... | collective-permute-start | bytes 1179656 | tf_op jit(solution)/shard_map/ppermute | solution.py:302
  509.0 67.9 %collective-permute-start.30 = (bf16[4,384,128]{2,1,0:T(8,128)(2,1)}, bf16[4,384,128]{2,1,0:T(8,128)(2,1)}, u32[]{:S(2)}, u32[]{:S(2)}) collective-permute-start(bf16[4,384,128]{2,1,0:T(8,128)(2,1)} %get-tuple-element.151), channel_id=1, source_target_pairs={{8,0},{16,8},{24,16},{9,1},{17,9},{25,17},{10,2},{18,10},{26,18},{... | collective-permute-start | bytes 1179656 | tf_op jit(solution)/shard_map/ppermute | solution.py:305
  570.3 22.5 %collective-permute-start.34 = (bf16[4,2,384,128]{3,2,1,0:T(8,128)(2,1)}, bf16[4,2,384,128]{3,2,1,0:T(8,128)(2,1)S(1)}, u32[]{:S(2)}, u32[]{:S(2)}) collective-permute-start(bf16[4,2,384,128]{3,2,1,0:T(8,128)(2,1)} %get-tuple-element.152.refs_4_), channel_id=1, source_target_pairs={{0,1},{1,0},{2,3},{3,2},{4,5},{5,4},{6,7},{7,6},{8,9},{9,8},{10,11... | collective-permute-start | bytes 2359304 | tf_op jit(solution)/shard_map/ppermute | solution.py:299
  571.1 21.7 %collective-permute-start.32 = (bf16[2,384,128]{2,1,0:T(8,128)(2,1)}, bf16[2,384,128]{2,1,0:T(8,128)(2,1)S(1)}, u32[]{:S(2)}, u32[]{:S(2)}) collective-permute-start(bf16[2,384,128]{2,1,0:T(8,128)(2,1)} %get-tuple-element.153), channel_id=1, source_target_pairs={{0,8},{8,16},{16,24},{1,9},{9,17},{17,25},{2,10},{10,18},{18,26},{... | collective-permute-start | bytes 589832 | tf_op jit(solution)/shard_map/ppermute | solution.py:302
  575.6 17.2 %collective-permute-start.33 = (bf16[2,384,128]{2,1,0:T(8,128)(2,1)}, bf16[2,384,128]{2,1,0:T(8,128)(2,1)S(1)}, u32[]{:S(2)}, u32[]{:S(2)}) collective-permute-start(bf16[2,384,128]{2,1,0:T(8,128)(2,1)} %get-tuple-element.154), channel_id=1, source_target_pairs={{8,0},{16,8},{24,16},{9,1},{17,9},{25,17},{10,2},{18,10},{26,18},{... | collective-permute-start | bytes 589832 | tf_op jit(solution)/shard_map/ppermute | solution.py:305
  605.7 5.1 collective-permute-start.37
  607.4 4.1 collective-permute-start.36
  607.8 4.1 collective-permute-start.35
  612.7 5.2 collective-permute-start.40
  616.4 4.8 collective-permute-start.39
  616.9 5.7 collective-permute-start.38
  (24 other events, 312.0 us)

commit v3 on v2

--- a/solution.py
+++ b/solution.py
@@ -12,7 +12,7 @@
 
 
 def chunk_rows(total):
-    sizes = [4, 6, 6, 4, 2]
+    sizes = [4, 6, 6, 6]
     if sum(sizes) == total:
         return sizes
     sizes = []
@@ -118,10 +118,14 @@
     else:
         out_ref[...] = jnp.zeros_like(out_ref)
 
+    rows_16 = lax.broadcasted_iota(jnp.int32, (16, size_z), 0)
+    lanes_16 = lax.broadcasted_iota(jnp.int32, (16, size_z), 1)
+    turn = lax.rem(rows_16 - lanes_16 + 16 * size_z + 1, 16)
+    diag = [turn == d for d in range(3)]
     gap = lax.broadcasted_iota(jnp.int32, (size_z, size_z), 0) - lax.broadcasted_iota(
         jnp.int32, (size_z, size_z), 1
     )
-    diag = [gap == d - 1 for d in range(3)]
+    near_diag = jnp.where(jnp.abs(gap) <= 1, 1.0, 0.0).astype(jnp.bfloat16)
 
     def bands(g_ref, y, x, ab):
         a, b = AB[ab]
@@ -131,13 +135,14 @@
             coeff = tap_ref[kind, ab] * g
             high = coeff.astype(jnp.bfloat16).astype(jnp.float32)
             for half, part in enumerate((high, coeff - high)):
-                band = jnp.zeros((size_z, size_z), jnp.float32)
+                strip = jnp.zeros((16, size_z), jnp.float32)
                 for d in range(3):
-                    band = jnp.where(diag[d], part[d : d + 1], band)
+                    strip = jnp.where(diag[d], part[d : d + 1], strip)
+                strip = strip.astype(jnp.bfloat16)
                 g_ref[
                     (2 * ab + half) * size_z : (2 * ab + half + 1) * size_z,
                     kind * size_z : (kind + 1) * size_z,
-                ] = band.astype(jnp.bfloat16)
+                ] = jnp.concatenate([strip] * (size_z // 16), axis=0) * near_diag
 
     def modes_of(block, c):
         return jnp.concatenate(
@@ -213,7 +218,7 @@
         compiler_params=pltpu.CompilerParams(vmem_limit_bytes=VMEM_BYTES),
         name="load",
         cost_estimate=pl.CostEstimate(
-            flops=2 * done * planes * width * depth * 2 * size_z,
+            flops=50000000000,
             bytes_accessed=4 * done * planes * width * size_z,
             transcendentals=0,
         ),
@@ -221,20 +226,33 @@
 
 
 def join_kernel(parts, *refs):
-    blocks, (field, lowest, highest, sems) = refs[:parts], refs[parts:]
+    blocks, (field, lowest, highest, held, in_sems, out_sems) = refs[:parts], refs[parts:]
     planes = field.shape[0]
     size = field.shape[2] // parts
-    copies = []
-    for k, block in enumerate(blocks):
-        at = slice(k * size, (k + 1) * size)
-        copies += [
-            pltpu.make_async_copy(block.at[0], lowest.at[:, at], sems.at[k, 0]),
-            pltpu.make_async_copy(block.at[planes - 1], highest.at[:, at], sems.at[k, 1]),
-            pltpu.make_async_copy(block, field.at[:, :, at], sems.at[k, 2]),
+    order = [0, planes - 1] + list(range(1, planes - 1))
+    arrivals = {
+        x: [
+            pltpu.make_async_copy(block.at[x], held.at[x, :, k * size : (k + 1) * size], in_sems.at[x, k])
+            for k, block in enumerate(blocks)
         ]
-    for copy in copies:
-        copy.start()
-    for copy in copies:
+        for x in order
+    }
+    for x in order:
+        for copy in arrivals[x]:
+            copy.start()
+    leaving = []
+    for x in order:
+        for copy in arrivals[x]:
+            copy.wait()
+        if x == 0:
+            leaving.append(pltpu.make_async_copy(held.at[x], lowest, out_sems.at[planes]))
+            leaving[-1].start()
+        if x == planes - 1:
+            leaving.append(pltpu.make_async_copy(held.at[x], highest, out_sems.at[planes + 1]))
+            leaving[-1].start()
+        leaving.append(pltpu.make_async_copy(held.at[x], field.at[x], out_sems.at[x]))
+        leaving[-1].start()
+    for copy in leaving:
         copy.wait()
 
 
@@ -243,13 +261,22 @@
     parts = len(blocks)
     hbm = pl.BlockSpec(memory_space=pl.ANY)
     plane = jax.ShapeDtypeStruct((rows, size * parts, size_z), blocks[0].dtype)
+    field = jax.ShapeDtypeStruct((planes,) + plane.shape, plane.dtype)
     return pl.pallas_call(
         functools.partial(join_kernel, parts),
         in_specs=[hbm] * parts,
         out_specs=[hbm] * 3,
-        out_shape=[jax.ShapeDtypeStruct((planes,) + plane.shape, plane.dtype), plane, plane],
-        scratch_shapes=[pltpu.SemaphoreType.DMA((parts, 3))],
+        out_shape=[field, plane, plane],
+        scratch_shapes=[
+            pltpu.VMEM(field.shape, field.dtype),
+            pltpu.SemaphoreType.DMA((planes, parts)),
+            pltpu.SemaphoreType.DMA((planes + 2,)),
+        ],
+        compiler_params=pltpu.CompilerParams(vmem_limit_bytes=VMEM_BYTES),
         name="join",
+        cost_estimate=pl.CostEstimate(
+            flops=50000000000, bytes_accessed=0, transcendentals=0
+        ),
     )(*blocks)
 
 
@@ -292,17 +319,21 @@
     index = lax.axis_index("mode")
     me, mine = index // 2, index % 2
 
-    def other_part(value, k):
-        return lax.ppermute(value, "mode", [(i, i ^ (2 * k)) for i in range(groups)])
-
-    def other_half(value):
-        return lax.ppermute(value, "mode", [(i, i ^ 1) for i in range(groups)])
-
-    def from_below(value):
-        return lax.ppermute(value, "sector", [(i, i + 1) for i in range(sectors - 1)])
-
-    def from_above(value):
-        return lax.ppermute(value, "sector", [(i + 1, i) for i in range(sectors - 1)])
+    def other_part(value, k, name="pre"):
+        with jax.named_scope(f"{name}_{k}"):
+            return lax.ppermute(value, "mode", [(i, i ^ (2 * k)) for i in range(groups)])
+
+    def other_half(value, name="core"):
+        with jax.named_scope(name):
+            return lax.ppermute(value, "mode", [(i, i ^ 1) for i in range(groups)])
+
+    def from_below(value, name="pre_lo"):
+        with jax.named_scope(name):
+            return lax.ppermute(value, "sector", [(i, i + 1) for i in range(sectors - 1)])
+
+    def from_above(value, name="pre_hi"):
+        with jax.named_scope(name):
+            return lax.ppermute(value, "sector", [(i + 1, i) for i in range(sectors - 1)])
 
     bounds, at = [], 0
     for size in chunk_rows(height + 2):
@@ -319,40 +350,60 @@
     taps = jnp.stack([stiff_taps, mass_taps]).reshape(2, 9, 3, 1)
     taps = jnp.broadcast_to(taps, (2, 9, 3, size_z))
 
+    with jax.named_scope("pre_eig"):
+        held_back, packed[0] = lax.optimization_barrier((eigenvalues, packed[0]))
+        lams = lax.all_to_all(
+            jnp.broadcast_to(held_back[None], (groups, local)), "mode", 0, 0, tiled=True
+        )
+    lams = lams.reshape(parts, 2, local)
+    lams = lax.dynamic_index_in_dim(lams, mine, 1, keepdims=False)
     lams = jnp.concatenate(
-        [eigenvalues] + [other_part(eigenvalues, k) for k in range(1, parts)], axis=0
+        [lax.dynamic_index_in_dim(lams, me ^ k, 0, keepdims=False) for k in range(parts)], axis=0
     )
     lams = jnp.broadcast_to(lams[:, None], (own, size_z))
 
-    sums, before, at = None, None, 0
     count = len(bounds)
     received, joined = {}, {}
 
     def receive(r):
-        received[r] = [packed[r][0]] + [other_part(packed[r][k], k) for k in range(1, parts)]
+        received[r] = [packed[r][0]] + [other_part(packed[r][k], k, f"xy{r}") for k in range(1, parts)]
 
     def gather(r):
         planes_, rows_ = received[r][0].shape[:2]
         blocks = [v.reshape(planes_, rows_, comps * local, size_z) for v in received[r]]
         field, lowest, highest = join(blocks)
-        joined[r] = (field, from_below(highest), from_above(lowest), other_half(field))
+        joined[r] = (
+            field,
+            from_below(highest, f"z{r}_lo"),
+            from_above(lowest, f"z{r}_hi"),
+            other_half(field, f"core{r}"),
+        )
 
     for r in range(min(2, count)):
         receive(r)
+    received[0], thick, taps, packed[1:] = lax.optimization_barrier(
+        (received[0], thick, taps, packed[1:])
+    )
+    sums, at = None, 0
+
+    def follow(r):
+        if r + 2 < count:
+            received[r], packed[r + 2] = lax.optimization_barrier((received[r], packed[r + 2]))
+            receive(r + 2)
+
+    follow(0)
     gather(0)
-    sums = None
     for r in range(count):
-        if r + 2 < count:
-            fenced, packed[r + 2] = lax.optimization_barrier((joined[r][0], packed[r + 2]))
-            joined[r] = (fenced,) + joined[r][1:]
-            receive(r + 2)
         if r + 1 < count:
-            if r > 0:
-                received[r + 1], sums = lax.optimization_barrier((received[r + 1], sums))
+            field, lowest, highest, theirs = joined[r]
+            received[r + 1], lowest, highest, sums = lax.optimization_barrier(
+                (received[r + 1], lowest, highest, sums)
+            )
+            follow(r + 1)
             gather(r + 1)
-            fenced, nearby = lax.optimization_barrier((joined[r + 1][0], joined[r][1]))
+            fenced, lowest = lax.optimization_barrier((joined[r + 1][0], lowest))
             joined[r + 1] = (fenced,) + joined[r + 1][1:]
-            joined[r] = (joined[r][0], nearby) + joined[r][2:]
+            joined[r] = (field, lowest, highest, theirs)
         before = joined[r - 1] if r else None
         done = bounds[r][1] - bounds[r][0] - (0 if r else 2)
         sums = load(at, thick, taps, lams, sums, joined[r], before, own, parts)
@@ -362,7 +413,7 @@
     strips = arrange(pos, sums, parts, local, sectors)
     total = strips[0]
     for k in range(1, parts):
-        total = total + other_part(strips[k], k)
+        total = total + other_part(strips[k], k, "fin")
     summed = total
     for step in range(1, sectors):
         summed = summed + lax.ppermute(

time: 624 us -> 189 us (0.30)
  Pallas kernels: 492 us -> 95.7 us
  waiting for transfers between devices: 53.9 us -> 23.4 us
  starting transfers between devices: 64.5 us -> 57.6 us
    pallas_call x5 -> x4, Pallas kernels: 399 us -> 12.4 us  [join(): pl.pallas_call(functools.partial(join_kernel, parts), in_specs=[hbm] * pa...]
    ppermute x21 -> x15, waiting for transfers between devices: 28.2 us -> 8.2 us  [other_part(): return lax.ppermute(value, 'mode', [(i, i ^ 2 * k) for i in range(groups)])]
    ppermute x6 -> x5, waiting for transfers between devices: 13.3 us -> 0.01 us  [from_below(): lax.ppermute(value, 'sector', [(i, i + 1) for i in range(sectors - 1)])]
    all_to_all x0 -> x1, waiting for transfers between devices: none -> 10.4 us  [on_device(): lax.all_to_all(jnp.broadcast_to(held_back[None], (groups, local)), 'mode'...]
    pallas_call x5 -> x4, Pallas kernels: 78.7 us -> 68.7 us  [load(): pl.pallas_call(functools.partial(load_kernel, first_row, prev_rows, rows,...]
    ppermute x6 -> x5, waiting for transfers between devices: 7.04 us -> 0.01 us  [from_above(): lax.ppermute(value, 'sector', [(i + 1, i) for i in range(sectors - 1)])]
    ppermute x21 -> x15, starting transfers between devices: 25.7 us -> 19.6 us  [other_part(): return lax.ppermute(value, 'mode', [(i, i ^ 2 * k) for i in range(groups)])]
    ppermute x6 -> x5, starting transfers between devices: 25.4 us -> 20.7 us  [from_below(): lax.ppermute(value, 'sector', [(i, i + 1) for i in range(sectors - 1)])]
  transfers between devices with their start and end apart: 41 -> 33, of which waited for: 17 -> 10; matrix products, arithmetic and copies ran while one was open for 1% -> 2% of each run, Pallas kernels for 76% -> 37%
where the time goes in v3:
time: 189 us; the launch traced here: 188 us
  Pallas kernels  95.7 us (51%)
  starting transfers between devices  57.6 us (30%)
  waiting for transfers between devices  23.4 us (12%)
  local copies, waits for them, and re-layouts  8.12 us (4%)
  other arithmetic  2.6 us (1%)
    pallas_call x4, Pallas kernels, load(): pl.pallas_call(functools.partial(load_kernel, first_row, prev_rows, rows,...  68.7 us
    ppermute x5, starting transfers between devices, from_below(): lax.ppermute(value, 'sector', [(i, i + 1) for i in range(sectors - 1)])  20.7 us
    ppermute x15, starting transfers between devices, other_part(): return lax.ppermute(value, 'mode', [(i, i ^ 2 * k) for i in range(groups)])  19.6 us
    pallas_call x2, Pallas kernels, pack(): pl.pallas_call(functools.partial(pack_kernel, height, parts, chunks), gri...  12.9 us
    pallas_call x4, Pallas kernels, join(): pl.pallas_call(functools.partial(join_kernel, parts), in_specs=[hbm] * pa...  12.4 us
    all_to_all x1, waiting for transfers between devices, on_device(): lax.all_to_all(jnp.broadcast_to(held_back[None], (groups, local)), 'mode'...  10.4 us
    ppermute x15, waiting for transfers between devices, other_part(): return lax.ppermute(value, 'mode', [(i, i ^ 2 * k) for i in range(groups)])  8.2 us
    ppermute x5, starting transfers between devices, from_above(): lax.ppermute(value, 'sector', [(i + 1, i) for i in range(sectors - 1)])  6.89 us
  transfers between devices with their start and end apart: 33, of which 10 were waited for; matrix products, arithmetic and copies ran while one was open for 2% of the time, Pallas kernels for 37%

profile of v3, /device:TPU:0, one launch (start us, length us, event | category | flops | bytes accessed | tf_op | source)
XLA Modules:
  0.0 187.9 jit_solution(3189875951780491752)
XLA Ops:
  0.0 5.3 %pack.2 = (bf16[4,4,3,32,128]{4,3,2,1,0:T(8,128)(2,1)}, bf16[4,4,3,32,128]{4,3,2,1,0:T(8,128)(2,1)}, bf16[4,4,3,32,128]{4,3,2,1,0:T(8,128)(2,1)}, bf16[4,4,3,32,128]{4,3,2,1,0:T(8,128)(2,1)}) custom-call(s32[1]{0:T(128)} %bitcast.me_ref, bf16[32,3,4,80,128]{4,3,2,1,0:T(8,128)(2,1)} %in_ref.3), custom_call_target="tpu_custom_call" | custom-call | bytes 15728640 | tf_op jit(solution)/shard_map/pack/pallas_call | solution.py:61
  5.3 3.0 %collective-permute-start = (bf16[4,4,3,32,128]{4,3,2,1,0:T(8,128)(2,1)}, bf16[4,4,3,32,128]{4,3,2,1,0:T(8,128)(2,1)S(1)}, u32[]{:S(2)}, u32[]{:S(2)}) collective-permute-start(bf16[4,4,3,32,128]{4,3,2,1,0:T(8,128)(2,1)} %get-tuple-element.103), channel_id=1, source_target_pairs={{0,2},{1,3},{2,0},{3,1},{4,6},{5,7},{6,4},{7,5},{8,10},{9,11},{10,... | collective-permute-start | bytes 1179656 | tf_op jit(solution)/shard_map/xy0_1/ppermute | solution.py:324
  8.3 1.5 collective-permute-start.1
  9.8 4.0 %collective-permute-start.3 = (f32[1,80,128]{2,1,0:T(8,128)S(1)}, f32[1,80,128]{2,1,0:T(8,128)S(1)}, u32[]{:S(2)}, u32[]{:S(2)}) collective-permute-start(f32[1,80,128]{2,1,0:T(8,128)S(1)} %get-tuple-element.192), channel_id=1, source_target_pairs={{0,8},{8,16},{16,24},{1,9},{9,17},{17,25},{2,10},{10,18},{18,26},{... | collective-permute-start | bytes 122888 | tf_op jit(solution)/shard_map/pre_lo/ppermute | solution.py:332
  13.8 1.3 collective-permute-start.4
  15.5 7.6 %pack.3 = (bf16[4,6,3,32,128]{4,3,2,1,0:T(8,128)(2,1)}, bf16[4,6,3,32,128]{4,3,2,1,0:T(8,128)(2,1)}, bf16[4,6,3,32,128]{4,3,2,1,0:T(8,128)(2,1)}, bf16[4,6,3,32,...) custom-call(s32[1]{0:T(128)} %bitcast.me_ref, ...), custom_call_target="tpu_custom_call" | custom-call | bytes 15728640 | tf_op jit(solution)/shard_map/pack/pallas_call | solution.py:61
  23.3 1.5 collective-permute-start.5
  24.8 1.5 collective-permute-start.6
  26.8 0.9 pad_maximum_fusion.refs_0_
  29.2 2.7 %join.4 = (bf16[4,4,384,128]{3,2,1,0:T(8,128)(2,1)}, bf16[4,384,128]{2,1,0:T(8,128)(2,1)}, bf16[4,384,128]{2,1,0:T(8,128)(2,1)}) custom-call(bf16[4,4,96,128]{3,2,1,0:T(8,128)(2,1)} %bitcast.40, bf16[4,4,96,128]{3,2,1,0:T(8,128)(2,1)} %bitcast.41, bf16[4,4,96,128]{3,2,1,0:T(8,128)(2,1)} %bitcast.42, bf16[4,4,96,128]{3,2,1,0:T(8,128)(2,1)} %bitcast.13.refs_3_), custom_call_target="tpu_custom_call" | custom-call | flops 49999998976 | tf_op jit(solution)/shard_map/join/pallas_call | solution.py:265
  32.0 4.3 %collective-permute-start.8 = (bf16[4,384,128]{2,1,0:T(8,128)(2,1)}, bf16[4,384,128]{2,1,0:T(8,128)(2,1)S(1)}, u32[]{:S(2)}, u32[]{:S(2)}) collective-permute-start(bf16[4,384,128]{2,1,0:T(8,128)(2,1)} %get-tuple-element.133), channel_id=1, source_target_pairs={{0,8},{8,16},{16,24},{1,9},{9,17},{17,25},{2,10},{10,18},{18,26},{... | collective-permute-start | bytes 1179656 | tf_op jit(solution)/shard_map/z0_lo/ppermute | solution.py:332
  36.2 1.3 collective-permute-start.9
  38.1 3.7 %all-to-all-start = ((f32[8,1,32]{2,1,0:T(1,128)}), f32[8,1,32]{2,1,0:T(1,128)S(1)}, u32[]{:S(2)}, u32[]{:S(2)}) async-start(f32[8,1,32]{2,1,0:T(1,128)} %broadcast_in_dim.10), calls=%async_computation | async-start | bytes 8192 | tf_op jit(solution)/shard_map/pre_eig/all_to_all | solution.py:355
  42.4 10.4 %all-to-all-done = f32[8,1,32]{2,1,0:T(1,128)S(1)} async-done(((f32[8,1,32]{2,1,0:T(1,128)}), f32[8,1,32]{2,1,0:T(1,128)S(1)}, u32[]{:S(2)}, u32[]{:S(2)}) %all-to-all-start) | async-done | bytes 1056 | tf_op jit(solution)/shard_map/pre_eig/all_to_all | solution.py:355
  52.9 1.3 collective-permute-start.13
  54.2 0.8 collective-permute-start.14
  55.1 1.4 collective-permute-start.15
  57.3 3.1 %join.5 = (bf16[4,6,384,128]{3,2,1,0:T(8,128)(2,1)}, bf16[6,384,128]{2,1,0:T(8,128)(2,1)}, bf16[6,384,128]{2,1,0:T(8,128)(2,1)}) custom-call(bf16[4,6,96,128]{3,2,1,0:T(8,128)(2,1)} %bitcast.36, bf16[4,6,96,128]{3,2,1,0:T(8,128)(2,1)} %bitcast.37, bf16[4,6,96,128]{3,2,1,0:T(8,128)(2,1)} %bitcast.38, bf16[4,6,96,128]{3,2,1,0:T(8,128)(2,1)} %bitcast.39), custom_call_target="tpu_custom_call" | custom-call | flops 49999998976 | tf_op jit(solution)/shard_map/join/pallas_call | solution.py:265
  60.4 4.4 %collective-permute-start.16 = (bf16[6,384,128]{2,1,0:T(8,128)(2,1)}, bf16[6,384,128]{2,1,0:T(8,128)(2,1)}, u32[]{:S(2)}, u32[]{:S(2)}) collective-permute-start(bf16[6,384,128]{2,1,0:T(8,128)(2,1)} %get-tuple-element.155), channel_id=1, source_target_pairs={{0,8},{8,16},{16,24},{1,9},{9,17},{17,25},{2,10},{10,18},{18,26},{... | collective-permute-start | bytes 1769480 | tf_op jit(solution)/shard_map/z1_lo/ppermute | solution.py:332
  64.8 1.3 collective-permute-start.17
  66.8 9.1 %load.4.refs_3_ = f32[256,128]{1,0:T(8,128)} custom-call(f32[6,22,3,128]{3,2,1,0:T(4,128)} %pad_maximum_fusion.refs_0_, f32[2,9,3,128]{3,2,1,0:T(4,128)} %broadcast_in_dim.9.refs_1_, f32[128,128]{1,0:T(8,128)} %broadcast_in_dim.22.refs_2_, bf16[4,4,384,128]{3,2,1,0:T(8,128)(2,1)} %get-tuple-element.157.refs_3_.refs_8_, bf16[4,384,128]{2,1,0:T(8,128)(2,1)} %copy-done.20, ...), custom_call_target="tpu_custom_call" | custom-call | flops 49999998976 | bytes 1572864 | tf_op jit(solution)/shard_map/load/pallas_call | solution.py:205
  76.2 3.5 %collective-permute-done.14 = bf16[4,6,3,32,128]{4,3,2,1,0:T(8,128)(2,1)} collective-permute-done((bf16[4,6,3,32,128]{4,3,2,1,0:T(8,128)(2,1)}, bf16[4,6,3,32,128]{4,3,2,1,0:T(8,128)(2,1)}, u32[]{:S(2)}, u32[]{:S(2)}) %collective-permute-start.14) | collective-permute-done | bytes 589856 | tf_op jit(solution)/shard_map/xy2_2/ppermute | solution.py:324
  79.7 2.5 %collective-permute-start.10 = (bf16[4,6,3,32,128]{4,3,2,1,0:T(8,128)(2,1)S(1)}, bf16[4,6,3,32,128]{4,3,2,1,0:T(8,128)(2,1)}, u32[]{:S(2)}, u32[]{:S(2)}) collective-permute-start(bf16[4,6,3,32,128]{4,3,2,1,0:T(8,128)(2,1)S(1)} %copy-done.12), channel_id=1, source_target_pairs={{0,2},{1,3},{2,0},{3,1},{4,6},{5,7},{6,4},{7,5},{8,10},{9,11},{10,... | collective-permute-start | bytes 1769480 | tf_op jit(solution)/shard_map/xy3_1/ppermute | solution.py:324
  82.2 0.9 collective-permute-done.15
  83.1 1.0 collective-permute-start.11
  84.1 1.1 collective-permute-start.12
  85.2 3.1 %join.6 = (bf16[4,6,384,128]{3,2,1,0:T(8,128)(2,1)}, bf16[6,384,128]{2,1,0:T(8,128)(2,1)}, bf16[6,384,128]{2,1,0:T(8,128)(2,1)}) custom-call(bf16[4,6,96,128]{3,2,1,0:T(8,128)(2,1)} %bitcast.35, bf16[4,6,96,128]{3,2,1,0:T(8,128)(2,1)} %bitcast.19.refs_1_, bf16[4,6,96,128]{3,2,1,0:T(8,128)(2,1)} %bitcast.20.refs_2_, bf16[4,6,96,128]{3,2,1,0:T(8,128)(2,1)} %bitcast.21.refs_3_), custom_call_target="tpu_custom_call" | custom-call | flops 49999998976 | tf_op jit(solution)/shard_map/join/pallas_call | solution.py:265
  88.3 3.5 %collective-permute-start.19 = (bf16[6,384,128]{2,1,0:T(8,128)(2,1)}, bf16[6,384,128]{2,1,0:T(8,128)(2,1)S(1)}, u32[]{:S(2)}, u32[]{:S(2)}) collective-permute-start(bf16[6,384,128]{2,1,0:T(8,128)(2,1)} %get-tuple-element.166), channel_id=1, source_target_pairs={{0,8},{8,16},{16,24},{1,9},{9,17},{17,25},{2,10},{10,18},{18,26},{... | collective-permute-start | bytes 1769480 | tf_op jit(solution)/shard_map/z2_lo/ppermute | solution.py:332
  91.8 1.6 collective-permute-start.20
  93.4 19.9 %load.5.refs_3_ = f32[256,128]{1,0:T(8,128)} custom-call(f32[6,22,3,128]{3,2,1,0:T(4,128)} %pad_maximum_fusion.refs_0_, f32[2,9,3,128]{3,2,1,0:T(4,128)} %broadcast_in_dim.9.refs_1_, f32[128,128]{1,0:T(8,128)} %broadcast_in_dim.22.refs_2_, f32[256,128]{1,0:T(8,128)} %load.4.refs_3_, bf16[4,6,384,128]{3,2,1,0:T(8,128)(2,1)} %get-tuple-element.169.refs_4_.refs_8_, ...), custom_call_target="tpu_custom_call" | custom-call | flops 49999998976 | bytes 4718592 | tf_op jit(solution)/shard_map/load/pallas_call | solution.py:205
  113.4 3.5 %join.7 = (bf16[4,6,384,128]{3,2,1,0:T(8,128)(2,1)}, bf16[6,384,128]{2,1,0:T(8,128)(2,1)}, bf16[6,384,128]{2,1,0:T(8,128)(2,1)}) custom-call(bf16[4,6,96,128]{3,2,1,0:T(8,128)(2,1)} %bitcast.34, bf16[4,6,96,128]{3,2,1,0:T(8,128)(2,1)} %bitcast.23.refs_1_, bf16[4,6,96,128]{3,2,1,0:T(8,128)(2,1)} %bitcast.24.refs_2_, bf16[4,6,96,128]{3,2,1,0:T(8,128)(2,1)} %bitcast.25.refs_3_), custom_call_target="tpu_custom_call" | custom-call | flops 49999998976 | tf_op jit(solution)/shard_map/join/pallas_call | solution.py:265
  117.5 4.6 %collective-permute-start.23 = (bf16[6,384,128]{2,1,0:T(8,128)(2,1)}, bf16[6,384,128]{2,1,0:T(8,128)(2,1)S(1)}, u32[]{:S(2)}, u32[]{:S(2)}) collective-permute-start(bf16[6,384,128]{2,1,0:T(8,128)(2,1)} %get-tuple-element.185), channel_id=1, source_target_pairs={{0,8},{8,16},{16,24},{1,9},{9,17},{17,25},{2,10},{10,18},{18,26},{... | collective-permute-start | bytes 1769480 | tf_op jit(solution)/shard_map/z3_lo/ppermute | solution.py:332
  122.1 1.5 collective-permute-start.24
  123.6 1.4 copy-done.7
  125.0 19.9 %load.6.refs_3_ = f32[256,128]{1,0:T(8,128)} custom-call(f32[6,22,3,128]{3,2,1,0:T(4,128)} %pad_maximum_fusion.refs_0_, f32[2,9,3,128]{3,2,1,0:T(4,128)} %broadcast_in_dim.9.refs_1_, f32[128,128]{1,0:T(8,128)} %broadcast_in_dim.22.refs_2_, f32[256,128]{1,0:T(8,128)} %load.5.refs_3_, bf16[4,6,384,128]{3,2,1,0:T(8,128)(2,1)} %get-tuple-element.175.refs_4_.refs_8_, ...), custom_call_target="tpu_custom_call" | custom-call | flops 49999998976 | bytes 4718592 | tf_op jit(solution)/shard_map/load/pallas_call | solution.py:205
  144.9 0.8 copy-done.18
  146.0 1.4 copy-done.8
  147.4 19.8 %load.7.s_ref = f32[256,128]{1,0:T(8,128)} custom-call(f32[6,22,3,128]{3,2,1,0:T(4,128)} %pad_maximum_fusion.refs_0_, f32[2,9,3,128]{3,2,1,0:T(4,128)} %broadcast_in_dim.9.refs_1_, f32[128,128]{1,0:T(8,128)} %broadcast_in_dim.22.refs_2_, f32[256,128]{1,0:T(8,128)} %load.6.refs_3_, bf16[4,6,384,128]{3,2,1,0:T(8,128)(2,1)} %get-tuple-element.184.refs_4_, ...), custom_call_target="tpu_custom_call" | custom-call | flops 49999998976 | bytes 4718592 | tf_op jit(solution)/shard_map/load/pallas_call | solution.py:205
  167.2 1.7 arrange.1
  168.9 1.9 collective-permute-start.28
  170.8 1.0 collective-permute-start.27
  172.4 1.5 collective-permute-done.28
  173.9 1.0 collective-permute-done.27
  174.9 1.0 collective-permute-done.26
  176.6 4.8 %collective-permute-start.31 = (f32[64,128]{1,0:T(8,128)S(1)}, f32[64,128]{1,0:T(8,128)S(1)}, u32[]{:S(2)}, u32[]{:S(2)}) collective-permute-start(f32[64,128]{1,0:T(8,128)S(1)} %add_add_fusion), channel_id=1, source_target_pairs={{0,24},{8,0},{16,8},{24,16},{1,25},{9,1},{17,9},{25,17},{2,26},{10... | collective-permute-start | bytes 98312 | tf_op jit(solution)/shard_map/ppermute | solution.py:419
  181.4 1.0 collective-permute-start.29
  183.0 3.2 %collective-permute-done.30 = f32[64,128]{1,0:T(8,128)S(1)} collective-permute-done((f32[64,128]{1,0:T(8,128)S(1)}, f32[64,128]{1,0:T(8,128)S(1)}, u32[]{:S(2)}, u32[]{:S(2)}) %collective-permute-start.30) | collective-permute-done | bytes 32800 | tf_op jit(solution)/shard_map/ppermute | solution.py:419
  186.2 0.9 collective-permute-done.29
  (98 shorter events, 9.3 us)
Async XLA Ops:
  0.0 9.8 %copy-start = (f32[4,80,128]{2,1,0:T(8,128)S(1)}, f32[4,80,128]{2,1,0:T(8,128)}, u32[]{:S(2)}) copy-start(f32[4,80,128]{2,1,0:T(8,128)} %param.6) | copy-start | bytes 491524
  0.0 15.1 %copy-start.1 = (f32[27]{0:T(128)S(1)}, f32[27]{0:T(128)}, u32[]{:S(2)}) copy-start(f32[27]{0:T(128)} %param.8) | copy-start | bytes 328
  0.0 15.3 %copy-start.2 = (f32[27]{0:T(128)S(1)}, f32[27]{0:T(128)}, u32[]{:S(2)}) copy-start(f32[27]{0:T(128)} %param.7) | copy-start | bytes 328
  5.3 22.4 %collective-permute-start = (bf16[4,4,3,32,128]{4,3,2,1,0:T(8,128)(2,1)}, bf16[4,4,3,32,128]{4,3,2,1,0:T(8,128)(2,1)S(1)}, u32[]{:S(2)}, u32[]{:S(2)}) collective-permute-start(bf16[4,4,3,32,128]{4,3,2,1,0:T(8,128)(2,1)} %get-tuple-element.103), channel_id=1, source_target_pairs={{0,2},{1,3},{2,0},{3,1},{4,6},{5,7},{6,4},{7,5},{8,10},{9,11},{10,... | collective-permute-start | bytes 1179656 | tf_op jit(solution)/shard_map/xy0_1/ppermute | solution.py:324
  8.3 19.9 %collective-permute-start.1 = (bf16[4,4,3,32,128]{4,3,2,1,0:T(8,128)(2,1)}, bf16[4,4,3,32,128]{4,3,2,1,0:T(8,128)(2,1)S(1)}, u32[]{:S(2)}, u32[]{:S(2)}) collective-permute-start(bf16[4,4,3,32,128]{4,3,2,1,0:T(8,128)(2,1)} %get-tuple-element.104), channel_id=1, source_target_pairs={{0,4},{1,5},{2,6},{3,7},{4,0},{5,1},{6,2},{7,3},{8,12},{9,13},{10,... | collective-permute-start | bytes 1179656 | tf_op jit(solution)/shard_map/xy0_2/ppermute | solution.py:324
  9.8 18.7 %collective-permute-start.2 = (bf16[4,4,3,32,128]{4,3,2,1,0:T(8,128)(2,1)}, bf16[4,4,3,32,128]{4,3,2,1,0:T(8,128)(2,1)}, u32[]{:S(2)}, u32[]{:S(2)}) collective-permute-start(bf16[4,4,3,32,128]{4,3,2,1,0:T(8,128)(2,1)} %get-tuple-element.105), channel_id=1, source_target_pairs={{0,6},{1,7},{2,4},{3,5},{4,2},{5,3},{6,0},{7,1},{8,14},{9,15},{10,... | collective-permute-start | bytes 1179656 | tf_op jit(solution)/shard_map/xy0_3/ppermute | solution.py:324
  9.8 13.5 %collective-permute-start.3 = (f32[1,80,128]{2,1,0:T(8,128)S(1)}, f32[1,80,128]{2,1,0:T(8,128)S(1)}, u32[]{:S(2)}, u32[]{:S(2)}) collective-permute-start(f32[1,80,128]{2,1,0:T(8,128)S(1)} %get-tuple-element.192), channel_id=1, source_target_pairs={{0,8},{8,16},{16,24},{1,9},{9,17},{17,25},{2,10},{10,18},{18,26},{... | collective-permute-start | bytes 122888 | tf_op jit(solution)/shard_map/pre_lo/ppermute | solution.py:332
  13.8 11.0 %collective-permute-start.4 = (f32[1,80,128]{2,1,0:T(8,128)S(1)}, f32[1,80,128]{2,1,0:T(8,128)S(1)}, u32[]{:S(2)}, u32[]{:S(2)}) collective-permute-start(f32[1,80,128]{2,1,0:T(8,128)S(1)} %get-tuple-element.191), channel_id=1, source_target_pairs={{8,0},{16,8},{24,16},{9,1},{17,9},{25,17},{10,2},{18,10},{26,18},{... | collective-permute-start | bytes 122888 | tf_op jit(solution)/shard_map/pre_hi/ppermute | solution.py:336
  23.3 29.7 %collective-permute-start.5 = (bf16[4,6,3,32,128]{4,3,2,1,0:T(8,128)(2,1)}, bf16[4,6,3,32,128]{4,3,2,1,0:T(8,128)(2,1)S(1)}, u32[]{:S(2)}, u32[]{:S(2)}) collective-permute-start(bf16[4,6,3,32,128]{4,3,2,1,0:T(8,128)(2,1)} %get-tuple-element.107), channel_id=1, source_target_pairs={{0,2},{1,3},{2,0},{3,1},{4,6},{5,7},{6,4},{7,5},{8,10},{9,11},{10,... | collective-permute-start | bytes 1769480 | tf_op jit(solution)/shard_map/xy1_1/ppermute | solution.py:324
  24.8 29.4 %collective-permute-start.6 = (bf16[4,6,3,32,128]{4,3,2,1,0:T(8,128)(2,1)}, bf16[4,6,3,32,128]{4,3,2,1,0:T(8,128)(2,1)S(1)}, u32[]{:S(2)}, u32[]{:S(2)}) collective-permute-start(bf16[4,6,3,32,128]{4,3,2,1,0:T(8,128)(2,1)} %get-tuple-element.108), channel_id=1, source_target_pairs={{0,4},{1,5},{2,6},{3,7},{4,0},{5,1},{6,2},{7,3},{8,12},{9,13},{10,... | collective-permute-start | bytes 1769480 | tf_op jit(solution)/shard_map/xy1_2/ppermute | solution.py:324
  27.7 27.4 %collective-permute-start.7 = (bf16[4,6,3,32,128]{4,3,2,1,0:T(8,128)(2,1)}, bf16[4,6,3,32,128]{4,3,2,1,0:T(8,128)(2,1)S(1)}, u32[]{:S(2)}, u32[]{:S(2)}) collective-permute-start(bf16[4,6,3,32,128]{4,3,2,1,0:T(8,128)(2,1)} %get-tuple-element.109), channel_id=1, source_target_pairs={{0,6},{1,7},{2,4},{3,5},{4,2},{5,3},{6,0},{7,1},{8,14},{9,15},{10,... | collective-permute-start | bytes 1769480 | tf_op jit(solution)/shard_map/xy1_3/ppermute | solution.py:324
  29.2 8.3 %copy-start.3 = (f32[32]{0:T(128)S(1)}, f32[32]{0:T(128)}, u32[]{:S(2)}) copy-start(f32[32]{0:T(128)} %param.9) | copy-start | bytes 388
  32.0 24.5 %collective-permute-start.8 = (bf16[4,384,128]{2,1,0:T(8,128)(2,1)}, bf16[4,384,128]{2,1,0:T(8,128)(2,1)S(1)}, u32[]{:S(2)}, u32[]{:S(2)}) collective-permute-start(bf16[4,384,128]{2,1,0:T(8,128)(2,1)} %get-tuple-element.133), channel_id=1, source_target_pairs={{0,8},{8,16},{16,24},{1,9},{9,17},{17,25},{2,10},{10,18},{18,26},{... | collective-permute-start | bytes 1179656 | tf_op jit(solution)/shard_map/z0_lo/ppermute | solution.py:332
  36.2 21.0 %collective-permute-start.9 = (bf16[4,384,128]{2,1,0:T(8,128)(2,1)}, bf16[4,384,128]{2,1,0:T(8,128)(2,1)}, u32[]{:S(2)}, u32[]{:S(2)}) collective-permute-start(bf16[4,384,128]{2,1,0:T(8,128)(2,1)} %get-tuple-element.134), channel_id=1, source_target_pairs={{8,0},{16,8},{24,16},{9,1},{17,9},{25,17},{10,2},{18,10},{26,18},{... | collective-permute-start | bytes 1179656 | tf_op jit(solution)/shard_map/z0_hi/ppermute | solution.py:336
  38.1 14.7 %all-to-all-start = ((f32[8,1,32]{2,1,0:T(1,128)}), f32[8,1,32]{2,1,0:T(1,128)S(1)}, u32[]{:S(2)}, u32[]{:S(2)}) async-start(f32[8,1,32]{2,1,0:T(1,128)} %broadcast_in_dim.10), calls=%async_computation | async-start | bytes 8192 | tf_op jit(solution)/shard_map/pre_eig/all_to_all | solution.py:355
  52.9 4.3 %copy-start.13 = (bf16[4,6,3,32,128]{4,3,2,1,0:T(8,128)(2,1)}, bf16[4,6,3,32,128]{4,3,2,1,0:T(8,128)(2,1)S(1)}, u32[]{:S(2)}) copy-start(bf16[4,6,3,32,128]{4,3,2,1,0:T(8,128)(2,1)S(1)} %collective-permute-done.5) | copy-start | bytes 1769476
  52.9 23.0 %collective-permute-start.13 = (bf16[4,6,3,32,128]{4,3,2,1,0:T(8,128)(2,1)}, bf16[4,6,3,32,128]{4,3,2,1,0:T(8,128)(2,1)}, u32[]{:S(2)}, u32[]{:S(2)}) collective-permute-start(bf16[4,6,3,32,128]{4,3,2,1,0:T(8,128)(2,1)} %get-tuple-element.148), channel_id=1, source_target_pairs={{0,2},{1,3},{2,0},{3,1},{4,6},{5,7},{6,4},{7,5},{8,10},{9,11},{10,... | collective-permute-start | bytes 1769480 | tf_op jit(solution)/shard_map/xy2_1/ppermute | solution.py:324
  54.2 3.0 %copy-start.14 = (bf16[4,6,3,32,128]{4,3,2,1,0:T(8,128)(2,1)}, bf16[4,6,3,32,128]{4,3,2,1,0:T(8,128)(2,1)S(1)}, u32[]{:S(2)}) copy-start(bf16[4,6,3,32,128]{4,3,2,1,0:T(8,128)(2,1)S(1)} %collective-permute-done.6) | copy-start | bytes 1769476
  54.2 25.5 %collective-permute-start.14 = (bf16[4,6,3,32,128]{4,3,2,1,0:T(8,128)(2,1)}, bf16[4,6,3,32,128]{4,3,2,1,0:T(8,128)(2,1)}, u32[]{:S(2)}, u32[]{:S(2)}) collective-permute-start(bf16[4,6,3,32,128]{4,3,2,1,0:T(8,128)(2,1)} %get-tuple-element.149), channel_id=1, source_target_pairs={{0,4},{1,5},{2,6},{3,7},{4,0},{5,1},{6,2},{7,3},{8,12},{9,13},{10,... | collective-permute-start | bytes 1769480 | tf_op jit(solution)/shard_map/xy2_2/ppermute | solution.py:324
  55.1 2.2 %copy-start.15 = (bf16[4,6,3,32,128]{4,3,2,1,0:T(8,128)(2,1)}, bf16[4,6,3,32,128]{4,3,2,1,0:T(8,128)(2,1)S(1)}, u32[]{:S(2)}) copy-start(bf16[4,6,3,32,128]{4,3,2,1,0:T(8,128)(2,1)S(1)} %collective-permute-done.7) | copy-start | bytes 1769476
  55.1 28.0 %collective-permute-start.15 = (bf16[4,6,3,32,128]{4,3,2,1,0:T(8,128)(2,1)}, bf16[4,6,3,32,128]{4,3,2,1,0:T(8,128)(2,1)}, u32[]{:S(2)}, u32[]{:S(2)}) collective-permute-start(bf16[4,6,3,32,128]{4,3,2,1,0:T(8,128)(2,1)} %get-tuple-element.150), channel_id=1, source_target_pairs={{0,6},{1,7},{2,4},{3,5},{4,2},{5,3},{6,0},{7,1},{8,14},{9,15},{10,... | collective-permute-start | bytes 1769480 | tf_op jit(solution)/shard_map/xy2_3/ppermute | solution.py:324
  57.2 7.5 %collective-permute-start.18 = (bf16[4,4,384,128]{3,2,1,0:T(8,128)(2,1)}, bf16[4,4,384,128]{3,2,1,0:T(8,128)(2,1)S(1)}, u32[]{:S(2)}, u32[]{:S(2)}) collective-permute-start(bf16[4,4,384,128]{3,2,1,0:T(8,128)(2,1)} %get-tuple-element.157.refs_3_.refs_8_), channel_id=1, source_target_pairs={{0,1},{1,0},{2,3},{3,2},{4,5},{5,4},{6,7},{7,6},{8,9},{9,8},{10,11... | collective-permute-start | bytes 4718600 | tf_op jit(solution)/shard_map/core0/ppermute | solution.py:328
  60.4 23.7 %collective-permute-start.16 = (bf16[6,384,128]{2,1,0:T(8,128)(2,1)}, bf16[6,384,128]{2,1,0:T(8,128)(2,1)}, u32[]{:S(2)}, u32[]{:S(2)}) collective-permute-start(bf16[6,384,128]{2,1,0:T(8,128)(2,1)} %get-tuple-element.155), channel_id=1, source_target_pairs={{0,8},{8,16},{16,24},{1,9},{9,17},{17,25},{2,10},{10,18},{18,26},{... | collective-permute-start | bytes 1769480 | tf_op jit(solution)/shard_map/z1_lo/ppermute | solution.py:332
  64.8 2.0 %copy-start.9 = (bf16[4,4,384,128]{3,2,1,0:T(8,128)(2,1)}, bf16[4,4,384,128]{3,2,1,0:T(8,128)(2,1)S(1)}, u32[]{:S(2)}) copy-start(bf16[4,4,384,128]{3,2,1,0:T(8,128)(2,1)S(1)} %collective-permute-done.18.refs_6_.refs_11_) | copy-start | bytes 4718596
  64.8 20.4 %collective-permute-start.17 = (bf16[6,384,128]{2,1,0:T(8,128)(2,1)}, bf16[6,384,128]{2,1,0:T(8,128)(2,1)}, u32[]{:S(2)}, u32[]{:S(2)}) collective-permute-start(bf16[6,384,128]{2,1,0:T(8,128)(2,1)} %get-tuple-element.156), channel_id=1, source_target_pairs={{8,0},{16,8},{24,16},{9,1},{17,9},{25,17},{10,2},{18,10},{26,18},{... | collective-permute-start | bytes 1769480 | tf_op jit(solution)/shard_map/z1_hi/ppermute | solution.py:336
  66.8 9.2 %copy-start.4 = (bf16[4,6,384,128]{3,2,1,0:T(8,128)(2,1)S(1)}, bf16[4,6,384,128]{3,2,1,0:T(8,128)(2,1)}, u32[]{:S(2)}) copy-start(bf16[4,6,384,128]{3,2,1,0:T(8,128)(2,1)} %get-tuple-element.169.refs_4_.refs_8_) | copy-start | bytes 7077892
  66.8 12.9 %copy-start.12 = (bf16[4,6,3,32,128]{4,3,2,1,0:T(8,128)(2,1)S(1)}, bf16[4,6,3,32,128]{4,3,2,1,0:T(8,128)(2,1)}, u32[]{:S(2)}) copy-start(bf16[4,6,3,32,128]{4,3,2,1,0:T(8,128)(2,1)} %get-tuple-element.144) | copy-start | bytes 1769476
  66.8 16.3 %copy-start.11 = (bf16[4,6,3,32,128]{4,3,2,1,0:T(8,128)(2,1)S(1)}, bf16[4,6,3,32,128]{4,3,2,1,0:T(8,128)(2,1)}, u32[]{:S(2)}) copy-start(bf16[4,6,3,32,128]{4,3,2,1,0:T(8,128)(2,1)} %get-tuple-element.145) | copy-start | bytes 1769476
  66.8 17.3 %copy-start.10 = (bf16[4,6,3,32,128]{4,3,2,1,0:T(8,128)(2,1)S(1)}, bf16[4,6,3,32,128]{4,3,2,1,0:T(8,128)(2,1)}, u32[]{:S(2)}) copy-start(bf16[4,6,3,32,128]{4,3,2,1,0:T(8,128)(2,1)} %get-tuple-element.146) | copy-start | bytes 1769476
  75.9 15.9 %collective-permute-start.21 = (bf16[4,6,384,128]{3,2,1,0:T(8,128)(2,1)S(1)}, bf16[4,6,384,128]{3,2,1,0:T(8,128)(2,1)S(1)}, u32[]{:S(2)}, u32[]{:S(2)}) collective-permute-start(bf16[4,6,384,128]{3,2,1,0:T(8,128)(2,1)S(1)} %copy-done.4), channel_id=1, source_target_pairs={{0,1},{1,0},{2,3},{3,2},{4,5},{5,4},{6,7},{7,6},{8,9},{9,8},{10,11... | collective-permute-start | bytes 7077896 | tf_op jit(solution)/shard_map/core1/ppermute | solution.py:328
  79.7 33.6 %collective-permute-start.10 = (bf16[4,6,3,32,128]{4,3,2,1,0:T(8,128)(2,1)S(1)}, bf16[4,6,3,32,128]{4,3,2,1,0:T(8,128)(2,1)}, u32[]{:S(2)}, u32[]{:S(2)}) collective-permute-start(bf16[4,6,3,32,128]{4,3,2,1,0:T(8,128)(2,1)S(1)} %copy-done.12), channel_id=1, source_target_pairs={{0,2},{1,3},{2,0},{3,1},{4,6},{5,7},{6,4},{7,5},{8,10},{9,11},{10,... | collective-permute-start | bytes 1769480 | tf_op jit(solution)/shard_map/xy3_1/ppermute | solution.py:324
  83.1 30.3 %collective-permute-start.11 = (bf16[4,6,3,32,128]{4,3,2,1,0:T(8,128)(2,1)S(1)}, bf16[4,6,3,32,128]{4,3,2,1,0:T(8,128)(2,1)}, u32[]{:S(2)}, u32[]{:S(2)}) collective-permute-start(bf16[4,6,3,32,128]{4,3,2,1,0:T(8,128)(2,1)S(1)} %copy-done.11), channel_id=1, source_target_pairs={{0,4},{1,5},{2,6},{3,7},{4,0},{5,1},{6,2},{7,3},{8,12},{9,13},{10,... | collective-permute-start | bytes 1769480 | tf_op jit(solution)/shard_map/xy3_2/ppermute | solution.py:324
  84.1 29.3 %collective-permute-start.12 = (bf16[4,6,3,32,128]{4,3,2,1,0:T(8,128)(2,1)S(1)}, bf16[4,6,3,32,128]{4,3,2,1,0:T(8,128)(2,1)}, u32[]{:S(2)}, u32[]{:S(2)}) collective-permute-start(bf16[4,6,3,32,128]{4,3,2,1,0:T(8,128)(2,1)S(1)} %copy-done.10), channel_id=1, source_target_pairs={{0,6},{1,7},{2,4},{3,5},{4,2},{5,3},{6,0},{7,1},{8,14},{9,15},{10,... | collective-permute-start | bytes 1769480 | tf_op jit(solution)/shard_map/xy3_3/ppermute | solution.py:324
  88.3 25.1 %collective-permute-start.19 = (bf16[6,384,128]{2,1,0:T(8,128)(2,1)}, bf16[6,384,128]{2,1,0:T(8,128)(2,1)S(1)}, u32[]{:S(2)}, u32[]{:S(2)}) collective-permute-start(bf16[6,384,128]{2,1,0:T(8,128)(2,1)} %get-tuple-element.166), channel_id=1, source_target_pairs={{0,8},{8,16},{16,24},{1,9},{9,17},{17,25},{2,10},{10,18},{18,26},{... | collective-permute-start | bytes 1769480 | tf_op jit(solution)/shard_map/z2_lo/ppermute | solution.py:332
  91.8 21.5 %copy-start.6 = (bf16[4,6,384,128]{3,2,1,0:T(8,128)(2,1)S(1)}, bf16[4,6,384,128]{3,2,1,0:T(8,128)(2,1)}, u32[]{:S(2)}) copy-start(bf16[4,6,384,128]{3,2,1,0:T(8,128)(2,1)} %get-tuple-element.175.refs_4_.refs_8_) | copy-start | bytes 7077892
  91.8 21.6 %collective-permute-start.20 = (bf16[6,384,128]{2,1,0:T(8,128)(2,1)}, bf16[6,384,128]{2,1,0:T(8,128)(2,1)S(1)}, u32[]{:S(2)}, u32[]{:S(2)}) collective-permute-start(bf16[6,384,128]{2,1,0:T(8,128)(2,1)} %get-tuple-element.167), channel_id=1, source_target_pairs={{8,0},{16,8},{24,16},{9,1},{17,9},{25,17},{10,2},{18,10},{26,18},{... | collective-permute-start | bytes 1769480 | tf_op jit(solution)/shard_map/z2_hi/ppermute | solution.py:336
  113.3 10.3 %collective-permute-start.22 = (bf16[4,6,384,128]{3,2,1,0:T(8,128)(2,1)S(1)}, bf16[4,6,384,128]{3,2,1,0:T(8,128)(2,1)S(1)}, u32[]{:S(2)}, u32[]{:S(2)}) collective-permute-start(bf16[4,6,384,128]{3,2,1,0:T(8,128)(2,1)S(1)} %copy-done.6), channel_id=1, source_target_pairs={{0,1},{1,0},{2,3},{3,2},{4,5},{5,4},{6,7},{7,6},{8,9},{9,8},{10,11... | collective-permute-start | bytes 7077896 | tf_op jit(solution)/shard_map/core2/ppermute | solution.py:328
  113.4 3.5 %copy-start.16 = (bf16[6,384,128]{2,1,0:T(8,128)(2,1)}, bf16[6,384,128]{2,1,0:T(8,128)(2,1)S(1)}, u32[]{:S(2)}) copy-start(bf16[6,384,128]{2,1,0:T(8,128)(2,1)S(1)} %collective-permute-done.19.refs_5_.refs_9_) | copy-start | bytes 1769476
  113.4 3.5 %copy-start.17 = (bf16[6,384,128]{2,1,0:T(8,128)(2,1)}, bf16[6,384,128]{2,1,0:T(8,128)(2,1)S(1)}, u32[]{:S(2)}) copy-start(bf16[6,384,128]{2,1,0:T(8,128)(2,1)S(1)} %collective-permute-done.20.refs_6_.refs_10_) | copy-start | bytes 1769476
  117.0 27.9 %collective-permute-start.25 = (bf16[4,6,384,128]{3,2,1,0:T(8,128)(2,1)}, bf16[4,6,384,128]{3,2,1,0:T(8,128)(2,1)S(1)}, u32[]{:S(2)}, u32[]{:S(2)}) collective-permute-start(bf16[4,6,384,128]{3,2,1,0:T(8,128)(2,1)} %get-tuple-element.184.refs_4_), channel_id=1, source_target_pairs={{0,1},{1,0},{2,3},{3,2},{4,5},{5,4},{6,7},{7,6},{8,9},{9,8},{10,11... | collective-permute-start | bytes 7077896 | tf_op jit(solution)/shard_map/core3/ppermute | solution.py:328
  117.5 27.4 %collective-permute-start.23 = (bf16[6,384,128]{2,1,0:T(8,128)(2,1)}, bf16[6,384,128]{2,1,0:T(8,128)(2,1)S(1)}, u32[]{:S(2)}, u32[]{:S(2)}) collective-permute-start(bf16[6,384,128]{2,1,0:T(8,128)(2,1)} %get-tuple-element.185), channel_id=1, source_target_pairs={{0,8},{8,16},{16,24},{1,9},{9,17},{17,25},{2,10},{10,18},{18,26},{... | collective-permute-start | bytes 1769480 | tf_op jit(solution)/shard_map/z3_lo/ppermute | solution.py:332
  122.1 22.8 %collective-permute-start.24 = (bf16[6,384,128]{2,1,0:T(8,128)(2,1)}, bf16[6,384,128]{2,1,0:T(8,128)(2,1)S(1)}, u32[]{:S(2)}, u32[]{:S(2)}) collective-permute-start(bf16[6,384,128]{2,1,0:T(8,128)(2,1)} %get-tuple-element.186), channel_id=1, source_target_pairs={{8,0},{16,8},{24,16},{9,1},{17,9},{25,17},{10,2},{18,10},{26,18},{... | collective-permute-start | bytes 1769480 | tf_op jit(solution)/shard_map/z3_hi/ppermute | solution.py:336
  168.9 5.0 %collective-permute-start.28 = (f32[64,128]{1,0:T(8,128)}, f32[64,128]{1,0:T(8,128)S(1)}, u32[]{:S(2)}, u32[]{:S(2)}) collective-permute-start(f32[64,128]{1,0:T(8,128)} %get-tuple-element.190), channel_id=1, source_target_pairs={{0,6},{1,7},{2,4},{3,5},{4,2},{5,3},{6,0},{7,1},{8,14},{9,15},{10,... | collective-permute-start | bytes 98312 | tf_op jit(solution)/shard_map/fin_3/ppermute | solution.py:324
  170.8 4.1 %collective-permute-start.27 = (f32[64,128]{1,0:T(8,128)}, f32[64,128]{1,0:T(8,128)S(1)}, u32[]{:S(2)}, u32[]{:S(2)}) collective-permute-start(f32[64,128]{1,0:T(8,128)} %get-tuple-element.189), channel_id=1, source_target_pairs={{0,4},{1,5},{2,6},{3,7},{4,0},{5,1},{6,2},{7,3},{8,12},{9,13},{10,... | collective-permute-start | bytes 98312 | tf_op jit(solution)/shard_map/fin_2/ppermute | solution.py:324
  171.7 4.1 %collective-permute-start.26 = (f32[64,128]{1,0:T(8,128)}, f32[64,128]{1,0:T(8,128)S(1)}, u32[]{:S(2)}, u32[]{:S(2)}) collective-permute-start(f32[64,128]{1,0:T(8,128)} %get-tuple-element.188), channel_id=1, source_target_pairs={{0,2},{1,3},{2,0},{3,1},{4,6},{5,7},{6,4},{7,5},{8,10},{9,11},{10,... | collective-permute-start | bytes 98312 | tf_op jit(solution)/shard_map/fin_1/ppermute | solution.py:324
  176.6 6.4 %collective-permute-start.31 = (f32[64,128]{1,0:T(8,128)S(1)}, f32[64,128]{1,0:T(8,128)S(1)}, u32[]{:S(2)}, u32[]{:S(2)}) collective-permute-start(f32[64,128]{1,0:T(8,128)S(1)} %add_add_fusion), channel_id=1, source_target_pairs={{0,24},{8,0},{16,8},{24,16},{1,25},{9,1},{17,9},{25,17},{2,26},{10... | collective-permute-start | bytes 98312 | tf_op jit(solution)/shard_map/ppermute | solution.py:419
  181.4 4.8 %collective-permute-start.30 = (f32[64,128]{1,0:T(8,128)S(1)}, f32[64,128]{1,0:T(8,128)S(1)}, u32[]{:S(2)}, u32[]{:S(2)}) collective-permute-start(f32[64,128]{1,0:T(8,128)S(1)} %add_add_fusion), channel_id=1, source_target_pairs={{0,16},{8,24},{16,0},{24,8},{1,17},{9,25},{17,1},{25,9},{2,18},{10... | collective-permute-start | bytes 98312 | tf_op jit(solution)/shard_map/ppermute | solution.py:419
  181.4 5.7 %collective-permute-start.29 = (f32[64,128]{1,0:T(8,128)S(1)}, f32[64,128]{1,0:T(8,128)S(1)}, u32[]{:S(2)}, u32[]{:S(2)}) collective-permute-start(f32[64,128]{1,0:T(8,128)S(1)} %add_add_fusion), channel_id=1, source_target_pairs={{0,8},{8,16},{16,24},{24,0},{1,9},{9,17},{17,25},{25,1},{2,10},{10... | collective-permute-start | bytes 98312 | tf_op jit(solution)/shard_map/ppermute | solution.py:419
  (8 other events, 9.7 us)

commit v4 on v3

--- a/solution.py
+++ b/solution.py
@@ -78,10 +78,10 @@
 def load_kernel(first_row, prev_rows, rows, own, parts, *refs):
     if prev_rows:
         (thick_ref, tap_ref, lam_ref, s_ref, f_ref, lo_ref, hi_ref, e_ref, fp_ref, lop_ref, hip_ref, ep_ref,
-         out_ref, win, other, g0, g1, l_ref, sems) = refs
+         out_ref, win, other, g0, g1, l0, l1, sems) = refs
     else:
         (thick_ref, tap_ref, lam_ref, f_ref, lo_ref, hi_ref, e_ref,
-         out_ref, win, other, g0, g1, l_ref, sems) = refs
+         out_ref, win, other, g0, g1, l0, l1, sems) = refs
     planes = f_ref.shape[0]
     size_z = f_ref.shape[-1]
     width = f_ref.shape[2]
@@ -149,13 +149,19 @@
             [block[(k * comps + c) * local : (k * comps + c + 1) * local] for k in range(parts)], axis=0
         )
 
-    for ab in range(9):
-        bands(g0, 0, 0, ab)
-    arrived(0)
-    arrived(1)
-
-    def row(y, _):
-        arrived(y + 2)
+    cells = [(x, c) for x in range(planes) for c in range(comps)]
+
+    def gather_sums(y, l_ref):
+        mine = jnp.concatenate([modes_of(win[x + 1, y + 1], c) for x, c in cells], axis=1)
+        theirs = jnp.concatenate([modes_of(other[x, y], c) for x, c in cells], axis=1)
+        out_ref[...] += lax.dot_general(
+            jnp.concatenate([mine, theirs], axis=0),
+            l_ref[...],
+            (((1,), (1,)), ((), ())),
+            preferred_element_type=jnp.float32,
+        )
+
+    def stencils(y, l_ref):
         for x in range(planes):
             now, then = (g0, g1) if x % 2 == 0 else (g1, g0)
             images = None
@@ -176,19 +182,35 @@
                 l_ref[:, (x * comps + c) * size_z : (x * comps + c + 1) * size_z] = (
                     image[:, :size_z] - lam_ref[...] * image[:, size_z:]
                 ).astype(jnp.bfloat16)
+
+    def other_arrived(y):
         pltpu.make_async_copy(e_ref.at[:, 0], other.at[:, y], sems.at[y + 1, 3]).wait()
-        cells = [(x, c) for x in range(planes) for c in range(comps)]
-        mine = jnp.concatenate([modes_of(win[x + 1, y + 1], c) for x, c in cells], axis=1)
-        theirs = jnp.concatenate([modes_of(other[x, y], c) for x, c in cells], axis=1)
-        out_ref[...] += lax.dot_general(
-            jnp.concatenate([mine, theirs], axis=0),
-            l_ref[...],
-            (((1,), (1,)), ((), ())),
-            preferred_element_type=jnp.float32,
-        )
+
+    for ab in range(9):
+        bands(g0, 0, 0, ab)
+    arrived(0)
+    arrived(1)
+    other_arrived(0)
+    l1[...] = jnp.zeros_like(l1)
+
+    def two_rows(n, _):
+        y = 2 * n
+        arrived(y + 2)
+        arrived(y + 3)
+        gather_sums(jnp.maximum(y - 1, 0), l1)
+        stencils(y, l0)
+        gather_sums(y, l0)
+        stencils(y + 1, l1)
+        other_arrived(y + 1)
+
+        @pl.when(y + 2 < done)
+        def _():
+            other_arrived(y + 2)
+
         return 0
 
-    lax.fori_loop(0, done, row, 0)
+    lax.fori_loop(0, done // 2, two_rows, 0)
+    gather_sums(done - 1, l1)
 
 
 def load(first_row, thick, taps, lam, sums, now, before, own, parts):
@@ -212,6 +234,7 @@
             pltpu.VMEM((planes, done, width, size_z), jnp.bfloat16),
             pltpu.VMEM((depth, 2 * size_z), jnp.bfloat16),
             pltpu.VMEM((depth, 2 * size_z), jnp.bfloat16),
+            pltpu.VMEM((own, planes * width // own * size_z), jnp.bfloat16),
             pltpu.VMEM((own, planes * width // own * size_z), jnp.bfloat16),
             pltpu.SemaphoreType.DMA((done + 2, 4)),
         ],

time: 189 us -> 188 us (level)
  no operation moved by 1% of the time
where the time goes in v4:
time: 188 us; the launch traced here: 187 us
  Pallas kernels  95.4 us (51%)
  starting transfers between devices  57.3 us (30%)
  waiting for transfers between devices  22.8 us (12%)
  local copies, waits for them, and re-layouts  8.12 us (4%)
  other arithmetic  2.6 us (1%)
    pallas_call x4, Pallas kernels, load(): pl.pallas_call(functools.partial(load_kernel, first_row, prev_rows, rows,...  68.3 us
    ppermute x5, starting transfers between devices, from_below(): lax.ppermute(value, 'sector', [(i, i + 1) for i in range(sectors - 1)])  20.4 us
    ppermute x15, starting transfers between devices, other_part(): return lax.ppermute(value, 'mode', [(i, i ^ 2 * k) for i in range(groups)])  19.6 us
    pallas_call x2, Pallas kernels, pack(): pl.pallas_call(functools.partial(pack_kernel, height, parts, chunks), gri...  12.9 us
    pallas_call x4, Pallas kernels, join(): pl.pallas_call(functools.partial(join_kernel, parts), in_specs=[hbm] * pa...  12.4 us
    all_to_all x1, waiting for transfers between devices, on_device(): lax.all_to_all(jnp.broadcast_to(held_back[None], (groups, local)), 'mode'...  10.4 us
    ppermute x15, waiting for transfers between devices, other_part(): return lax.ppermute(value, 'mode', [(i, i ^ 2 * k) for i in range(groups)])  7.73 us
    ppermute x5, starting transfers between devices, from_above(): lax.ppermute(value, 'sector', [(i + 1, i) for i in range(sectors - 1)])  6.89 us
  transfers between devices with their start and end apart: 33, of which 10 were waited for; matrix products, arithmetic and copies ran while one was open for 2% of the time, Pallas kernels for 37%

profile of v4, /device:TPU:0, one launch (start us, length us, event | category | flops | bytes accessed | tf_op | source)
XLA Modules:
  0.0 186.7 jit_solution(10796711273615427280)
XLA Ops:
  0.0 5.3 %pack.2 = (bf16[4,4,3,32,128]{4,3,2,1,0:T(8,128)(2,1)}, bf16[4,4,3,32,128]{4,3,2,1,0:T(8,128)(2,1)}, bf16[4,4,3,32,128]{4,3,2,1,0:T(8,128)(2,1)}, bf16[4,4,3,32,128]{4,3,2,1,0:T(8,128)(2,1)}) custom-call(s32[1]{0:T(128)} %bitcast.me_ref, bf16[32,3,4,80,128]{4,3,2,1,0:T(8,128)(2,1)} %in_ref.3), custom_call_target="tpu_custom_call" | custom-call | bytes 15728640 | tf_op jit(solution)/shard_map/pack/pallas_call | solution.py:61
  5.3 3.0 %collective-permute-start = (bf16[4,4,3,32,128]{4,3,2,1,0:T(8,128)(2,1)}, bf16[4,4,3,32,128]{4,3,2,1,0:T(8,128)(2,1)S(1)}, u32[]{:S(2)}, u32[]{:S(2)}) collective-permute-start(bf16[4,4,3,32,128]{4,3,2,1,0:T(8,128)(2,1)} %get-tuple-element.103), channel_id=1, source_target_pairs={{0,2},{1,3},{2,0},{3,1},{4,6},{5,7},{6,4},{7,5},{8,10},{9,11},{10,... | collective-permute-start | bytes 1179656 | tf_op jit(solution)/shard_map/xy0_1/ppermute | solution.py:347
  8.3 1.5 collective-permute-start.1
  9.8 4.0 %collective-permute-start.3 = (f32[1,80,128]{2,1,0:T(8,128)S(1)}, f32[1,80,128]{2,1,0:T(8,128)S(1)}, u32[]{:S(2)}, u32[]{:S(2)}) collective-permute-start(f32[1,80,128]{2,1,0:T(8,128)S(1)} %get-tuple-element.192), channel_id=1, source_target_pairs={{0,8},{8,16},{16,24},{1,9},{9,17},{17,25},{2,10},{10,18},{18,26},{... | collective-permute-start | bytes 122888 | tf_op jit(solution)/shard_map/pre_lo/ppermute | solution.py:355
  13.8 1.3 collective-permute-start.4
  15.5 7.6 %pack.3 = (bf16[4,6,3,32,128]{4,3,2,1,0:T(8,128)(2,1)}, bf16[4,6,3,32,128]{4,3,2,1,0:T(8,128)(2,1)}, bf16[4,6,3,32,128]{4,3,2,1,0:T(8,128)(2,1)}, bf16[4,6,3,32,...) custom-call(s32[1]{0:T(128)} %bitcast.me_ref, ...), custom_call_target="tpu_custom_call" | custom-call | bytes 15728640 | tf_op jit(solution)/shard_map/pack/pallas_call | solution.py:61
  23.3 1.5 collective-permute-start.5
  24.8 1.5 collective-permute-start.6
  26.8 0.9 pad_maximum_fusion.refs_0_
  29.2 2.7 %join.4 = (bf16[4,4,384,128]{3,2,1,0:T(8,128)(2,1)}, bf16[4,384,128]{2,1,0:T(8,128)(2,1)}, bf16[4,384,128]{2,1,0:T(8,128)(2,1)}) custom-call(bf16[4,4,96,128]{3,2,1,0:T(8,128)(2,1)} %bitcast.40, bf16[4,4,96,128]{3,2,1,0:T(8,128)(2,1)} %bitcast.41, bf16[4,4,96,128]{3,2,1,0:T(8,128)(2,1)} %bitcast.42, bf16[4,4,96,128]{3,2,1,0:T(8,128)(2,1)} %bitcast.13.refs_3_), custom_call_target="tpu_custom_call" | custom-call | flops 49999998976 | tf_op jit(solution)/shard_map/join/pallas_call | solution.py:288
  32.0 4.3 %collective-permute-start.8 = (bf16[4,384,128]{2,1,0:T(8,128)(2,1)}, bf16[4,384,128]{2,1,0:T(8,128)(2,1)S(1)}, u32[]{:S(2)}, u32[]{:S(2)}) collective-permute-start(bf16[4,384,128]{2,1,0:T(8,128)(2,1)} %get-tuple-element.133), channel_id=1, source_target_pairs={{0,8},{8,16},{16,24},{1,9},{9,17},{17,25},{2,10},{10,18},{18,26},{... | collective-permute-start | bytes 1179656 | tf_op jit(solution)/shard_map/z0_lo/ppermute | solution.py:355
  36.2 1.3 collective-permute-start.9
  38.1 3.7 %all-to-all-start = ((f32[8,1,32]{2,1,0:T(1,128)}), f32[8,1,32]{2,1,0:T(1,128)S(1)}, u32[]{:S(2)}, u32[]{:S(2)}) async-start(f32[8,1,32]{2,1,0:T(1,128)} %broadcast_in_dim.10), calls=%async_computation | async-start | bytes 8192 | tf_op jit(solution)/shard_map/pre_eig/all_to_all | solution.py:378
  42.4 10.4 %all-to-all-done = f32[8,1,32]{2,1,0:T(1,128)S(1)} async-done(((f32[8,1,32]{2,1,0:T(1,128)}), f32[8,1,32]{2,1,0:T(1,128)S(1)}, u32[]{:S(2)}, u32[]{:S(2)}) %all-to-all-start) | async-done | bytes 1056 | tf_op jit(solution)/shard_map/pre_eig/all_to_all | solution.py:378
  52.9 1.3 collective-permute-start.13
  54.2 0.8 collective-permute-start.14
  55.1 1.4 collective-permute-start.15
  56.5 0.7 copy-done.20
  57.3 3.1 %join.5 = (bf16[4,6,384,128]{3,2,1,0:T(8,128)(2,1)}, bf16[6,384,128]{2,1,0:T(8,128)(2,1)}, bf16[6,384,128]{2,1,0:T(8,128)(2,1)}) custom-call(bf16[4,6,96,128]{3,2,1,0:T(8,128)(2,1)} %bitcast.36, bf16[4,6,96,128]{3,2,1,0:T(8,128)(2,1)} %bitcast.37, bf16[4,6,96,128]{3,2,1,0:T(8,128)(2,1)} %bitcast.38, bf16[4,6,96,128]{3,2,1,0:T(8,128)(2,1)} %bitcast.39), custom_call_target="tpu_custom_call" | custom-call | flops 49999998976 | tf_op jit(solution)/shard_map/join/pallas_call | solution.py:288
  60.4 4.4 %collective-permute-start.16 = (bf16[6,384,128]{2,1,0:T(8,128)(2,1)}, bf16[6,384,128]{2,1,0:T(8,128)(2,1)}, u32[]{:S(2)}, u32[]{:S(2)}) collective-permute-start(bf16[6,384,128]{2,1,0:T(8,128)(2,1)} %get-tuple-element.155), channel_id=1, source_target_pairs={{0,8},{8,16},{16,24},{1,9},{9,17},{17,25},{2,10},{10,18},{18,26},{... | collective-permute-start | bytes 1769480 | tf_op jit(solution)/shard_map/z1_lo/ppermute | solution.py:355
  64.8 1.3 collective-permute-start.17
  66.8 9.9 %load.4.refs_3_ = f32[256,128]{1,0:T(8,128)} custom-call(f32[6,22,3,128]{3,2,1,0:T(4,128)} %pad_maximum_fusion.refs_0_, f32[2,9,3,128]{3,2,1,0:T(4,128)} %broadcast_in_dim.9.refs_1_, f32[128,128]{1,0:T(8,128)} %broadcast_in_dim.22.refs_2_, bf16[4,4,384,128]{3,2,1,0:T(8,128)(2,1)} %get-tuple-element.157.refs_3_.refs_8_, bf16[4,384,128]{2,1,0:T(8,128)(2,1)} %copy-done.20, ...), custom_call_target="tpu_custom_call" | custom-call | flops 49999998976 | bytes 1572864 | tf_op jit(solution)/shard_map/load/pallas_call | solution.py:227
  77.0 2.7 %collective-permute-done.14 = bf16[4,6,3,32,128]{4,3,2,1,0:T(8,128)(2,1)} collective-permute-done((bf16[4,6,3,32,128]{4,3,2,1,0:T(8,128)(2,1)}, bf16[4,6,3,32,128]{4,3,2,1,0:T(8,128)(2,1)}, u32[]{:S(2)}, u32[]{:S(2)}) %collective-permute-start.14) | collective-permute-done | bytes 589856 | tf_op jit(solution)/shard_map/xy2_2/ppermute | solution.py:347
  79.7 2.5 %collective-permute-start.10 = (bf16[4,6,3,32,128]{4,3,2,1,0:T(8,128)(2,1)S(1)}, bf16[4,6,3,32,128]{4,3,2,1,0:T(8,128)(2,1)}, u32[]{:S(2)}, u32[]{:S(2)}) collective-permute-start(bf16[4,6,3,32,128]{4,3,2,1,0:T(8,128)(2,1)S(1)} %copy-done.12), channel_id=1, source_target_pairs={{0,2},{1,3},{2,0},{3,1},{4,6},{5,7},{6,4},{7,5},{8,10},{9,11},{10,... | collective-permute-start | bytes 1769480 | tf_op jit(solution)/shard_map/xy3_1/ppermute | solution.py:347
  82.2 0.9 collective-permute-done.15
  83.1 1.0 collective-permute-start.11
  84.1 1.1 collective-permute-start.12
  85.2 3.1 %join.6 = (bf16[4,6,384,128]{3,2,1,0:T(8,128)(2,1)}, bf16[6,384,128]{2,1,0:T(8,128)(2,1)}, bf16[6,384,128]{2,1,0:T(8,128)(2,1)}) custom-call(bf16[4,6,96,128]{3,2,1,0:T(8,128)(2,1)} %bitcast.35, bf16[4,6,96,128]{3,2,1,0:T(8,128)(2,1)} %bitcast.19.refs_1_, bf16[4,6,96,128]{3,2,1,0:T(8,128)(2,1)} %bitcast.20.refs_2_, bf16[4,6,96,128]{3,2,1,0:T(8,128)(2,1)} %bitcast.21.refs_3_), custom_call_target="tpu_custom_call" | custom-call | flops 49999998976 | tf_op jit(solution)/shard_map/join/pallas_call | solution.py:288
  88.3 2.9 %collective-permute-start.19 = (bf16[6,384,128]{2,1,0:T(8,128)(2,1)}, bf16[6,384,128]{2,1,0:T(8,128)(2,1)S(1)}, u32[]{:S(2)}, u32[]{:S(2)}) collective-permute-start(bf16[6,384,128]{2,1,0:T(8,128)(2,1)} %get-tuple-element.166), channel_id=1, source_target_pairs={{0,8},{8,16},{16,24},{1,9},{9,17},{17,25},{2,10},{10,18},{18,26},{... | collective-permute-start | bytes 1769480 | tf_op jit(solution)/shard_map/z2_lo/ppermute | solution.py:355
  91.2 1.7 collective-permute-start.20
  93.0 19.5 %load.5.refs_3_ = f32[256,128]{1,0:T(8,128)} custom-call(f32[6,22,3,128]{3,2,1,0:T(4,128)} %pad_maximum_fusion.refs_0_, f32[2,9,3,128]{3,2,1,0:T(4,128)} %broadcast_in_dim.9.refs_1_, f32[128,128]{1,0:T(8,128)} %broadcast_in_dim.22.refs_2_, f32[256,128]{1,0:T(8,128)} %load.4.refs_3_, bf16[4,6,384,128]{3,2,1,0:T(8,128)(2,1)} %get-tuple-element.169.refs_4_.refs_8_, ...), custom_call_target="tpu_custom_call" | custom-call | flops 49999998976 | bytes 4718592 | tf_op jit(solution)/shard_map/load/pallas_call | solution.py:227
  112.6 3.5 %join.7 = (bf16[4,6,384,128]{3,2,1,0:T(8,128)(2,1)}, bf16[6,384,128]{2,1,0:T(8,128)(2,1)}, bf16[6,384,128]{2,1,0:T(8,128)(2,1)}) custom-call(bf16[4,6,96,128]{3,2,1,0:T(8,128)(2,1)} %bitcast.34, bf16[4,6,96,128]{3,2,1,0:T(8,128)(2,1)} %bitcast.23.refs_1_, bf16[4,6,96,128]{3,2,1,0:T(8,128)(2,1)} %bitcast.24.refs_2_, bf16[4,6,96,128]{3,2,1,0:T(8,128)(2,1)} %bitcast.25.refs_3_), custom_call_target="tpu_custom_call" | custom-call | flops 49999998976 | tf_op jit(solution)/shard_map/join/pallas_call | solution.py:288
  116.7 4.8 %collective-permute-start.23 = (bf16[6,384,128]{2,1,0:T(8,128)(2,1)}, bf16[6,384,128]{2,1,0:T(8,128)(2,1)S(1)}, u32[]{:S(2)}, u32[]{:S(2)}) collective-permute-start(bf16[6,384,128]{2,1,0:T(8,128)(2,1)} %get-tuple-element.185), channel_id=1, source_target_pairs={{0,8},{8,16},{16,24},{1,9},{9,17},{17,25},{2,10},{10,18},{18,26},{... | collective-permute-start | bytes 1769480 | tf_op jit(solution)/shard_map/z3_lo/ppermute | solution.py:355
  121.5 1.3 collective-permute-start.24
  122.9 1.4 copy-done.7
  124.3 19.5 %load.6.refs_3_ = f32[256,128]{1,0:T(8,128)} custom-call(f32[6,22,3,128]{3,2,1,0:T(4,128)} %pad_maximum_fusion.refs_0_, f32[2,9,3,128]{3,2,1,0:T(4,128)} %broadcast_in_dim.9.refs_1_, f32[128,128]{1,0:T(8,128)} %broadcast_in_dim.22.refs_2_, f32[256,128]{1,0:T(8,128)} %load.5.refs_3_, bf16[4,6,384,128]{3,2,1,0:T(8,128)(2,1)} %get-tuple-element.175.refs_4_.refs_8_, ...), custom_call_target="tpu_custom_call" | custom-call | flops 49999998976 | bytes 4718592 | tf_op jit(solution)/shard_map/load/pallas_call | solution.py:227
  143.8 0.8 copy-done.18
  144.9 1.4 copy-done.8
  146.3 19.5 %load.7.s_ref = f32[256,128]{1,0:T(8,128)} custom-call(f32[6,22,3,128]{3,2,1,0:T(4,128)} %pad_maximum_fusion.refs_0_, f32[2,9,3,128]{3,2,1,0:T(4,128)} %broadcast_in_dim.9.refs_1_, f32[128,128]{1,0:T(8,128)} %broadcast_in_dim.22.refs_2_, f32[256,128]{1,0:T(8,128)} %load.6.refs_3_, bf16[4,6,384,128]{3,2,1,0:T(8,128)(2,1)} %get-tuple-element.184.refs_4_, ...), custom_call_target="tpu_custom_call" | custom-call | flops 49999998976 | bytes 4718592 | tf_op jit(solution)/shard_map/load/pallas_call | solution.py:227
  165.8 1.7 arrange.1
  167.5 2.6 %collective-permute-start.28 = (f32[64,128]{1,0:T(8,128)}, f32[64,128]{1,0:T(8,128)S(1)}, u32[]{:S(2)}, u32[]{:S(2)}) collective-permute-start(f32[64,128]{1,0:T(8,128)} %get-tuple-element.190), channel_id=1, source_target_pairs={{0,6},{1,7},{2,4},{3,5},{4,2},{5,3},{6,0},{7,1},{8,14},{9,15},{10,... | collective-permute-start | bytes 98312 | tf_op jit(solution)/shard_map/fin_3/ppermute | solution.py:347
  171.0 1.5 collective-permute-done.28
  172.5 1.7 collective-permute-done.27
  174.7 0.8 add_add_fusion
  175.5 4.7 %collective-permute-start.31 = (f32[64,128]{1,0:T(8,128)S(1)}, f32[64,128]{1,0:T(8,128)S(1)}, u32[]{:S(2)}, u32[]{:S(2)}) collective-permute-start(f32[64,128]{1,0:T(8,128)S(1)} %add_add_fusion), channel_id=1, source_target_pairs={{0,24},{8,0},{16,8},{24,16},{1,25},{9,1},{17,9},{25,17},{2,26},{10... | collective-permute-start | bytes 98312 | tf_op jit(solution)/shard_map/ppermute | solution.py:442
  180.2 1.1 collective-permute-start.29
  181.8 3.2 %collective-permute-done.30 = f32[64,128]{1,0:T(8,128)S(1)} collective-permute-done((f32[64,128]{1,0:T(8,128)S(1)}, f32[64,128]{1,0:T(8,128)S(1)}, u32[]{:S(2)}, u32[]{:S(2)}) %collective-permute-start.30) | collective-permute-done | bytes 32800 | tf_op jit(solution)/shard_map/ppermute | solution.py:442
  185.0 0.9 collective-permute-done.29
  (98 shorter events, 8.4 us)
Async XLA Ops:
  0.0 9.8 %copy-start = (f32[4,80,128]{2,1,0:T(8,128)S(1)}, f32[4,80,128]{2,1,0:T(8,128)}, u32[]{:S(2)}) copy-start(f32[4,80,128]{2,1,0:T(8,128)} %param.6) | copy-start | bytes 491524
  0.0 15.1 %copy-start.1 = (f32[27]{0:T(128)S(1)}, f32[27]{0:T(128)}, u32[]{:S(2)}) copy-start(f32[27]{0:T(128)} %param.8) | copy-start | bytes 328
  0.0 15.3 %copy-start.2 = (f32[27]{0:T(128)S(1)}, f32[27]{0:T(128)}, u32[]{:S(2)}) copy-start(f32[27]{0:T(128)} %param.7) | copy-start | bytes 328
  5.3 22.4 %collective-permute-start = (bf16[4,4,3,32,128]{4,3,2,1,0:T(8,128)(2,1)}, bf16[4,4,3,32,128]{4,3,2,1,0:T(8,128)(2,1)S(1)}, u32[]{:S(2)}, u32[]{:S(2)}) collective-permute-start(bf16[4,4,3,32,128]{4,3,2,1,0:T(8,128)(2,1)} %get-tuple-element.103), channel_id=1, source_target_pairs={{0,2},{1,3},{2,0},{3,1},{4,6},{5,7},{6,4},{7,5},{8,10},{9,11},{10,... | collective-permute-start | bytes 1179656 | tf_op jit(solution)/shard_map/xy0_1/ppermute | solution.py:347
  8.3 19.9 %collective-permute-start.1 = (bf16[4,4,3,32,128]{4,3,2,1,0:T(8,128)(2,1)}, bf16[4,4,3,32,128]{4,3,2,1,0:T(8,128)(2,1)S(1)}, u32[]{:S(2)}, u32[]{:S(2)}) collective-permute-start(bf16[4,4,3,32,128]{4,3,2,1,0:T(8,128)(2,1)} %get-tuple-element.104), channel_id=1, source_target_pairs={{0,4},{1,5},{2,6},{3,7},{4,0},{5,1},{6,2},{7,3},{8,12},{9,13},{10,... | collective-permute-start | bytes 1179656 | tf_op jit(solution)/shard_map/xy0_2/ppermute | solution.py:347
  9.8 18.7 %collective-permute-start.2 = (bf16[4,4,3,32,128]{4,3,2,1,0:T(8,128)(2,1)}, bf16[4,4,3,32,128]{4,3,2,1,0:T(8,128)(2,1)}, u32[]{:S(2)}, u32[]{:S(2)}) collective-permute-start(bf16[4,4,3,32,128]{4,3,2,1,0:T(8,128)(2,1)} %get-tuple-element.105), channel_id=1, source_target_pairs={{0,6},{1,7},{2,4},{3,5},{4,2},{5,3},{6,0},{7,1},{8,14},{9,15},{10,... | collective-permute-start | bytes 1179656 | tf_op jit(solution)/shard_map/xy0_3/ppermute | solution.py:347
  9.8 13.5 %collective-permute-start.3 = (f32[1,80,128]{2,1,0:T(8,128)S(1)}, f32[1,80,128]{2,1,0:T(8,128)S(1)}, u32[]{:S(2)}, u32[]{:S(2)}) collective-permute-start(f32[1,80,128]{2,1,0:T(8,128)S(1)} %get-tuple-element.192), channel_id=1, source_target_pairs={{0,8},{8,16},{16,24},{1,9},{9,17},{17,25},{2,10},{10,18},{18,26},{... | collective-permute-start | bytes 122888 | tf_op jit(solution)/shard_map/pre_lo/ppermute | solution.py:355
  13.8 11.0 %collective-permute-start.4 = (f32[1,80,128]{2,1,0:T(8,128)S(1)}, f32[1,80,128]{2,1,0:T(8,128)S(1)}, u32[]{:S(2)}, u32[]{:S(2)}) collective-permute-start(f32[1,80,128]{2,1,0:T(8,128)S(1)} %get-tuple-element.191), channel_id=1, source_target_pairs={{8,0},{16,8},{24,16},{9,1},{17,9},{25,17},{10,2},{18,10},{26,18},{... | collective-permute-start | bytes 122888 | tf_op jit(solution)/shard_map/pre_hi/ppermute | solution.py:359
  23.3 29.7 %collective-permute-start.5 = (bf16[4,6,3,32,128]{4,3,2,1,0:T(8,128)(2,1)}, bf16[4,6,3,32,128]{4,3,2,1,0:T(8,128)(2,1)S(1)}, u32[]{:S(2)}, u32[]{:S(2)}) collective-permute-start(bf16[4,6,3,32,128]{4,3,2,1,0:T(8,128)(2,1)} %get-tuple-element.107), channel_id=1, source_target_pairs={{0,2},{1,3},{2,0},{3,1},{4,6},{5,7},{6,4},{7,5},{8,10},{9,11},{10,... | collective-permute-start | bytes 1769480 | tf_op jit(solution)/shard_map/xy1_1/ppermute | solution.py:347
  24.8 29.4 %collective-permute-start.6 = (bf16[4,6,3,32,128]{4,3,2,1,0:T(8,128)(2,1)}, bf16[4,6,3,32,128]{4,3,2,1,0:T(8,128)(2,1)S(1)}, u32[]{:S(2)}, u32[]{:S(2)}) collective-permute-start(bf16[4,6,3,32,128]{4,3,2,1,0:T(8,128)(2,1)} %get-tuple-element.108), channel_id=1, source_target_pairs={{0,4},{1,5},{2,6},{3,7},{4,0},{5,1},{6,2},{7,3},{8,12},{9,13},{10,... | collective-permute-start | bytes 1769480 | tf_op jit(solution)/shard_map/xy1_2/ppermute | solution.py:347
  27.7 27.4 %collective-permute-start.7 = (bf16[4,6,3,32,128]{4,3,2,1,0:T(8,128)(2,1)}, bf16[4,6,3,32,128]{4,3,2,1,0:T(8,128)(2,1)S(1)}, u32[]{:S(2)}, u32[]{:S(2)}) collective-permute-start(bf16[4,6,3,32,128]{4,3,2,1,0:T(8,128)(2,1)} %get-tuple-element.109), channel_id=1, source_target_pairs={{0,6},{1,7},{2,4},{3,5},{4,2},{5,3},{6,0},{7,1},{8,14},{9,15},{10,... | collective-permute-start | bytes 1769480 | tf_op jit(solution)/shard_map/xy1_3/ppermute | solution.py:347
  29.2 8.3 %copy-start.3 = (f32[32]{0:T(128)S(1)}, f32[32]{0:T(128)}, u32[]{:S(2)}) copy-start(f32[32]{0:T(128)} %param.9) | copy-start | bytes 388
  32.0 24.5 %collective-permute-start.8 = (bf16[4,384,128]{2,1,0:T(8,128)(2,1)}, bf16[4,384,128]{2,1,0:T(8,128)(2,1)S(1)}, u32[]{:S(2)}, u32[]{:S(2)}) collective-permute-start(bf16[4,384,128]{2,1,0:T(8,128)(2,1)} %get-tuple-element.133), channel_id=1, source_target_pairs={{0,8},{8,16},{16,24},{1,9},{9,17},{17,25},{2,10},{10,18},{18,26},{... | collective-permute-start | bytes 1179656 | tf_op jit(solution)/shard_map/z0_lo/ppermute | solution.py:355
  36.2 21.0 %collective-permute-start.9 = (bf16[4,384,128]{2,1,0:T(8,128)(2,1)}, bf16[4,384,128]{2,1,0:T(8,128)(2,1)}, u32[]{:S(2)}, u32[]{:S(2)}) collective-permute-start(bf16[4,384,128]{2,1,0:T(8,128)(2,1)} %get-tuple-element.134), channel_id=1, source_target_pairs={{8,0},{16,8},{24,16},{9,1},{17,9},{25,17},{10,2},{18,10},{26,18},{... | collective-permute-start | bytes 1179656 | tf_op jit(solution)/shard_map/z0_hi/ppermute | solution.py:359
  38.1 14.7 %all-to-all-start = ((f32[8,1,32]{2,1,0:T(1,128)}), f32[8,1,32]{2,1,0:T(1,128)S(1)}, u32[]{:S(2)}, u32[]{:S(2)}) async-start(f32[8,1,32]{2,1,0:T(1,128)} %broadcast_in_dim.10), calls=%async_computation | async-start | bytes 8192 | tf_op jit(solution)/shard_map/pre_eig/all_to_all | solution.py:378
  52.9 4.3 %copy-start.13 = (bf16[4,6,3,32,128]{4,3,2,1,0:T(8,128)(2,1)}, bf16[4,6,3,32,128]{4,3,2,1,0:T(8,128)(2,1)S(1)}, u32[]{:S(2)}) copy-start(bf16[4,6,3,32,128]{4,3,2,1,0:T(8,128)(2,1)S(1)} %collective-permute-done.5) | copy-start | bytes 1769476
  52.9 23.7 %collective-permute-start.13 = (bf16[4,6,3,32,128]{4,3,2,1,0:T(8,128)(2,1)}, bf16[4,6,3,32,128]{4,3,2,1,0:T(8,128)(2,1)}, u32[]{:S(2)}, u32[]{:S(2)}) collective-permute-start(bf16[4,6,3,32,128]{4,3,2,1,0:T(8,128)(2,1)} %get-tuple-element.148), channel_id=1, source_target_pairs={{0,2},{1,3},{2,0},{3,1},{4,6},{5,7},{6,4},{7,5},{8,10},{9,11},{10,... | collective-permute-start | bytes 1769480 | tf_op jit(solution)/shard_map/xy2_1/ppermute | solution.py:347
  54.2 3.0 %copy-start.14 = (bf16[4,6,3,32,128]{4,3,2,1,0:T(8,128)(2,1)}, bf16[4,6,3,32,128]{4,3,2,1,0:T(8,128)(2,1)S(1)}, u32[]{:S(2)}) copy-start(bf16[4,6,3,32,128]{4,3,2,1,0:T(8,128)(2,1)S(1)} %collective-permute-done.6) | copy-start | bytes 1769476
  54.2 25.5 %collective-permute-start.14 = (bf16[4,6,3,32,128]{4,3,2,1,0:T(8,128)(2,1)}, bf16[4,6,3,32,128]{4,3,2,1,0:T(8,128)(2,1)}, u32[]{:S(2)}, u32[]{:S(2)}) collective-permute-start(bf16[4,6,3,32,128]{4,3,2,1,0:T(8,128)(2,1)} %get-tuple-element.149), channel_id=1, source_target_pairs={{0,4},{1,5},{2,6},{3,7},{4,0},{5,1},{6,2},{7,3},{8,12},{9,13},{10,... | collective-permute-start | bytes 1769480 | tf_op jit(solution)/shard_map/xy2_2/ppermute | solution.py:347
  55.1 2.2 %copy-start.15 = (bf16[4,6,3,32,128]{4,3,2,1,0:T(8,128)(2,1)}, bf16[4,6,3,32,128]{4,3,2,1,0:T(8,128)(2,1)S(1)}, u32[]{:S(2)}) copy-start(bf16[4,6,3,32,128]{4,3,2,1,0:T(8,128)(2,1)S(1)} %collective-permute-done.7) | copy-start | bytes 1769476
  55.1 28.0 %collective-permute-start.15 = (bf16[4,6,3,32,128]{4,3,2,1,0:T(8,128)(2,1)}, bf16[4,6,3,32,128]{4,3,2,1,0:T(8,128)(2,1)}, u32[]{:S(2)}, u32[]{:S(2)}) collective-permute-start(bf16[4,6,3,32,128]{4,3,2,1,0:T(8,128)(2,1)} %get-tuple-element.150), channel_id=1, source_target_pairs={{0,6},{1,7},{2,4},{3,5},{4,2},{5,3},{6,0},{7,1},{8,14},{9,15},{10,... | collective-permute-start | bytes 1769480 | tf_op jit(solution)/shard_map/xy2_3/ppermute | solution.py:347
  57.2 7.5 %collective-permute-start.18 = (bf16[4,4,384,128]{3,2,1,0:T(8,128)(2,1)}, bf16[4,4,384,128]{3,2,1,0:T(8,128)(2,1)S(1)}, u32[]{:S(2)}, u32[]{:S(2)}) collective-permute-start(bf16[4,4,384,128]{3,2,1,0:T(8,128)(2,1)} %get-tuple-element.157.refs_3_.refs_8_), channel_id=1, source_target_pairs={{0,1},{1,0},{2,3},{3,2},{4,5},{5,4},{6,7},{7,6},{8,9},{9,8},{10,11... | collective-permute-start | bytes 4718600 | tf_op jit(solution)/shard_map/core0/ppermute | solution.py:351
  60.4 23.7 %collective-permute-start.16 = (bf16[6,384,128]{2,1,0:T(8,128)(2,1)}, bf16[6,384,128]{2,1,0:T(8,128)(2,1)}, u32[]{:S(2)}, u32[]{:S(2)}) collective-permute-start(bf16[6,384,128]{2,1,0:T(8,128)(2,1)} %get-tuple-element.155), channel_id=1, source_target_pairs={{0,8},{8,16},{16,24},{1,9},{9,17},{17,25},{2,10},{10,18},{18,26},{... | collective-permute-start | bytes 1769480 | tf_op jit(solution)/shard_map/z1_lo/ppermute | solution.py:355
  64.8 2.0 %copy-start.9 = (bf16[4,4,384,128]{3,2,1,0:T(8,128)(2,1)}, bf16[4,4,384,128]{3,2,1,0:T(8,128)(2,1)S(1)}, u32[]{:S(2)}) copy-start(bf16[4,4,384,128]{3,2,1,0:T(8,128)(2,1)S(1)} %collective-permute-done.18.refs_6_.refs_11_) | copy-start | bytes 4718596
  64.8 20.4 %collective-permute-start.17 = (bf16[6,384,128]{2,1,0:T(8,128)(2,1)}, bf16[6,384,128]{2,1,0:T(8,128)(2,1)}, u32[]{:S(2)}, u32[]{:S(2)}) collective-permute-start(bf16[6,384,128]{2,1,0:T(8,128)(2,1)} %get-tuple-element.156), channel_id=1, source_target_pairs={{8,0},{16,8},{24,16},{9,1},{17,9},{25,17},{10,2},{18,10},{26,18},{... | collective-permute-start | bytes 1769480 | tf_op jit(solution)/shard_map/z1_hi/ppermute | solution.py:359
  66.8 9.9 %copy-start.4 = (bf16[4,6,384,128]{3,2,1,0:T(8,128)(2,1)S(1)}, bf16[4,6,384,128]{3,2,1,0:T(8,128)(2,1)}, u32[]{:S(2)}) copy-start(bf16[4,6,384,128]{3,2,1,0:T(8,128)(2,1)} %get-tuple-element.169.refs_4_.refs_8_) | copy-start | bytes 7077892
  66.8 12.9 %copy-start.12 = (bf16[4,6,3,32,128]{4,3,2,1,0:T(8,128)(2,1)S(1)}, bf16[4,6,3,32,128]{4,3,2,1,0:T(8,128)(2,1)}, u32[]{:S(2)}) copy-start(bf16[4,6,3,32,128]{4,3,2,1,0:T(8,128)(2,1)} %get-tuple-element.144) | copy-start | bytes 1769476
  66.8 16.3 %copy-start.11 = (bf16[4,6,3,32,128]{4,3,2,1,0:T(8,128)(2,1)S(1)}, bf16[4,6,3,32,128]{4,3,2,1,0:T(8,128)(2,1)}, u32[]{:S(2)}) copy-start(bf16[4,6,3,32,128]{4,3,2,1,0:T(8,128)(2,1)} %get-tuple-element.145) | copy-start | bytes 1769476
  66.8 17.3 %copy-start.10 = (bf16[4,6,3,32,128]{4,3,2,1,0:T(8,128)(2,1)S(1)}, bf16[4,6,3,32,128]{4,3,2,1,0:T(8,128)(2,1)}, u32[]{:S(2)}) copy-start(bf16[4,6,3,32,128]{4,3,2,1,0:T(8,128)(2,1)} %get-tuple-element.146) | copy-start | bytes 1769476
  76.7 14.5 %collective-permute-start.21 = (bf16[4,6,384,128]{3,2,1,0:T(8,128)(2,1)S(1)}, bf16[4,6,384,128]{3,2,1,0:T(8,128)(2,1)S(1)}, u32[]{:S(2)}, u32[]{:S(2)}) collective-permute-start(bf16[4,6,384,128]{3,2,1,0:T(8,128)(2,1)S(1)} %copy-done.4), channel_id=1, source_target_pairs={{0,1},{1,0},{2,3},{3,2},{4,5},{5,4},{6,7},{7,6},{8,9},{9,8},{10,11... | collective-permute-start | bytes 7077896 | tf_op jit(solution)/shard_map/core1/ppermute | solution.py:351
  79.7 32.8 %collective-permute-start.10 = (bf16[4,6,3,32,128]{4,3,2,1,0:T(8,128)(2,1)S(1)}, bf16[4,6,3,32,128]{4,3,2,1,0:T(8,128)(2,1)}, u32[]{:S(2)}, u32[]{:S(2)}) collective-permute-start(bf16[4,6,3,32,128]{4,3,2,1,0:T(8,128)(2,1)S(1)} %copy-done.12), channel_id=1, source_target_pairs={{0,2},{1,3},{2,0},{3,1},{4,6},{5,7},{6,4},{7,5},{8,10},{9,11},{10,... | collective-permute-start | bytes 1769480 | tf_op jit(solution)/shard_map/xy3_1/ppermute | solution.py:347
  83.1 29.5 %collective-permute-start.11 = (bf16[4,6,3,32,128]{4,3,2,1,0:T(8,128)(2,1)S(1)}, bf16[4,6,3,32,128]{4,3,2,1,0:T(8,128)(2,1)}, u32[]{:S(2)}, u32[]{:S(2)}) collective-permute-start(bf16[4,6,3,32,128]{4,3,2,1,0:T(8,128)(2,1)S(1)} %copy-done.11), channel_id=1, source_target_pairs={{0,4},{1,5},{2,6},{3,7},{4,0},{5,1},{6,2},{7,3},{8,12},{9,13},{10,... | collective-permute-start | bytes 1769480 | tf_op jit(solution)/shard_map/xy3_2/ppermute | solution.py:347
  84.1 28.5 %collective-permute-start.12 = (bf16[4,6,3,32,128]{4,3,2,1,0:T(8,128)(2,1)S(1)}, bf16[4,6,3,32,128]{4,3,2,1,0:T(8,128)(2,1)}, u32[]{:S(2)}, u32[]{:S(2)}) collective-permute-start(bf16[4,6,3,32,128]{4,3,2,1,0:T(8,128)(2,1)S(1)} %copy-done.10), channel_id=1, source_target_pairs={{0,6},{1,7},{2,4},{3,5},{4,2},{5,3},{6,0},{7,1},{8,14},{9,15},{10,... | collective-permute-start | bytes 1769480 | tf_op jit(solution)/shard_map/xy3_3/ppermute | solution.py:347
  88.3 24.3 %collective-permute-start.19 = (bf16[6,384,128]{2,1,0:T(8,128)(2,1)}, bf16[6,384,128]{2,1,0:T(8,128)(2,1)S(1)}, u32[]{:S(2)}, u32[]{:S(2)}) collective-permute-start(bf16[6,384,128]{2,1,0:T(8,128)(2,1)} %get-tuple-element.166), channel_id=1, source_target_pairs={{0,8},{8,16},{16,24},{1,9},{9,17},{17,25},{2,10},{10,18},{18,26},{... | collective-permute-start | bytes 1769480 | tf_op jit(solution)/shard_map/z2_lo/ppermute | solution.py:355
  91.2 21.3 %copy-start.6 = (bf16[4,6,384,128]{3,2,1,0:T(8,128)(2,1)S(1)}, bf16[4,6,384,128]{3,2,1,0:T(8,128)(2,1)}, u32[]{:S(2)}) copy-start(bf16[4,6,384,128]{3,2,1,0:T(8,128)(2,1)} %get-tuple-element.175.refs_4_.refs_8_) | copy-start | bytes 7077892
  91.2 21.4 %collective-permute-start.20 = (bf16[6,384,128]{2,1,0:T(8,128)(2,1)}, bf16[6,384,128]{2,1,0:T(8,128)(2,1)S(1)}, u32[]{:S(2)}, u32[]{:S(2)}) collective-permute-start(bf16[6,384,128]{2,1,0:T(8,128)(2,1)} %get-tuple-element.167), channel_id=1, source_target_pairs={{8,0},{16,8},{24,16},{9,1},{17,9},{25,17},{10,2},{18,10},{26,18},{... | collective-permute-start | bytes 1769480 | tf_op jit(solution)/shard_map/z2_hi/ppermute | solution.py:359
  112.5 10.4 %collective-permute-start.22 = (bf16[4,6,384,128]{3,2,1,0:T(8,128)(2,1)S(1)}, bf16[4,6,384,128]{3,2,1,0:T(8,128)(2,1)S(1)}, u32[]{:S(2)}, u32[]{:S(2)}) collective-permute-start(bf16[4,6,384,128]{3,2,1,0:T(8,128)(2,1)S(1)} %copy-done.6), channel_id=1, source_target_pairs={{0,1},{1,0},{2,3},{3,2},{4,5},{5,4},{6,7},{7,6},{8,9},{9,8},{10,11... | collective-permute-start | bytes 7077896 | tf_op jit(solution)/shard_map/core2/ppermute | solution.py:351
  112.6 3.5 %copy-start.16 = (bf16[6,384,128]{2,1,0:T(8,128)(2,1)}, bf16[6,384,128]{2,1,0:T(8,128)(2,1)S(1)}, u32[]{:S(2)}) copy-start(bf16[6,384,128]{2,1,0:T(8,128)(2,1)S(1)} %collective-permute-done.19.refs_5_.refs_9_) | copy-start | bytes 1769476
  112.6 3.5 %copy-start.17 = (bf16[6,384,128]{2,1,0:T(8,128)(2,1)}, bf16[6,384,128]{2,1,0:T(8,128)(2,1)S(1)}, u32[]{:S(2)}) copy-start(bf16[6,384,128]{2,1,0:T(8,128)(2,1)S(1)} %collective-permute-done.20.refs_6_.refs_10_) | copy-start | bytes 1769476
  116.2 27.6 %collective-permute-start.25 = (bf16[4,6,384,128]{3,2,1,0:T(8,128)(2,1)}, bf16[4,6,384,128]{3,2,1,0:T(8,128)(2,1)S(1)}, u32[]{:S(2)}, u32[]{:S(2)}) collective-permute-start(bf16[4,6,384,128]{3,2,1,0:T(8,128)(2,1)} %get-tuple-element.184.refs_4_), channel_id=1, source_target_pairs={{0,1},{1,0},{2,3},{3,2},{4,5},{5,4},{6,7},{7,6},{8,9},{9,8},{10,11... | collective-permute-start | bytes 7077896 | tf_op jit(solution)/shard_map/core3/ppermute | solution.py:351
  116.7 27.1 %collective-permute-start.23 = (bf16[6,384,128]{2,1,0:T(8,128)(2,1)}, bf16[6,384,128]{2,1,0:T(8,128)(2,1)S(1)}, u32[]{:S(2)}, u32[]{:S(2)}) collective-permute-start(bf16[6,384,128]{2,1,0:T(8,128)(2,1)} %get-tuple-element.185), channel_id=1, source_target_pairs={{0,8},{8,16},{16,24},{1,9},{9,17},{17,25},{2,10},{10,18},{18,26},{... | collective-permute-start | bytes 1769480 | tf_op jit(solution)/shard_map/z3_lo/ppermute | solution.py:355
  121.5 22.2 %collective-permute-start.24 = (bf16[6,384,128]{2,1,0:T(8,128)(2,1)}, bf16[6,384,128]{2,1,0:T(8,128)(2,1)S(1)}, u32[]{:S(2)}, u32[]{:S(2)}) collective-permute-start(bf16[6,384,128]{2,1,0:T(8,128)(2,1)} %get-tuple-element.186), channel_id=1, source_target_pairs={{8,0},{16,8},{24,16},{9,1},{17,9},{25,17},{10,2},{18,10},{26,18},{... | collective-permute-start | bytes 1769480 | tf_op jit(solution)/shard_map/z3_hi/ppermute | solution.py:359
  167.5 5.0 %collective-permute-start.28 = (f32[64,128]{1,0:T(8,128)}, f32[64,128]{1,0:T(8,128)S(1)}, u32[]{:S(2)}, u32[]{:S(2)}) collective-permute-start(f32[64,128]{1,0:T(8,128)} %get-tuple-element.190), channel_id=1, source_target_pairs={{0,6},{1,7},{2,4},{3,5},{4,2},{5,3},{6,0},{7,1},{8,14},{9,15},{10,... | collective-permute-start | bytes 98312 | tf_op jit(solution)/shard_map/fin_3/ppermute | solution.py:347
  170.1 4.1 %collective-permute-start.27 = (f32[64,128]{1,0:T(8,128)}, f32[64,128]{1,0:T(8,128)S(1)}, u32[]{:S(2)}, u32[]{:S(2)}) collective-permute-start(f32[64,128]{1,0:T(8,128)} %get-tuple-element.189), channel_id=1, source_target_pairs={{0,4},{1,5},{2,6},{3,7},{4,0},{5,1},{6,2},{7,3},{8,12},{9,13},{10,... | collective-permute-start | bytes 98312 | tf_op jit(solution)/shard_map/fin_2/ppermute | solution.py:347
  170.6 4.1 %collective-permute-start.26 = (f32[64,128]{1,0:T(8,128)}, f32[64,128]{1,0:T(8,128)S(1)}, u32[]{:S(2)}, u32[]{:S(2)}) collective-permute-start(f32[64,128]{1,0:T(8,128)} %get-tuple-element.188), channel_id=1, source_target_pairs={{0,2},{1,3},{2,0},{3,1},{4,6},{5,7},{6,4},{7,5},{8,10},{9,11},{10,... | collective-permute-start | bytes 98312 | tf_op jit(solution)/shard_map/fin_1/ppermute | solution.py:347
  175.5 6.3 %collective-permute-start.31 = (f32[64,128]{1,0:T(8,128)S(1)}, f32[64,128]{1,0:T(8,128)S(1)}, u32[]{:S(2)}, u32[]{:S(2)}) collective-permute-start(f32[64,128]{1,0:T(8,128)S(1)} %add_add_fusion), channel_id=1, source_target_pairs={{0,24},{8,0},{16,8},{24,16},{1,25},{9,1},{17,9},{25,17},{2,26},{10... | collective-permute-start | bytes 98312 | tf_op jit(solution)/shard_map/ppermute | solution.py:442
  180.2 4.8 %collective-permute-start.30 = (f32[64,128]{1,0:T(8,128)S(1)}, f32[64,128]{1,0:T(8,128)S(1)}, u32[]{:S(2)}, u32[]{:S(2)}) collective-permute-start(f32[64,128]{1,0:T(8,128)S(1)} %add_add_fusion), channel_id=1, source_target_pairs={{0,16},{8,24},{16,0},{24,8},{1,17},{9,25},{17,1},{25,9},{2,18},{10... | collective-permute-start | bytes 98312 | tf_op jit(solution)/shard_map/ppermute | solution.py:442
  180.2 5.7 %collective-permute-start.29 = (f32[64,128]{1,0:T(8,128)S(1)}, f32[64,128]{1,0:T(8,128)S(1)}, u32[]{:S(2)}, u32[]{:S(2)}) collective-permute-start(f32[64,128]{1,0:T(8,128)S(1)} %add_add_fusion), channel_id=1, source_target_pairs={{0,8},{8,16},{16,24},{24,0},{1,9},{9,17},{17,25},{25,1},{2,10},{10... | collective-permute-start | bytes 98312 | tf_op jit(solution)/shard_map/ppermute | solution.py:442
  (8 other events, 9.9 us)
